TPU v7x, 512 devices: a whole 4x4x16 slice. The times are simulated.
512 devices in a mesh: fsdp: 32 (over y_lo, z), tp: 16 (over y_hi, x, core).
Axes of the slice: x: 4, y: 4 (y_hi: 2, y_lo: 2; y = y_hi * 2 + y_lo), z: 16, core: 2. Of those that a mesh axis runs over, the one named last changes fastest.
Arguments:
- tokens: bfloat16 [4096, 4096], P('fsdp', 'tp'), may hold values from -6 to 6
- base_weight: bfloat16 [1, 4096, 4096], P(None, None, 'tp'), may hold values from -0.09375 to 0.09375
- a_old: bfloat16 [1, 128, 4096], P(None, 'fsdp'), may hold values from -0.09375 to 0.09375
- a_new: bfloat16 [1, 128, 4096], P(None, 'fsdp'), may hold values from -0.09375 to 0.09375
- b_old: bfloat16 [1, 4096, 128], P(None, 'fsdp'), may hold values from -0.5 to 0.5
- b_new: bfloat16 [1, 4096, 128], P(None, 'fsdp'), may hold values from -0.5 to 0.5
- gains: float32 [1, 4096], replicated, may hold values from 0.5 to 1.5
Outputs:
- stream_out: bfloat16 [4, 4096, 4096], P(None, 'fsdp', 'tp')
- merged: bfloat16 [1, 4096, 4096], P(None, None, 'tp')
All inputs are finite; a program needn't handle non-finite values.
Results may differ from a plain program's by a relative error of at most 0.0069.
Values may be sent and summed in bfloat16 or wider, within the bound.
No kernel may reach another device: no remote copies, remote signals or barrier semaphores. Data moves between devices by JAX's collectives and lax.ppermute only.
A program may use at most 64 MiB of HBM per device.

v0:
```python
import jax
import jax.numpy as jnp
from jax import lax
from jax.sharding import PartitionSpec as P

STEPS = 4


def shards(tokens, base_weight, a_old, a_new, b_old, b_new, gains):
    out_cols = base_weight.shape[2]
    tp_index = lax.axis_index("tp")
    layer = 0
    b_full = (
        lax.all_gather(b_old[layer], "fsdp", axis=0, tiled=True),
        lax.all_gather(b_new[layer], "fsdp", axis=0, tiled=True),
    )
    local_old = lax.dynamic_slice_in_dim(b_full[0], tp_index * out_cols, out_cols, 0)
    local_new = lax.dynamic_slice_in_dim(b_full[1], tp_index * out_cols, out_cols, 0)
    contract = (((0,), (1,)), ((), ()))
    fresh = lax.dot_general(
        lax.all_gather(a_new[layer], "fsdp", axis=0, tiled=True),
        local_new,
        contract,
        preferred_element_type=jnp.float32,
    )
    stale = lax.dot_general(
        lax.all_gather(a_old[layer], "fsdp", axis=0, tiled=True),
        local_old,
        contract,
        preferred_element_type=jnp.float32,
    )
    delta = fresh - stale
    merged_all = [(base_weight[layer].astype(jnp.float32) + delta).astype(jnp.bfloat16)]
    stream = tokens
    results = []
    for step in range(STEPS):
        layer = 0
        values = stream.astype(jnp.float32)
        whole = lax.all_gather(stream, "tp", axis=1, tiled=True).astype(jnp.float32)
        scale = lax.rsqrt(jnp.mean(whole * whole, axis=-1, keepdims=True) + 1e-06)
        normed = (whole * scale * gains[layer]).astype(jnp.bfloat16)
        branch = jnp.dot(normed, merged_all[layer], preferred_element_type=jnp.float32)
        stream = (values + branch).astype(jnp.bfloat16)
        results.append(stream)
    return (jnp.stack(results), jnp.stack(merged_all))


def solution(mesh):
    placed = (
        P("fsdp", "tp"),
        P(None, None, "tp"),
        P(None, "fsdp", None),
        P(None, "fsdp", None),
        P(None, "fsdp", None),
        P(None, "fsdp", None),
        P(),
    )
    return jax.shard_map(
        shards,
        mesh=mesh,
        in_specs=placed,
        out_specs=(P(None, "fsdp", "tp"), P(None, None, "tp")),
        check_vma=False,
    )
```

profile of v0, /device:TPU:1, one launch (start us, length us, event | category | flops | bytes accessed | tf_op | source)
XLA Modules:
  0.0 795.5 jit_solution(15147034701901946917)
XLA Ops:
  7.2 0.7 all-gather.13.cloned.1.call-update
  7.9 1.4 copy.16
  9.4 0.0 all-gather.21.cloned.1.call-start
  9.5 0.7 all-gather.21.cloned.1.call-update
  10.1 0.0 all-gather.27.cloned.1.call-start
  10.2 1.4 copy.17
  11.7 0.0 all-gather.25.cloned.1.call-start
  11.7 0.5 all-gather.25.cloned.1.call-update
  12.2 0.0 all-gather.15.cloned.1.call-start
  12.3 4.1 copy.15
  16.4 61.3 %all-gather.13.cloned.1.call-done = bf16[128,4096]{1,0:T(8,128)(2,1)} async-done(((bf16[128,256]{1,0:T(8,128)(2,1)}), bf16[128,4096]{1,0:T(8,128)(2,1)}) %all-gather.13.cloned.1.call-update) | async-done | bytes 1048592 | tf_op jit(solution)/shard_map/all_gather | solution.py:39
  77.6 1.5 fusion.3
  79.2 112.6 %all-gather.23.cloned.1.call-done = bf16[1,128,4096]{2,0,1:T(2,128)(2,1)} async-done(((bf16[1,4,4096]{2,0,1:T(2,128)(2,1)}), bf16[1,128,4096]{2,0,1:T(2,128)(2,1)}) %all-gather.23.cloned.1.call-update) | async-done | bytes 1048592 | tf_op jit(solution)/shard_map/all_gather | solution.py:21
  191.8 126.2 %all-gather.21.cloned.1.call-done = bf16[1,4096,128]{2,1,0:T(8,128)(2,1)} async-done(((bf16[1,128,128]{2,1,0:T(8,128)(2,1)}), bf16[1,4096,128]{2,1,0:T(8,128)(2,1)}) %all-gather.21.cloned.1.call-update) | async-done | bytes 1048592 | tf_op jit(solution)/shard_map/all_gather | solution.py:15
  317.9 5.1 fusion.26
  323.1 124.4 %all-gather.27.cloned.1.call-done = bf16[1,128,4096]{2,0,1:T(2,128)(2,1)} async-done(((bf16[1,4,4096]{2,0,1:T(2,128)(2,1)}), bf16[1,128,4096]{2,0,1:T(2,128)(2,1)}) %all-gather.27.cloned.1.call-update) | async-done | bytes 1048592 | tf_op jit(solution)/shard_map/all_gather | solution.py:27
  447.5 126.0 %all-gather.25.cloned.1.call-done = bf16[1,4096,128]{2,1,0:T(8,128)(2,1)} async-done(((bf16[1,128,128]{2,1,0:T(8,128)(2,1)}), bf16[1,4096,128]{2,1,0:T(8,128)(2,1)}) %all-gather.25.cloned.1.call-update) | async-done | bytes 1048592 | tf_op jit(solution)/shard_map/all_gather | solution.py:14
  573.5 5.2 fusion.2
  578.7 1.5 fusion.15
  580.2 0.0 all-gather.17.cloned.1.call-start
  580.3 75.9 %all-gather.15.cloned.1.call-done = bf16[128,4096]{1,0:T(8,128)(2,1)} async-done(((bf16[128,256]{1,0:T(8,128)(2,1)}), bf16[128,4096]{1,0:T(8,128)(2,1)}) %all-gather.15.cloned.1.call-update) | async-done | bytes 1048592 | tf_op jit(solution)/shard_map/all_gather | solution.py:39
  656.2 1.5 fusion.6
  657.7 2.7 fusion.16
  660.4 0.0 all-gather.19.cloned.1.call-start
  660.5 59.7 %all-gather.17.cloned.1.call-done = bf16[128,4096]{1,0:T(8,128)(2,1)} async-done(((bf16[128,256]{1,0:T(8,128)(2,1)}), bf16[128,4096]{1,0:T(8,128)(2,1)}) %all-gather.17.cloned.1.call-update) | async-done | bytes 1048592 | tf_op jit(solution)/shard_map/all_gather | solution.py:39
  720.2 1.5 fusion.9
  721.7 2.7 fusion.17
  724.5 2.5 copy.18
  726.9 57.3 %all-gather.19.cloned.1.call-done = bf16[128,4096]{1,0:T(8,128)(2,1)} async-done(((bf16[128,256]{1,0:T(8,128)(2,1)}), bf16[128,4096]{1,0:T(8,128)(2,1)}) %all-gather.19.cloned.1.call-update) | async-done | bytes 1048592 | tf_op jit(solution)/shard_map/all_gather | solution.py:39
  784.3 1.5 fusion.12
  785.8 2.1 fusion.19
  788.0 0.7 pad_maximum_fusion
  (23 shorter events, 0.2 us)
Async XLA Ops:
  7.2 70.5 %all-gather.13.cloned.1.call-start = ((), (), s32[]{:S(2)}) async-start(), calls=%async_computation | async-start | bytes 1114112 | tf_op jit(solution)/shard_map/all_gather | solution.py:39
  7.9 183.9 %all-gather.23.cloned.1.call-start = ((), (), s32[]{:S(2)}) async-start(), calls=%async_computation.5 | async-start | bytes 2162688 | tf_op jit(solution)/shard_map/all_gather | solution.py:21
  9.4 308.5 %all-gather.21.cloned.1.call-start = ((), (), s32[]{:S(2)}) async-start(), calls=%async_computation.4 | async-start | bytes 1081344 | tf_op jit(solution)/shard_map/all_gather | solution.py:15
  10.1 437.3 %all-gather.27.cloned.1.call-start = ((), (), s32[]{:S(2)}) async-start(), calls=%async_computation.7 | async-start | bytes 2162688 | tf_op jit(solution)/shard_map/all_gather | solution.py:27
  11.7 561.9 %all-gather.25.cloned.1.call-start = ((), (), s32[]{:S(2)}) async-start(), calls=%async_computation.6 | async-start | bytes 1081344 | tf_op jit(solution)/shard_map/all_gather | solution.py:14
  12.2 643.9 %all-gather.15.cloned.1.call-start = ((), (), s32[]{:S(2)}) async-start(), calls=%async_computation.1 | async-start | bytes 1114112 | tf_op jit(solution)/shard_map/all_gather | solution.py:39
  323.1 255.6 %copy-start = (bf16[128,4096]{1,0:T(8,128)(2,1)S(1)}, bf16[128,4096]{1,0:T(8,128)(2,1)}, u32[]{:S(2)}) copy-start(bf16[128,4096]{1,0:T(8,128)(2,1)} %all-gather.13.cloned.1.call-done) | copy-start | bytes 3145732
  323.1 255.6 %copy-start.4 = (bf16[128,256]{1,0:T(8,128)(2,1)S(1)}, bf16[128,256]{1,0:T(8,128)(2,1)}, u32[]{:S(2)}) copy-start(bf16[128,256]{1,0:T(8,128)(2,1)} %param.7) | copy-start | bytes 196612
  323.1 255.6 %copy-start.5 = (f32[1,4096]{1,0:T(1,128)S(1)}, f32[1,4096]{1,0:T(1,128)}, u32[]{:S(2)}) copy-start(f32[1,4096]{1,0:T(1,128)} %param.13) | copy-start | bytes 49156
  580.2 140.0 %all-gather.17.cloned.1.call-start = ((), (), s32[]{:S(2)}) async-start(), calls=%async_computation.2 | async-start | bytes 1114112 | tf_op jit(solution)/shard_map/all_gather | solution.py:39
  660.4 123.8 %all-gather.19.cloned.1.call-start = ((), (), s32[]{:S(2)}) async-start(), calls=%async_computation.3 | async-start | bytes 1114112 | tf_op jit(solution)/shard_map/all_gather | solution.py:39
  724.5 61.3 %copy-start.3 = (bf16[128,256]{1,0:T(8,128)(2,1)S(1)}, bf16[128,256]{1,0:T(8,128)(2,1)}, u32[]{:S(2)}) copy-start(bf16[128,256]{1,0:T(8,128)(2,1)} %fusion.17) | copy-start | bytes 196612
  785.8 2.1 copy-start.1
  785.8 2.2 copy-start.2
Sparse Core Ops, SparseCore 0:
  11.1 66.4 all-gather.12
  80.3 111.4 all-gather.22
  193.8 124.0 all-gather.20
  319.9 127.5 all-gather.26
  449.4 124.0 all-gather.24
  580.3 75.7 all-gather.14
  660.5 59.6 all-gather.16
  724.6 59.6 all-gather.18
where the time goes:
time: 796 us
  waiting for transfers between devices  745 us (94%)
  matrix products  19.3 us (2%)
  between operations  14.2 us (2%)
  local copies, waits for them, and re-layouts  9.44 us (1%)
    all_gather x4, waiting for transfers between devices, shards(): whole = lax.all_gather(stream, 'tp', axis=1, tiled=True).astype(jnp.float32)  254 us
    all_gather x1, waiting for transfers between devices, shards(): lax.all_gather(b_new[layer], 'fsdp', axis=0, tiled=True)  126 us
    all_gather x1, waiting for transfers between devices, shards(): lax.all_gather(b_old[layer], 'fsdp', axis=0, tiled=True)  126 us
    all_gather x1, waiting for transfers between devices, shards(): lax.all_gather(a_old[layer], 'fsdp', axis=0, tiled=True)  124 us
    all_gather x1, waiting for transfers between devices, shards(): lax.all_gather(a_new[layer], 'fsdp', axis=0, tiled=True)  113 us
  transfers between devices with their start and end apart: 8, of which 8 were waited for; matrix products, arithmetic and copies ran while one was open for 2% of the time, Pallas kernels for 0%

commit v1 on v0

v1 whole, which is shorter than its diff:
```python
import jax
import jax.numpy as jnp
from jax import lax
from jax.sharding import PartitionSpec as P

STEPS = 4
CHIPS = 8
GROUPS = [[2 * chip + core for chip in range(CHIPS)] for core in range(2)]
SWAP = [(i, i ^ 1) for i in range(2 * CHIPS)]


def spread(blocks):
    own = lax.all_to_all(blocks, "tp", 0, 0, axis_index_groups=GROUPS)
    return own, lax.ppermute(own, "tp", SWAP)


def shards(tokens, base_weight, a_old, a_new, b_old, b_new, gains):
    rows, cols = tokens.shape
    tp = lax.axis_size("tp")
    fsdp = lax.axis_size("fsdp")
    t = lax.axis_index("tp")
    core = lax.rem(t, 2)

    def ordered(own, other):
        even = jnp.where(core == 0, own, other)
        odd = jnp.where(core == 0, other, own)
        return jnp.stack([even, odd], 1)

    share = b_old.shape[1] // tp
    low = a_old.shape[1]
    pick_a = lambda a: lax.dynamic_slice_in_dim(a[0], t * cols, cols, 1)
    pick_b = lambda b: lax.dynamic_slice_in_dim(b[0], t * share, share, 0)
    up = jnp.concatenate([pick_b(b_new), pick_b(b_old)], 1)
    message = jnp.concatenate([pick_a(a_new), pick_a(a_old), up], 0)
    got = lax.all_to_all(jnp.broadcast_to(message[None], (fsdp,) + message.shape), "fsdp", 0, 0)
    down_new = got[:, :low].reshape(fsdp * low, cols)
    down_old = got[:, low : 2 * low].reshape(fsdp * low, cols)
    ups = got[:, 2 * low :].reshape(CHIPS, -1, cols)

    common = jnp.concatenate([tokens, down_new, down_old], 0)
    first = jnp.concatenate([jnp.broadcast_to(common[None], (CHIPS,) + common.shape), ups], 1)
    own, other = spread(first)
    down = ordered(own[:, rows : rows + 2 * fsdp * low], other[:, rows : rows + 2 * fsdp * low])
    down = down.reshape(tp, 2 * fsdp * low, cols)
    ups = ordered(own[:, rows + 2 * fsdp * low :], other[:, rows + 2 * fsdp * low :])
    ups = ups.reshape(CHIPS, 2, 2, 2, share, cols)
    ups = lax.dynamic_index_in_dim(ups, core, 2, keepdims=False)
    ups = ups.transpose(2, 0, 1, 3, 4).reshape(cols, cols)
    half = cols // 2
    ups = jnp.concatenate([ups[:, :half], -ups[:, half:]], 1)
    delta = lax.dot_general(down, ups, (((1,), (1,)), ((), ())), preferred_element_type=jnp.float32)
    merged = (base_weight[0].astype(jnp.float32) + delta.reshape(tp * cols, cols)).astype(jnp.bfloat16)

    weights = merged.reshape(tp, cols, cols)
    gain = gains[0].reshape(tp, 1, cols)
    own, other = own[:, :rows], other[:, :rows]
    stream = tokens
    results = []
    for step in range(STEPS):
        if step:
            own, other = spread(jnp.broadcast_to(stream[None], (CHIPS,) + stream.shape))
        whole = ordered(own, other).reshape(tp, rows, cols).astype(jnp.float32)
        mean = jnp.sum(whole * whole, axis=(0, 2)) / (tp * cols)
        scale = lax.rsqrt(mean + 1e-06)[None, :, None]
        normed = (whole * scale * gain).astype(jnp.bfloat16)
        branch = lax.dot_general(
            normed.transpose(1, 0, 2).reshape(rows, tp * cols),
            merged,
            (((1,), (0,)), ((), ())),
            preferred_element_type=jnp.float32,
        )
        stream = (stream.astype(jnp.float32) + branch).astype(jnp.bfloat16)
        results.append(stream)
    return jnp.stack(results), merged[None]


def solution(mesh):
    placed = (
        P("fsdp", "tp"),
        P(None, None, "tp"),
        P(None, "fsdp", None),
        P(None, "fsdp", None),
        P(None, "fsdp", None),
        P(None, "fsdp", None),
        P(),
    )
    return jax.shard_map(
        shards,
        mesh=mesh,
        in_specs=placed,
        out_specs=(P(None, "fsdp", "tp"), P(None, None, "tp")),
        check_vma=False,
    )
```

time: 796 us -> 163 us (0.20)
  waiting for transfers between devices: 745 us -> 6.51 us
  blocking collectives: 0 us -> 107 us
  matrix products: 19.3 us -> 5.32 us
  starting transfers between devices: 0.32 us -> 14.1 us
  between operations: 14.2 us -> 1.03 us
    all_gather x8 -> x0, waiting for transfers between devices: 743 us -> none  [the longest x4 254 us: shards(): whole = lax.all_gather(stream, 'tp', axis=1, tiled=True).astype(jnp.float32)]
    all_to_all x0 -> x5, blocking collectives: none -> 107 us  [the longest x4 69.7 us: spread(): own = lax.all_to_all(blocks, 'tp', 0, 0, axis_index_groups=GROUPS)]
    ppermute x0 -> x4, starting transfers between devices: none -> 14.1 us  [spread(): return (own, lax.ppermute(own, 'tp', SWAP))]
    dot_general x6 -> x5, matrix products: 19.3 us -> 5.32 us  [the longest x1 2.99 us: shards(): lax.dot_general(down, ups, (((1,), (1,)), ((), ())), preferred_element_ty...]
  transfers between devices with their start and end apart: 8 -> 4, of which waited for: 8 -> 4; matrix products, arithmetic and copies ran while one was open for 2% -> 1% of each run, Pallas kernels for 0% -> 0%
where the time goes in v1:
time: 163 us; the launch traced here: 162 us
  blocking collectives  107 us (66%)
  local copies, waits for them, and re-layouts  17.1 us (10%)
  starting transfers between devices  14.1 us (9%)
  other arithmetic  11.5 us (7%)
  waiting for transfers between devices  6.51 us (4%)
  matrix products  5.32 us (3%)
    all_to_all x4, blocking collectives, spread(): own = lax.all_to_all(blocks, 'tp', 0, 0, axis_index_groups=GROUPS)  69.7 us
    all_to_all x1, blocking collectives, shards(): lax.all_to_all(jnp.broadcast_to(message[None], (fsdp,) + message.shape),...  36.8 us
    ppermute x4, starting transfers between devices, spread(): return (own, lax.ppermute(own, 'tp', SWAP))  14.1 us
    ppermute x4, waiting for transfers between devices, spread(): return (own, lax.ppermute(own, 'tp', SWAP))  6.51 us
    transpose x4, local copies, waits for them, and re-layouts, shards(): normed.transpose(1, 0, 2).reshape(rows, tp * cols)  6.45 us
    convert_element_type x4, other arithmetic, shards(): normed = (whole * scale * gain).astype(jnp.bfloat16)  5.77 us
    dot_general x1, local copies, waits for them, and re-layouts, shards(): lax.dot_general(down, ups, (((1,), (1,)), ((), ())), preferred_element_ty...  3.91 us
  transfers between devices with their start and end apart: 4, of which 4 were waited for; matrix products, arithmetic and copies ran while one was open for 1% of the time, Pallas kernels for 0%

profile of v1, /device:TPU:1, one launch (start us, length us, event | category | flops | bytes accessed | tf_op | source)
XLA Modules:
  0.0 162.1 jit_solution(11833936978995744478)
XLA Ops:
  0.6 0.7 dynamic-slice_bitcast_fusion.2
  1.3 0.7 dynamic-slice_bitcast_fusion
  2.1 36.8 %all_to_all.25 = bf16[32,16,256]{2,1,0:T(8,128)(2,1)S(1)} all-to-all(bf16[32,16,256]{2,1,0:T(8,128)(2,1)S(1)} %broadcast_in_dim.12), channel_id=1, replica_groups=mesh['fsdp'=32,'tp'=16] {'fsdp'}, dimensions={0} | all-to-all | bytes 524288 | tf_op jit(solution)/shard_map/all_to_all | solution.py:35
  39.0 0.9 pad_maximum_fusion.3
  40.1 27.3 %all_to_all.26 = bf16[8,416,256]{2,1,0:T(8,128)(2,1)S(1)} all-to-all(bf16[8,416,256]{2,1,0:T(8,128)(2,1)S(1)} %pad_maximum_fusion.1), channel_id=1, replica_groups={{0,2,4,6,8,10,12,14},{1,3,5,7,9,11,13,15},{16,18,20,22,24,26,28,30},{17..., dimensions={0} | all-to-all | bytes 3407872 | tf_op jit(solution)/shard_map/all_to_all | solution.py:13
  67.4 5.9 %collective-permute-start = (bf16[8,416,256]{2,1,0:T(8,128)(2,1)S(1)}, bf16[8,416,256]{2,1,0:T(8,128)(2,1)S(1)}, u32[]{:S(2)}, u32[]{:S(2)}) collective-permute-start(bf16[8,416,256]{2,1,0:T(8,128)(2,1)S(1)} %all_to_all.26), channel_id=1, source_target_pairs={{0,1},{1,0},{2,3},{3,2},{4,5},{5,4},{6,7},{7,6},{8,9},{9,8},{10,11... | collective-permute-start | bytes 5111816 | tf_op jit(solution)/shard_map/ppermute | solution.py:14
  73.9 0.7 reduce.7
  74.6 2.0 %collective-permute-done = bf16[8,416,256]{2,1,0:T(8,128)(2,1)S(1)} collective-permute-done((bf16[8,416,256]{2,1,0:T(8,128)(2,1)S(1)}, bf16[8,416,256]{2,1,0:T(8,128)(2,1)S(1)}, u32[]{:S(2)}, u32[]{:S(2)}) %collective-permute-start) | collective-permute-done | bytes 1703968 | tf_op jit(solution)/shard_map/ppermute | solution.py:14
  76.7 1.1 copy-done.3
  78.2 1.3 copy-done.2
  79.5 0.9 broadcast_select_fusion
  80.9 1.5 copy.11
  82.4 3.9 %copy.12 = bf16[16,256,256]{2,1,0:T(8,128)(2,1)} copy(bf16[16,256,256]{1,2,0:T(8,128)(2,1)} %bitcast.94) | data formatting | bytes 4194304 | tf_op jit(solution)/shard_map/dot_general | solution.py:51
  86.3 1.4 fusion.8
  87.7 1.6 copy.10
  89.3 3.0 %fusion = bf16[4096,256]{1,0:T(8,128)(2,1)S(1)} fusion(bf16[4096,256]{1,0:T(8,128)(2,1)} %bitcast.93, bf16[1,4096,256]{2,1,0:T(8,128)(2,1)} %param.8, bf16[256,128]{1,0:T(8,128)(2,1)S(1)} %get-tuple-element.17, bf16[256,128]{1,0:T(8,128)(2,1)S(1)} %get-tuple-element.16), kind=kOutput, calls=%fused_computation.1 | convolution fusion | flops 540278784 | bytes 6422528 | tf_op jit(solution)/shard_map/dot_general | solution.py:51
  93.0 14.1 %all_to_all.27 = bf16[8,128,256]{2,1,0:T(8,128)(2,1)S(1)} all-to-all(bf16[8,128,256]{2,1,0:T(8,128)(2,1)S(1)} %broadcast_in_dim.14), channel_id=1, replica_groups={{0,2,4,6,8,10,12,14},{1,3,5,7,9,11,13,15},{16,18,20,22,24,26,28,30},{17..., dimensions={0} | all-to-all | bytes 1048576 | tf_op jit(solution)/shard_map/all_to_all | solution.py:13
  107.1 2.7 %collective-permute-start.1 = (bf16[8,128,256]{2,1,0:T(8,128)(2,1)S(1)}, bf16[8,128,256]{2,1,0:T(8,128)(2,1)S(1)}, u32[]{:S(2)}, u32[]{:S(2)}) collective-permute-start(bf16[8,128,256]{2,1,0:T(8,128)(2,1)S(1)} %all_to_all.27), channel_id=1, source_target_pairs={{0,1},{1,0},{2,3},{3,2},{4,5},{5,4},{6,7},{7,6},{8,9},{9,8},{10,11... | collective-permute-start | bytes 1572872 | tf_op jit(solution)/shard_map/ppermute | solution.py:14
  109.9 1.5 collective-permute-done.1
  112.1 1.4 fusion.6
  113.5 1.6 copy.15
  115.8 14.2 %all_to_all.28 = bf16[8,128,256]{2,1,0:T(8,128)(2,1)S(1)} all-to-all(bf16[8,128,256]{2,1,0:T(8,128)(2,1)S(1)} %broadcast_in_dim.15), channel_id=1, replica_groups={{0,2,4,6,8,10,12,14},{1,3,5,7,9,11,13,15},{16,18,20,22,24,26,28,30},{17..., dimensions={0} | all-to-all | bytes 1048576 | tf_op jit(solution)/shard_map/all_to_all | solution.py:13
  129.9 2.7 %collective-permute-start.2 = (bf16[8,128,256]{2,1,0:T(8,128)(2,1)S(1)}, bf16[8,128,256]{2,1,0:T(8,128)(2,1)S(1)}, u32[]{:S(2)}, u32[]{:S(2)}) collective-permute-start(bf16[8,128,256]{2,1,0:T(8,128)(2,1)S(1)} %all_to_all.28), channel_id=1, source_target_pairs={{0,1},{1,0},{2,3},{3,2},{4,5},{5,4},{6,7},{7,6},{8,9},{9,8},{10,11... | collective-permute-start | bytes 1572872 | tf_op jit(solution)/shard_map/ppermute | solution.py:14
  132.6 1.5 collective-permute-done.2
  134.9 1.4 fusion.4
  136.3 1.6 copy.17
  138.6 14.1 %all_to_all.29 = bf16[8,128,256]{2,1,0:T(8,128)(2,1)S(1)} all-to-all(bf16[8,128,256]{2,1,0:T(8,128)(2,1)S(1)} %broadcast_in_dim.16), channel_id=1, replica_groups={{0,2,4,6,8,10,12,14},{1,3,5,7,9,11,13,15},{16,18,20,22,24,26,28,30},{17..., dimensions={0} | all-to-all | bytes 1048576 | tf_op jit(solution)/shard_map/all_to_all | solution.py:13
  152.7 2.7 %collective-permute-start.3 = (bf16[8,128,256]{2,1,0:T(8,128)(2,1)S(1)}, bf16[8,128,256]{2,1,0:T(8,128)(2,1)S(1)}, u32[]{:S(2)}, u32[]{:S(2)}) collective-permute-start(bf16[8,128,256]{2,1,0:T(8,128)(2,1)S(1)} %all_to_all.29), channel_id=1, source_target_pairs={{0,1},{1,0},{2,3},{3,2},{4,5},{5,4},{6,7},{7,6},{8,9},{9,8},{10,11... | collective-permute-start | bytes 1572872 | tf_op jit(solution)/shard_map/ppermute | solution.py:14
  155.4 1.5 collective-permute-done.3
  157.7 1.4 fusion.2
  159.1 1.6 copy.19
  161.3 0.7 pad_maximum_fusion.2
  (53 shorter events, 6.3 us)
Async XLA Ops:
  40.1 33.8 %copy-start.6 = (f32[1,4096]{1,0:T(1,128)S(1)}, f32[1,4096]{1,0:T(1,128)}, u32[]{:S(2)}) copy-start(f32[1,4096]{1,0:T(1,128)} %param.13) | copy-start | bytes 49156
  67.4 9.2 %copy-start.1 = (bf16[8,416,256]{2,1,0:T(8,128)(2,1)}, bf16[8,416,256]{2,1,0:T(8,128)(2,1)S(1)}, u32[]{:S(2)}) copy-start(bf16[8,416,256]{2,1,0:T(8,128)(2,1)S(1)} %all_to_all.26) | copy-start | bytes 5111812
  67.4 9.2 %collective-permute-start = (bf16[8,416,256]{2,1,0:T(8,128)(2,1)S(1)}, bf16[8,416,256]{2,1,0:T(8,128)(2,1)S(1)}, u32[]{:S(2)}, u32[]{:S(2)}) collective-permute-start(bf16[8,416,256]{2,1,0:T(8,128)(2,1)S(1)} %all_to_all.26), channel_id=1, source_target_pairs={{0,1},{1,0},{2,3},{3,2},{4,5},{5,4},{6,7},{7,6},{8,9},{9,8},{10,11... | collective-permute-start | bytes 5111816 | tf_op jit(solution)/shard_map/ppermute | solution.py:14
  76.6 1.2 copy-start.3
  78.1 1.5 copy-start.2
  78.1 2.5 %copy-start.4 = (bf16[8,416,256]{2,1,0:T(8,128)(2,1)S(1)}, bf16[8,416,256]{2,1,0:T(8,128)(2,1)}, u32[]{:S(2)}) copy-start(bf16[8,416,256]{2,1,0:T(8,128)(2,1)} %copy-done.3) | copy-start | bytes 5111812
  89.3 3.0 %copy-start.5 = (bf16[128,256]{1,0:T(8,128)(2,1)S(1)}, bf16[128,256]{1,0:T(8,128)(2,1)}, u32[]{:S(2)}) copy-start(bf16[128,256]{1,0:T(8,128)(2,1)} %param.7) | copy-start | bytes 196612
  92.3 68.4 %copy-start = (bf16[4096,256]{1,0:T(8,128)(2,1)}, bf16[4096,256]{1,0:T(8,128)(2,1)S(1)}, u32[]{:S(2)}) copy-start(bf16[4096,256]{1,0:T(8,128)(2,1)S(1)} %fusion) | copy-start | bytes 6291460
  107.1 4.2 %collective-permute-start.1 = (bf16[8,128,256]{2,1,0:T(8,128)(2,1)S(1)}, bf16[8,128,256]{2,1,0:T(8,128)(2,1)S(1)}, u32[]{:S(2)}, u32[]{:S(2)}) collective-permute-start(bf16[8,128,256]{2,1,0:T(8,128)(2,1)S(1)} %all_to_all.27), channel_id=1, source_target_pairs={{0,1},{1,0},{2,3},{3,2},{4,5},{5,4},{6,7},{7,6},{8,9},{9,8},{10,11... | collective-permute-start | bytes 1572872 | tf_op jit(solution)/shard_map/ppermute | solution.py:14
  129.9 4.2 %collective-permute-start.2 = (bf16[8,128,256]{2,1,0:T(8,128)(2,1)S(1)}, bf16[8,128,256]{2,1,0:T(8,128)(2,1)S(1)}, u32[]{:S(2)}, u32[]{:S(2)}) collective-permute-start(bf16[8,128,256]{2,1,0:T(8,128)(2,1)S(1)} %all_to_all.28), channel_id=1, source_target_pairs={{0,1},{1,0},{2,3},{3,2},{4,5},{5,4},{6,7},{7,6},{8,9},{9,8},{10,11... | collective-permute-start | bytes 1572872 | tf_op jit(solution)/shard_map/ppermute | solution.py:14
  152.7 4.2 %collective-permute-start.3 = (bf16[8,128,256]{2,1,0:T(8,128)(2,1)S(1)}, bf16[8,128,256]{2,1,0:T(8,128)(2,1)S(1)}, u32[]{:S(2)}, u32[]{:S(2)}) collective-permute-start(bf16[8,128,256]{2,1,0:T(8,128)(2,1)S(1)} %all_to_all.29), channel_id=1, source_target_pairs={{0,1},{1,0},{2,3},{3,2},{4,5},{5,4},{6,7},{7,6},{8,9},{9,8},{10,11... | collective-permute-start | bytes 1572872 | tf_op jit(solution)/shard_map/ppermute | solution.py:14

commit v2 on v1

v2 whole, which is shorter than its diff:
```python
import jax
import jax.numpy as jnp
from jax import lax
from jax.experimental import pallas as pl
from jax.experimental.pallas import tpu as pltpu
from jax.sharding import PartitionSpec as P

STEPS = 4
CHIPS = 8
GROUPS = [[2 * chip + core for chip in range(CHIPS)] for core in range(2)]
PAIRS = [[2 * chip, 2 * chip + 1] for chip in range(CHIPS)]
SWAP = [(i, i ^ 1) for i in range(2 * CHIPS)]

VMEM = pl.BlockSpec(memory_space=pltpu.VMEM)
SMEM = pl.BlockSpec(memory_space=pltpu.SMEM)
ROOM = pltpu.CompilerParams(vmem_limit_bytes=24 * 1024 * 1024)


def spread(blocks):
    return lax.all_to_all(blocks, "tp", 0, 0, axis_index_groups=GROUPS)


def pack_kernel(got_ref, stream_ref, out_ref):
    fsdp, _, cols = got_ref.shape
    got = got_ref[...].astype(jnp.float32).reshape(fsdp, 2, 8, cols)
    down = got[:, 0].reshape(8 * fsdp, cols)
    came = lax.broadcasted_iota(jnp.int32, (8 * fsdp, cols), 0)
    goes = lax.broadcasted_iota(jnp.int32, (8 * fsdp, cols), 1)
    place = (came // 4 % 2) * (4 * fsdp) + came // 8 * 4 + came % 4
    order = jnp.where(place == goes, 1.0, 0.0).astype(jnp.bfloat16)
    down = jnp.dot(down.T.astype(jnp.bfloat16), order, preferred_element_type=jnp.float32).astype(jnp.bfloat16)
    stream = stream_ref[...].reshape(-1, cols)
    rows = stream.shape[0]
    each = fsdp // CHIPS
    for chip in range(CHIPS):
        out_ref[chip, :rows, :] = stream
        out_ref[chip, rows : rows + cols, :] = down
        ups = got[chip * each : (chip + 1) * each, 1].reshape(8 * each, cols)
        out_ref[chip, rows + cols :, :] = ups.astype(jnp.bfloat16)


def merge_kernel(core_ref, own_ref, other_ref, base_ref, mate_ref, weight_ref, merged_ref, up_ref):
    core = core_ref[0]
    cols = base_ref.shape[1]
    share = up_ref.shape[3]
    first = own_ref.shape[1] - cols - 4 * share
    for chip in range(CHIPS):
        for which, source in enumerate((own_ref, other_ref)):
            block = 2 * chip + (core if which == 0 else 1 - core)
            ups = source[chip, first + cols :, :].astype(jnp.float32).reshape(2, 2, share, cols)
            for j in range(2):
                up_ref[core, j, block] = ups[0, j]
                up_ref[1 - core, j, block] = ups[1, j]
    up = up_ref[...].reshape(2 * cols, cols).astype(jnp.bfloat16)
    for chip in range(CHIPS):
        for which, source in enumerate((own_ref, other_ref)):
            down = source[chip, first : first + cols, :]
            delta = lax.dot_general(down, up, (((1,), (1,)), ((), ())), preferred_element_type=jnp.float32)
            block = 2 * chip + (core if which == 0 else 1 - core)
            rows = pl.ds(pl.multiple_of(block * cols, cols), cols)
            mine = (base_ref[rows, :].astype(jnp.float32) + delta[:, :cols]).astype(jnp.bfloat16)
            merged_ref[rows, :] = mine
            weight_ref[2 * chip + which, :, :cols] = mine
            weight_ref[2 * chip + which, :, cols:] = (
                mate_ref[rows, :].astype(jnp.float32) + delta[:, cols:]
            ).astype(jnp.bfloat16)


def step_kernel(x_ref, weight_ref, gain_ref, mine_ref, out_ref):
    _, rows, cols = mine_ref.shape
    blocks = weight_ref.shape[0]
    part = lambda i: x_ref[i // 2, (i % 2) * rows : (i % 2 + 1) * rows, :].astype(jnp.float32)
    squares = part(0) * part(0)
    for i in range(1, blocks):
        squares += part(i) * part(i)
    mean = jnp.sum(squares, axis=1, keepdims=True) / (blocks * cols)
    scale = lax.rsqrt(mean + 1e-06)
    total = jnp.zeros((rows, 2 * cols), jnp.float32)
    for i in range(blocks):
        normed = (part(i) * scale * gain_ref[i]).astype(jnp.bfloat16)
        total += jnp.dot(normed, weight_ref[i], preferred_element_type=jnp.float32)
    for half in range(2):
        branch = total[:, half * cols : (half + 1) * cols]
        out_ref[half] = (mine_ref[half].astype(jnp.float32) + branch).astype(jnp.bfloat16)


def shards(tokens, base_weight, a_old, a_new, b_old, b_new, gains):
    rows, cols = tokens.shape
    tp = lax.axis_size("tp")
    fsdp = lax.axis_size("fsdp")
    t = lax.axis_index("tp")
    core = lax.rem(t, 2)
    half = rows // 2

    mate = lax.ppermute(base_weight[0], "tp", SWAP)
    both = lax.all_gather(tokens, "tp", axis=0, axis_index_groups=PAIRS)
    both = lax.dynamic_slice_in_dim(both, core * half, half, 1)
    stream = jnp.where(core == 0, both, both[::-1])

    share = b_old.shape[1] // tp
    low = a_old.shape[1]
    pick_a = lambda a: lax.dynamic_slice_in_dim(a[0], t * cols, cols, 1)
    pick_b = lambda b: lax.dynamic_slice_in_dim(b[0], t * share, share, 0)
    up = jnp.concatenate([pick_b(b_new), -pick_b(b_old)], 1)
    message = jnp.concatenate([pick_a(a_new), pick_a(a_old), up], 0)
    got = lax.all_to_all(jnp.broadcast_to(message[None], (fsdp,) + message.shape), "fsdp", 0, 0)
    packed = pl.pallas_call(
        pack_kernel,
        out_shape=jax.ShapeDtypeStruct((CHIPS, rows + cols + 4 * share, cols), jnp.bfloat16),
        in_specs=[VMEM] * 2,
        out_specs=VMEM,
        name="pack",
        compiler_params=ROOM,
    )(got, stream)
    packed, mate = lax.optimization_barrier((packed, mate))

    own = spread(packed)
    other = lax.ppermute(own, "tp", SWAP)
    weights, merged = pl.pallas_call(
        merge_kernel,
        out_shape=(
            jax.ShapeDtypeStruct((tp, cols, 2 * cols), jnp.bfloat16),
            jax.ShapeDtypeStruct((tp * cols, cols), jnp.bfloat16),
        ),
        in_specs=[SMEM] + [VMEM] * 4,
        out_specs=(VMEM, VMEM),
        scratch_shapes=[pltpu.VMEM((2, 2, tp, share, cols), jnp.float32)],
        name="merge",
        compiler_params=ROOM,
    )(core[None], own, other, base_weight[0], mate)

    gain = gains[0].reshape(CHIPS, 2, 1, cols)
    gain = jnp.where(core == 0, gain, gain[:, ::-1]).reshape(tp, 1, cols)
    x = own
    results = []
    for step in range(STEPS):
        if step:
            x = spread(jnp.broadcast_to(stream.reshape(1, rows, cols), (CHIPS, rows, cols)))
        stream = pl.pallas_call(
            step_kernel,
            out_shape=jax.ShapeDtypeStruct((2, half, cols), jnp.bfloat16),
            in_specs=[VMEM] * 4,
            out_specs=VMEM,
            name="step",
            compiler_params=ROOM,
        )(x, weights, gain, stream)
        results.append(stream)

    done = jnp.stack(results)
    swapped = lax.all_gather(done[:, 1], "tp", axis=0, axis_index_groups=PAIRS)
    swapped = lax.dynamic_index_in_dim(swapped, 1 - core, 0, keepdims=False)
    ends = jnp.stack([done[:, 0], swapped], 1)
    ends = jnp.where(core == 0, ends, ends[:, ::-1])
    return ends.reshape(STEPS, rows, cols), merged[None]


def solution(mesh):
    placed = (
        P("fsdp", "tp"),
        P(None, None, "tp"),
        P(None, "fsdp", None),
        P(None, "fsdp", None),
        P(None, "fsdp", None),
        P(None, "fsdp", None),
        P(),
    )
    return jax.shard_map(
        shards,
        mesh=mesh,
        in_specs=placed,
        out_specs=(P(None, "fsdp", "tp"), P(None, None, "tp")),
        check_vma=False,
    )
```

time: 163 us -> 136 us (0.83)
  blocking collectives: 107 us -> 60.1 us
  waiting for transfers between devices: 6.51 us -> 32.8 us
  starting transfers between devices: 14.1 us -> 28.9 us
  local copies, waits for them, and re-layouts: 17.1 us -> 4.56 us
  other arithmetic: 11.5 us -> 1.56 us
  Pallas kernels: 0 us -> 6.94 us
  matrix products: 5.32 us -> 0 us
    all_to_all x5 -> x3, blocking collectives: 107 us -> 54.8 us  [spread(): return lax.all_to_all(blocks, 'tp', 0, 0, axis_index_groups=GROUPS)]
    all_to_all x0 -> x2, waiting for transfers between devices: none -> 29.6 us  [the longest x1 18.6 us: shards(): lax.all_to_all(jnp.broadcast_to(message[None], (fsdp,) + message.shape),...]
    all_to_all x0 -> x2, starting transfers between devices: none -> 14.3 us  [the longest x1 10.8 us: shards(): lax.all_to_all(jnp.broadcast_to(message[None], (fsdp,) + message.shape),...]
    pallas_call x0 -> x6, Pallas kernels: none -> 6.94 us  [the longest x4 4 us: shards(): pl.pallas_call(step_kernel, out_shape=jax.ShapeDtypeStruct((2, half, cols...]
    transpose x4 -> x0, local copies, waits for them, and re-layouts: 6.45 us -> none  [shards(): normed.transpose(1, 0, 2).reshape(rows, tp * cols)]
    convert_element_type x8 -> x0, other arithmetic: 6.33 us -> none  [the longest x4 5.77 us: shards(): normed = (whole * scale * gain).astype(jnp.bfloat16)]
    dot_general x5 -> x0, matrix products: 5.32 us -> none  [the longest x1 2.99 us: shards(): lax.dot_general(down, ups, (((1,), (1,)), ((), ())), preferred_element_ty...]
    all_gather x0 -> x2, blocking collectives: none -> 5.21 us  [the longest x1 3.1 us: shards(): swapped = lax.all_gather(done[:, 1], 'tp', axis=0, axis_index_groups=PAIRS)]
  transfers between devices with their start and end apart: 4 -> 4, of which waited for: 4 -> 3; matrix products, arithmetic and copies ran while one was open for 1% -> 2% of each run, Pallas kernels for 0% -> 0%
where the time goes in v2:
time: 136 us
  blocking collectives  60.1 us (44%)
  waiting for transfers between devices  32.8 us (24%)
  starting transfers between devices  28.9 us (21%)
  Pallas kernels  6.94 us (5%)
  local copies, waits for them, and re-layouts  4.56 us (3%)
  other arithmetic  1.56 us (1%)
    all_to_all x3, blocking collectives, spread(): return lax.all_to_all(blocks, 'tp', 0, 0, axis_index_groups=GROUPS)  54.8 us
    all_to_all x1, waiting for transfers between devices, shards(): lax.all_to_all(jnp.broadcast_to(message[None], (fsdp,) + message.shape),...  18.6 us
    all_to_all x1, waiting for transfers between devices, spread(): return lax.all_to_all(blocks, 'tp', 0, 0, axis_index_groups=GROUPS)  11 us
    all_to_all x1, starting transfers between devices, shards(): lax.all_to_all(jnp.broadcast_to(message[None], (fsdp,) + message.shape),...  10.8 us
    ppermute x1, starting transfers between devices, shards(): mate = lax.ppermute(base_weight[0], 'tp', SWAP)  8.79 us
    ppermute x1, starting transfers between devices, shards(): other = lax.ppermute(own, 'tp', SWAP)  5.8 us
    pallas_call x4, Pallas kernels, shards(): pl.pallas_call(step_kernel, out_shape=jax.ShapeDtypeStruct((2, half, cols...  4 us
    all_to_all x1, starting transfers between devices, spread(): return lax.all_to_all(blocks, 'tp', 0, 0, axis_index_groups=GROUPS)  3.49 us
  transfers between devices with their start and end apart: 4, of which 3 were waited for; matrix products, arithmetic and copies ran while one was open for 2% of the time, Pallas kernels for 0%

profile of v2, /device:TPU:1, one launch (start us, length us, event | category | flops | bytes accessed | tf_op | source)
XLA Modules:
  0.0 135.7 jit_solution(682083806149300049)
XLA Ops:
  0.6 8.8 %collective-permute-start = (bf16[4096,256]{1,0:T(8,128)(2,1)}, bf16[4096,256]{1,0:T(8,128)(2,1)S(1)}, u32[]{:S(2)}, u32[]{:S(2)}) collective-permute-start(bf16[4096,256]{1,0:T(8,128)(2,1)} %bitcast.25), channel_id=1, source_target_pairs={{0,1},{1,0},{2,3},{3,2},{4,5},{5,4},{6,7},{7,6},{8,9},{9,8},{10,11... | collective-permute-start | bytes 6291464 | tf_op jit(solution)/shard_map/ppermute | solution.py:95
  9.4 0.7 dynamic-slice_bitcast_fusion.2
  10.1 0.7 negate_bitcast_fusion
  10.9 0.7 broadcast_in_dim.33
  11.6 10.8 %all-to-all-start = ((bf16[32,16,256]{2,1,0:T(8,128)(2,1)}), bf16[32,16,256]{2,1,0:T(8,128)(2,1)S(1)}, u32[]{:S(2)}, u32[]{:S(2)}) async-start(bf16[32,16,256]{2,1,0:T(8,128)(2,1)} %broadcast_in_dim.33), calls=%async_computation | async-start | bytes 524288 | tf_op jit(solution)/shard_map/all_to_all | solution.py:106
  22.4 2.1 %all-gather = bf16[256,256]{1,0:T(8,128)(2,1)S(1)} all-gather(bf16[128,256]{1,0:T(8,128)(2,1)} %param.7), channel_id=2, replica_groups={{0,1},{2,3},{4,5},{6,7},{8,9},{10,11},{12,13},{14,15},{16,17},{18,19},{..., dimensions={0}, use_global_device_ids=true | all-gather | bytes 196608 | tf_op jit(solution)/shard_map/all_gather | solution.py:96
  24.6 18.6 %all-to-all-done.got_ref = bf16[32,16,256]{2,1,0:T(8,128)(2,1)S(1)} async-done(((bf16[32,16,256]{2,1,0:T(8,128)(2,1)}), bf16[32,16,256]{2,1,0:T(8,128)(2,1)S(1)}, u32[]{:S(2)}, u32[]{:S(2)}) %all-to-all-start) | async-done | bytes 262176 | tf_op jit(solution)/shard_map/all_to_all | solution.py:106
  43.2 0.3 pack.1
  43.5 0.0 copy-start.3
  43.5 0.0 copy-start.2
  43.5 0.0 collective-permute-done.mate_ref
  43.5 27.6 %all_to_all.25.own_ref.x_ref = bf16[8,416,256]{2,1,0:T(8,128)(2,1)S(1)} all-to-all(bf16[8,416,256]{2,1,0:T(8,128)(2,1)S(1)} %pack.1), channel_id=1, replica_groups={{0,2,4,6,8,10,12,14},{1,3,5,7,9,11,13,15},{16,18,20,22,24,26,28,30},{17..., dimensions={0} | all-to-all | bytes 3407872 | tf_op jit(solution)/shard_map/all_to_all | solution.py:20
  71.1 5.8 %collective-permute-start.1 = (bf16[8,416,256]{2,1,0:T(8,128)(2,1)S(1)}, bf16[8,416,256]{2,1,0:T(8,128)(2,1)S(1)}, u32[]{:S(2)}, u32[]{:S(2)}) collective-permute-start(bf16[8,416,256]{2,1,0:T(8,128)(2,1)S(1)} %all_to_all.25.own_ref.x_ref), channel_id=1, source_target_pairs={{0,1},{1,0},{2,3},{3,2},{4,5},{5,4},{6,7},{7,6},{8,9},{9,8},{10,11... | collective-permute-start | bytes 5111816 | tf_op jit(solution)/shard_map/ppermute | solution.py:118
  76.9 0.0 copy-done.3
  76.9 3.2 %collective-permute-done.1.other_ref = bf16[8,416,256]{2,1,0:T(8,128)(2,1)S(1)} collective-permute-done((bf16[8,416,256]{2,1,0:T(8,128)(2,1)S(1)}, bf16[8,416,256]{2,1,0:T(8,128)(2,1)S(1)}, u32[]{:S(2)}, u32[]{:S(2)}) %collective-permute-start.1) | collective-permute-done | bytes 1703968 | tf_op jit(solution)/shard_map/ppermute | solution.py:118
  80.1 0.0 copy-done.2
  80.1 2.6 %merge.1 = (bf16[16,256,512]{2,1,0:T(8,128)(2,1)S(1)}, bf16[4096,256]{1,0:T(8,128)(2,1)}) custom-call(s32[1]{0:T(128)} %bitcast.6.core_ref, bf16[8,416,256]{2,1,0:T(8,128)(2,1)S(1)} %all_to_all.25.own_ref.x_ref, bf16[8,416,256]{2,1,0:T(8,128)(2,1)S(1)} %collective-permute-done.1.other_ref, bf16[4096,256]{1,0:T(8,128)(2,1)S(1)} %bitcast.26, ...), custom_call_target="tpu_custom_call" | custom-call | tf_op jit(solution)/shard_map/merge/pallas_call | solution.py:119
  82.8 0.0 copy-start
  82.8 1.0 step.4.mine_ref
  83.8 14.1 %all_to_all.26.x_ref = bf16[8,128,256]{2,1,0:T(8,128)(2,1)S(1)} all-to-all(bf16[8,128,256]{2,1,0:T(8,128)(2,1)S(1)} %broadcast_in_dim.36), channel_id=1, replica_groups={{0,2,4,6,8,10,12,14},{1,3,5,7,9,11,13,15},{16,18,20,22,24,26,28,30},{17..., dimensions={0} | all-to-all | bytes 1048576 | tf_op jit(solution)/shard_map/all_to_all | solution.py:20
  98.0 1.0 step.5.mine_ref
  99.0 13.1 %all_to_all.27.x_ref = bf16[8,128,256]{2,1,0:T(8,128)(2,1)S(1)} all-to-all(bf16[8,128,256]{2,1,0:T(8,128)(2,1)S(1)} %broadcast_in_dim.38), channel_id=1, replica_groups={{0,2,4,6,8,10,12,14},{1,3,5,7,9,11,13,15},{16,18,20,22,24,26,28,30},{17..., dimensions={0} | all-to-all | bytes 1048576 | tf_op jit(solution)/shard_map/all_to_all | solution.py:20
  112.2 0.0 copy-done
  112.2 1.0 step.6.mine_ref
  113.2 0.8 broadcast_in_dim.40
  114.0 3.5 %all-to-all-start.4 = ((bf16[8,128,256]{2,1,0:T(8,128)(2,1)}), bf16[8,128,256]{2,1,0:T(8,128)(2,1)S(1)}, u32[]{:S(2)}, u32[]{:S(2)}) async-start(bf16[8,128,256]{2,1,0:T(8,128)(2,1)} %broadcast_in_dim.40), calls=%async_computation.4 | async-start | bytes 1048576 | tf_op jit(solution)/shard_map/all_to_all | solution.py:20
  117.5 11.0 %all-to-all-done.4.x_ref = bf16[8,128,256]{2,1,0:T(8,128)(2,1)S(1)} async-done(((bf16[8,128,256]{2,1,0:T(8,128)(2,1)}), bf16[8,128,256]{2,1,0:T(8,128)(2,1)S(1)}, u32[]{:S(2)}, u32[]{:S(2)}) %all-to-all-start.4) | async-done | bytes 524320 | tf_op jit(solution)/shard_map/all_to_all | solution.py:20
  128.5 0.0 copy-start.1
  128.5 2.2 %copy-done.1 = bf16[16,256,512]{2,1,0:T(8,128)(2,1)S(1)} copy-done((bf16[16,256,512]{2,1,0:T(8,128)(2,1)S(1)}, bf16[16,256,512]{2,1,0:T(8,128)(2,1)}, u32[]{:S(2)}) %copy-start.1) | copy-done | bytes 4194328
  130.7 1.0 step.7
  131.8 3.1 %all-gather.1 = bf16[8,1,64,256]{3,2,1,0:T(8,128)(2,1)S(1)} all-gather(bf16[4,1,64,256]{3,2,1,0:T(8,128)(2,1)S(1)} %get-tuple-element.11), channel_id=3, replica_groups={{0,1},{2,3},{4,5},{6,7},{8,9},{10,11},{12,13},{14,15},{16,17},{18,19},{..., dimensions={0}, use_global_device_ids=true | all-gather | bytes 393216 | tf_op jit(solution)/shard_map/all_gather | solution.py:150
  134.9 0.8 reverse_select_fusion
  (10 shorter events, 0.2 us)
Async XLA Ops:
  0.6 42.9 %collective-permute-start = (bf16[4096,256]{1,0:T(8,128)(2,1)}, bf16[4096,256]{1,0:T(8,128)(2,1)S(1)}, u32[]{:S(2)}, u32[]{:S(2)}) collective-permute-start(bf16[4096,256]{1,0:T(8,128)(2,1)} %bitcast.25), channel_id=1, source_target_pairs={{0,1},{1,0},{2,3},{3,2},{4,5},{5,4},{6,7},{7,6},{8,9},{9,8},{10,11... | collective-permute-start | bytes 6291464 | tf_op jit(solution)/shard_map/ppermute | solution.py:95
  11.6 31.6 %all-to-all-start = ((bf16[32,16,256]{2,1,0:T(8,128)(2,1)}), bf16[32,16,256]{2,1,0:T(8,128)(2,1)S(1)}, u32[]{:S(2)}, u32[]{:S(2)}) async-start(bf16[32,16,256]{2,1,0:T(8,128)(2,1)} %broadcast_in_dim.33), calls=%async_computation | async-start | bytes 524288 | tf_op jit(solution)/shard_map/all_to_all | solution.py:106
  43.5 33.4 %copy-start.3 = (f32[1,4096]{1,0:T(1,128)S(1)}, f32[1,4096]{1,0:T(1,128)}, u32[]{:S(2)}) copy-start(f32[1,4096]{1,0:T(1,128)} %param.13) | copy-start | bytes 49156
  43.5 36.6 %copy-start.2 = (bf16[1,4096,256]{2,1,0:T(8,128)(2,1)S(1)}, bf16[1,4096,256]{2,1,0:T(8,128)(2,1)}, u32[]{:S(2)}) copy-start(bf16[1,4096,256]{2,1,0:T(8,128)(2,1)} %param.8) | copy-start | bytes 6291460
  71.1 9.0 %collective-permute-start.1 = (bf16[8,416,256]{2,1,0:T(8,128)(2,1)S(1)}, bf16[8,416,256]{2,1,0:T(8,128)(2,1)S(1)}, u32[]{:S(2)}, u32[]{:S(2)}) collective-permute-start(bf16[8,416,256]{2,1,0:T(8,128)(2,1)S(1)} %all_to_all.25.own_ref.x_ref), channel_id=1, source_target_pairs={{0,1},{1,0},{2,3},{3,2},{4,5},{5,4},{6,7},{7,6},{8,9},{9,8},{10,11... | collective-permute-start | bytes 5111816 | tf_op jit(solution)/shard_map/ppermute | solution.py:118
  82.8 29.4 %copy-start = (bf16[16,256,512]{2,1,0:T(8,128)(2,1)}, bf16[16,256,512]{2,1,0:T(8,128)(2,1)S(1)}, u32[]{:S(2)}) copy-start(bf16[16,256,512]{2,1,0:T(8,128)(2,1)S(1)} %get-tuple-element.8.weight_ref) | copy-start | bytes 12582916
  114.0 14.5 %all-to-all-start.4 = ((bf16[8,128,256]{2,1,0:T(8,128)(2,1)}), bf16[8,128,256]{2,1,0:T(8,128)(2,1)S(1)}, u32[]{:S(2)}, u32[]{:S(2)}) async-start(bf16[8,128,256]{2,1,0:T(8,128)(2,1)} %broadcast_in_dim.40), calls=%async_computation.4 | async-start | bytes 1048576 | tf_op jit(solution)/shard_map/all_to_all | solution.py:20
  128.5 2.2 %copy-start.1 = (bf16[16,256,512]{2,1,0:T(8,128)(2,1)S(1)}, bf16[16,256,512]{2,1,0:T(8,128)(2,1)}, u32[]{:S(2)}) copy-start(bf16[16,256,512]{2,1,0:T(8,128)(2,1)} %copy-done) | copy-start | bytes 12582916

commit v3 on v2

--- a/solution.py
+++ b/solution.py
@@ -10,10 +10,12 @@
 GROUPS = [[2 * chip + core for chip in range(CHIPS)] for core in range(2)]
 PAIRS = [[2 * chip, 2 * chip + 1] for chip in range(CHIPS)]
 SWAP = [(i, i ^ 1) for i in range(2 * CHIPS)]
+LINES = [[16 * low + z for z in range(16)] for low in range(2)]
+RUNGS = [[z, 16 + z] for z in range(16)]
 
 VMEM = pl.BlockSpec(memory_space=pltpu.VMEM)
 SMEM = pl.BlockSpec(memory_space=pltpu.SMEM)
-ROOM = pltpu.CompilerParams(vmem_limit_bytes=24 * 1024 * 1024)
+ROOM = pltpu.CompilerParams(vmem_limit_bytes=16 * 1024 * 1024)
 
 
 def spread(blocks):
@@ -84,6 +86,17 @@
         out_ref[half] = (mine_ref[half].astype(jnp.float32) + branch).astype(jnp.bfloat16)
 
 
+def finish_kernel(core_ref, swapped_ref, *refs):
+    core = core_ref[0]
+    out_ref = refs[-1]
+    half = swapped_ref.shape[1]
+    mine = pl.ds(pl.multiple_of(core * half, half), half)
+    theirs = pl.ds(pl.multiple_of((1 - core) * half, half), half)
+    for step in range(STEPS):
+        out_ref[step, mine, :] = refs[step][0]
+        out_ref[step, theirs, :] = swapped_ref[step]
+
+
 def shards(tokens, base_weight, a_old, a_new, b_old, b_new, gains):
     rows, cols = tokens.shape
     tp = lax.axis_size("tp")
@@ -92,8 +105,9 @@
     core = lax.rem(t, 2)
     half = rows // 2
 
-    mate = lax.ppermute(base_weight[0], "tp", SWAP)
     both = lax.all_gather(tokens, "tp", axis=0, axis_index_groups=PAIRS)
+    both, base = lax.optimization_barrier((both, base_weight[0]))
+    mate = lax.ppermute(base, "tp", SWAP)
     both = lax.dynamic_slice_in_dim(both, core * half, half, 1)
     stream = jnp.where(core == 0, both, both[::-1])
 
@@ -103,7 +117,11 @@
     pick_b = lambda b: lax.dynamic_slice_in_dim(b[0], t * share, share, 0)
     up = jnp.concatenate([pick_b(b_new), -pick_b(b_old)], 1)
     message = jnp.concatenate([pick_a(a_new), pick_a(a_old), up], 0)
-    got = lax.all_to_all(jnp.broadcast_to(message[None], (fsdp,) + message.shape), "fsdp", 0, 0)
+    line = len(LINES[0])
+    got = lax.all_to_all(
+        jnp.broadcast_to(message[None], (line,) + message.shape), "fsdp", 0, 0, axis_index_groups=LINES
+    )
+    got = lax.all_gather(got, "fsdp", axis=0, tiled=True, axis_index_groups=RUNGS)
     packed = pl.pallas_call(
         pack_kernel,
         out_shape=jax.ShapeDtypeStruct((CHIPS, rows + cols + 4 * share, cols), jnp.bfloat16),
@@ -146,12 +164,16 @@
         )(x, weights, gain, stream)
         results.append(stream)
 
-    done = jnp.stack(results)
-    swapped = lax.all_gather(done[:, 1], "tp", axis=0, axis_index_groups=PAIRS)
-    swapped = lax.dynamic_index_in_dim(swapped, 1 - core, 0, keepdims=False)
-    ends = jnp.stack([done[:, 0], swapped], 1)
-    ends = jnp.where(core == 0, ends, ends[:, ::-1])
-    return ends.reshape(STEPS, rows, cols), merged[None]
+    swapped = lax.ppermute(jnp.stack([result[1] for result in results]), "tp", SWAP)
+    ends = pl.pallas_call(
+        finish_kernel,
+        out_shape=jax.ShapeDtypeStruct((STEPS, rows, cols), jnp.bfloat16),
+        in_specs=[SMEM] + [VMEM] * (STEPS + 1),
+        out_specs=VMEM,
+        name="finish",
+        compiler_params=ROOM,
+    )(core[None], swapped, *results)
+    return ends, merged[None]
 
 
 def solution(mesh):

time: 136 us -> 135 us (level)
  blocking collectives: 60.1 us -> 66.9 us
  waiting for transfers between devices: 32.8 us -> 27.2 us
  starting transfers between devices: 28.9 us -> 25.9 us
    all_to_all x1, waiting for transfers between devices: 18.6 us -> 12.1 us  [shards(): lax.all_to_all(jnp.broadcast_to(message[None], (line,) + message.shape),...]
    all_gather x1, blocking collectives: 2.11 us -> 8.64 us  [shards(): both = lax.all_gather(tokens, 'tp', axis=0, axis_index_groups=PAIRS)]
    ppermute x1 -> x2, starting transfers between devices: 8.79 us -> 5.63 us  [the longest x1 3.37 us: shards(): lax.ppermute(jnp.stack([result[1] for result in results]), 'tp', SWAP)]
    ppermute x1, starting transfers between devices: 5.8 us -> 7.2 us  [shards(): other = lax.ppermute(own, 'tp', SWAP)]
    all_gather x1, blocking collectives: 3.1 us -> 4.48 us  [shards(): lax.all_gather(got, 'fsdp', axis=0, tiled=True, axis_index_groups=RUNGS)]
  transfers between devices with their start and end apart: 4 -> 5, of which waited for: 3 -> 4; matrix products, arithmetic and copies ran while one was open for 2% -> 2% of each run, Pallas kernels for 0% -> 0%
where the time goes in v3:
time: 135 us; the launch traced here: 134 us
  blocking collectives  66.9 us (50%)
  waiting for transfers between devices  27.2 us (20%)
  starting transfers between devices  25.9 us (19%)
  Pallas kernels  7.66 us (6%)
  local copies, waits for them, and re-layouts  4.5 us (3%)
    all_to_all x3, blocking collectives, spread(): return lax.all_to_all(blocks, 'tp', 0, 0, axis_index_groups=GROUPS)  53.7 us
    all_to_all x1, waiting for transfers between devices, shards(): lax.all_to_all(jnp.broadcast_to(message[None], (line,) + message.shape),...  12.1 us
    all_to_all x1, waiting for transfers between devices, spread(): return lax.all_to_all(blocks, 'tp', 0, 0, axis_index_groups=GROUPS)  11 us
    all_to_all x1, starting transfers between devices, shards(): lax.all_to_all(jnp.broadcast_to(message[None], (line,) + message.shape),...  9.54 us
    all_gather x1, blocking collectives, shards(): both = lax.all_gather(tokens, 'tp', axis=0, axis_index_groups=PAIRS)  8.64 us
    ppermute x1, starting transfers between devices, shards(): other = lax.ppermute(own, 'tp', SWAP)  7.2 us
    all_gather x1, blocking collectives, shards(): lax.all_gather(got, 'fsdp', axis=0, tiled=True, axis_index_groups=RUNGS)  4.48 us
    pallas_call x4, Pallas kernels, shards(): pl.pallas_call(step_kernel, out_shape=jax.ShapeDtypeStruct((2, half, cols...  4 us
  transfers between devices with their start and end apart: 5, of which 4 were waited for; matrix products, arithmetic and copies ran while one was open for 2% of the time, Pallas kernels for 0%

profile of v3, /device:TPU:1, one launch (start us, length us, event | category | flops | bytes accessed | tf_op | source)
XLA Modules:
  0.0 133.7 jit_solution(8075825657420139227)
XLA Ops:
  0.6 8.6 %all-gather = bf16[256,256]{1,0:T(8,128)(2,1)S(1)} all-gather(bf16[128,256]{1,0:T(8,128)(2,1)} %param.7), channel_id=2, replica_groups={{0,1},{2,3},{4,5},{6,7},{8,9},{10,11},{12,13},{14,15},{16,17},{18,19},{..., dimensions={0}, use_global_device_ids=true | all-gather | bytes 196608 | tf_op jit(solution)/shard_map/all_gather | solution.py:108
  9.3 2.3 %collective-permute-start = (bf16[4096,256]{1,0:T(8,128)(2,1)}, bf16[4096,256]{1,0:T(8,128)(2,1)S(1)}, u32[]{:S(2)}, u32[]{:S(2)}) collective-permute-start(bf16[4096,256]{1,0:T(8,128)(2,1)} %bitcast.17), channel_id=1, source_target_pairs={{0,1},{1,0},{2,3},{3,2},{4,5},{5,4},{6,7},{7,6},{8,9},{9,8},{10,11... | collective-permute-start | bytes 6291464 | tf_op jit(solution)/shard_map/ppermute | solution.py:110
  11.5 0.7 dynamic-slice_bitcast_fusion.1
  12.2 0.7 negate_bitcast_fusion
  13.0 0.7 broadcast_in_dim.35
  13.6 9.5 %all-to-all-start = ((bf16[16,16,256]{2,1,0:T(8,128)(2,1)}), bf16[16,16,256]{2,1,0:T(8,128)(2,1)S(1)}, u32[]{:S(2)}, u32[]{:S(2)}) async-start(bf16[16,16,256]{2,1,0:T(8,128)(2,1)} %broadcast_in_dim.35), calls=%async_computation | async-start | bytes 262144 | tf_op jit(solution)/shard_map/all_to_all | solution.py:121
  23.2 12.1 %all-to-all-done = bf16[16,16,256]{2,1,0:T(8,128)(2,1)S(1)} async-done(((bf16[16,16,256]{2,1,0:T(8,128)(2,1)}), bf16[16,16,256]{2,1,0:T(8,128)(2,1)S(1)}, u32[]{:S(2)}, u32[]{:S(2)}) %all-to-all-start) | async-done | bytes 131104 | tf_op jit(solution)/shard_map/all_to_all | solution.py:121
  35.3 4.5 %all_gather.9.got_ref = bf16[32,16,256]{2,1,0:T(8,128)(2,1)S(1)} all-gather(bf16[16,16,256]{2,1,0:T(8,128)(2,1)S(1)} %all-to-all-done), channel_id=1, replica_groups={{0,256},{16,272},{32,288},{48,304},{64,320},{80,336},{96,352},{112,368}..., dimensions={0}, use_global_device_ids=true | all-gather | bytes 393216 | tf_op jit(solution)/shard_map/all_gather | solution.py:124
  39.8 0.3 pack.1
  40.1 0.0 copy-start.3
  40.1 0.0 copy-start.2
  40.1 0.0 collective-permute-done.mate_ref
  40.1 26.5 %all_to_all.25.own_ref.x_ref = bf16[8,416,256]{2,1,0:T(8,128)(2,1)S(1)} all-to-all(bf16[8,416,256]{2,1,0:T(8,128)(2,1)S(1)} %pack.1), channel_id=1, replica_groups={{0,2,4,6,8,10,12,14},{1,3,5,7,9,11,13,15},{16,18,20,22,24,26,28,30},{17..., dimensions={0} | all-to-all | bytes 3407872 | tf_op jit(solution)/shard_map/all_to_all | solution.py:22
  66.6 7.2 %collective-permute-start.1 = (bf16[8,416,256]{2,1,0:T(8,128)(2,1)S(1)}, bf16[8,416,256]{2,1,0:T(8,128)(2,1)S(1)}, u32[]{:S(2)}, u32[]{:S(2)}) collective-permute-start(bf16[8,416,256]{2,1,0:T(8,128)(2,1)S(1)} %all_to_all.25.own_ref.x_ref), channel_id=1, source_target_pairs={{0,1},{1,0},{2,3},{3,2},{4,5},{5,4},{6,7},{7,6},{8,9},{9,8},{10,11... | collective-permute-start | bytes 5111816 | tf_op jit(solution)/shard_map/ppermute | solution.py:136
  73.8 0.0 copy-done.3
  73.8 3.2 %collective-permute-done.1.other_ref = bf16[8,416,256]{2,1,0:T(8,128)(2,1)S(1)} collective-permute-done((bf16[8,416,256]{2,1,0:T(8,128)(2,1)S(1)}, bf16[8,416,256]{2,1,0:T(8,128)(2,1)S(1)}, u32[]{:S(2)}, u32[]{:S(2)}) %collective-permute-start.1) | collective-permute-done | bytes 1703968 | tf_op jit(solution)/shard_map/ppermute | solution.py:136
  77.0 0.0 copy-done.2
  77.0 2.7 %merge.1 = (bf16[16,256,512]{2,1,0:T(8,128)(2,1)S(1)}, bf16[4096,256]{1,0:T(8,128)(2,1)}) custom-call(s32[1]{0:T(128)} %bitcast.core_ref, bf16[8,416,256]{2,1,0:T(8,128)(2,1)S(1)} %all_to_all.25.own_ref.x_ref, bf16[8,416,256]{2,1,0:T(8,128)(2,1)S(1)} %collective-permute-done.1.other_ref, bf16[4096,256]{1,0:T(8,128)(2,1)S(1)} %bitcast.18, ...), custom_call_target="tpu_custom_call" | custom-call | tf_op jit(solution)/shard_map/merge/pallas_call | solution.py:137
  79.7 1.0 step.4.mine_ref.refs_0_
  80.7 14.1 %all_to_all.26.x_ref = bf16[8,128,256]{2,1,0:T(8,128)(2,1)S(1)} all-to-all(bf16[8,128,256]{2,1,0:T(8,128)(2,1)S(1)} %broadcast_in_dim.37), channel_id=1, replica_groups={{0,2,4,6,8,10,12,14},{1,3,5,7,9,11,13,15},{16,18,20,22,24,26,28,30},{17..., dimensions={0} | all-to-all | bytes 1048576 | tf_op jit(solution)/shard_map/all_to_all | solution.py:22
  94.9 1.0 step.5.mine_ref.refs_1_
  95.9 13.1 %all_to_all.27.x_ref = bf16[8,128,256]{2,1,0:T(8,128)(2,1)S(1)} all-to-all(bf16[8,128,256]{2,1,0:T(8,128)(2,1)S(1)} %broadcast_in_dim.39), channel_id=1, replica_groups={{0,2,4,6,8,10,12,14},{1,3,5,7,9,11,13,15},{16,18,20,22,24,26,28,30},{17..., dimensions={0} | all-to-all | bytes 1048576 | tf_op jit(solution)/shard_map/all_to_all | solution.py:22
  109.0 0.0 copy-done
  109.1 1.0 step.6.mine_ref.refs_2_
  110.1 0.8 broadcast_in_dim.41
  110.9 3.5 %all-to-all-start.4 = ((bf16[8,128,256]{2,1,0:T(8,128)(2,1)}), bf16[8,128,256]{2,1,0:T(8,128)(2,1)S(1)}, u32[]{:S(2)}, u32[]{:S(2)}) async-start(bf16[8,128,256]{2,1,0:T(8,128)(2,1)} %broadcast_in_dim.41), calls=%async_computation.4 | async-start | bytes 1048576 | tf_op jit(solution)/shard_map/all_to_all | solution.py:22
  114.4 11.0 %all-to-all-done.4.x_ref = bf16[8,128,256]{2,1,0:T(8,128)(2,1)S(1)} async-done(((bf16[8,128,256]{2,1,0:T(8,128)(2,1)}), bf16[8,128,256]{2,1,0:T(8,128)(2,1)S(1)}, u32[]{:S(2)}, u32[]{:S(2)}) %all-to-all-start.4) | async-done | bytes 524320 | tf_op jit(solution)/shard_map/all_to_all | solution.py:22
  125.4 2.2 %copy-done.1 = bf16[16,256,512]{2,1,0:T(8,128)(2,1)S(1)} copy-done((bf16[16,256,512]{2,1,0:T(8,128)(2,1)S(1)}, bf16[16,256,512]{2,1,0:T(8,128)(2,1)}, u32[]{:S(2)}) %copy-start.1) | copy-done | bytes 4194328
  127.6 1.0 step.7.refs_3_
  128.6 3.4 %collective-permute-start.2 = (bf16[4,64,256]{2,1,0:T(8,128)(2,1)S(1)}, bf16[4,64,256]{2,1,0:T(8,128)(2,1)S(1)}, u32[]{:S(2)}, u32[]{:S(2)}) collective-permute-start(bf16[4,64,256]{2,1,0:T(8,128)(2,1)S(1)} %pad_maximum_fusion), channel_id=1, source_target_pairs={{0,1},{1,0},{2,3},{3,2},{4,5},{5,4},{6,7},{7,6},{8,9},{9,8},{10,11... | collective-permute-start | bytes 393224 | tf_op jit(solution)/shard_map/ppermute | solution.py:167
  132.0 1.0 collective-permute-done.2.swapped_ref
  133.0 0.7 finish.1
  (13 shorter events, 0.2 us)
Async XLA Ops:
  9.3 30.9 %collective-permute-start = (bf16[4096,256]{1,0:T(8,128)(2,1)}, bf16[4096,256]{1,0:T(8,128)(2,1)S(1)}, u32[]{:S(2)}, u32[]{:S(2)}) collective-permute-start(bf16[4096,256]{1,0:T(8,128)(2,1)} %bitcast.17), channel_id=1, source_target_pairs={{0,1},{1,0},{2,3},{3,2},{4,5},{5,4},{6,7},{7,6},{8,9},{9,8},{10,11... | collective-permute-start | bytes 6291464 | tf_op jit(solution)/shard_map/ppermute | solution.py:110
  13.6 21.7 %all-to-all-start = ((bf16[16,16,256]{2,1,0:T(8,128)(2,1)}), bf16[16,16,256]{2,1,0:T(8,128)(2,1)S(1)}, u32[]{:S(2)}, u32[]{:S(2)}) async-start(bf16[16,16,256]{2,1,0:T(8,128)(2,1)} %broadcast_in_dim.35), calls=%async_computation | async-start | bytes 262144 | tf_op jit(solution)/shard_map/all_to_all | solution.py:121
  40.1 33.7 %copy-start.3 = (f32[1,4096]{1,0:T(1,128)S(1)}, f32[1,4096]{1,0:T(1,128)}, u32[]{:S(2)}) copy-start(f32[1,4096]{1,0:T(1,128)} %param.13) | copy-start | bytes 49156
  40.1 36.9 %copy-start.2 = (bf16[1,4096,256]{2,1,0:T(8,128)(2,1)S(1)}, bf16[1,4096,256]{2,1,0:T(8,128)(2,1)}, u32[]{:S(2)}) copy-start(bf16[1,4096,256]{2,1,0:T(8,128)(2,1)} %param.8) | copy-start | bytes 6291460
  66.6 10.4 %collective-permute-start.1 = (bf16[8,416,256]{2,1,0:T(8,128)(2,1)S(1)}, bf16[8,416,256]{2,1,0:T(8,128)(2,1)S(1)}, u32[]{:S(2)}, u32[]{:S(2)}) collective-permute-start(bf16[8,416,256]{2,1,0:T(8,128)(2,1)S(1)} %all_to_all.25.own_ref.x_ref), channel_id=1, source_target_pairs={{0,1},{1,0},{2,3},{3,2},{4,5},{5,4},{6,7},{7,6},{8,9},{9,8},{10,11... | collective-permute-start | bytes 5111816 | tf_op jit(solution)/shard_map/ppermute | solution.py:136
  79.7 29.4 %copy-start = (bf16[16,256,512]{2,1,0:T(8,128)(2,1)}, bf16[16,256,512]{2,1,0:T(8,128)(2,1)S(1)}, u32[]{:S(2)}) copy-start(bf16[16,256,512]{2,1,0:T(8,128)(2,1)S(1)} %get-tuple-element.12.weight_ref) | copy-start | bytes 12582916
  110.9 14.5 %all-to-all-start.4 = ((bf16[8,128,256]{2,1,0:T(8,128)(2,1)}), bf16[8,128,256]{2,1,0:T(8,128)(2,1)S(1)}, u32[]{:S(2)}, u32[]{:S(2)}) async-start(bf16[8,128,256]{2,1,0:T(8,128)(2,1)} %broadcast_in_dim.41), calls=%async_computation.4 | async-start | bytes 1048576 | tf_op jit(solution)/shard_map/all_to_all | solution.py:22
  125.4 2.2 %copy-start.1 = (bf16[16,256,512]{2,1,0:T(8,128)(2,1)S(1)}, bf16[16,256,512]{2,1,0:T(8,128)(2,1)}, u32[]{:S(2)}) copy-start(bf16[16,256,512]{2,1,0:T(8,128)(2,1)} %copy-done) | copy-start | bytes 12582916
  128.6 4.3 %collective-permute-start.2 = (bf16[4,64,256]{2,1,0:T(8,128)(2,1)S(1)}, bf16[4,64,256]{2,1,0:T(8,128)(2,1)S(1)}, u32[]{:S(2)}, u32[]{:S(2)}) collective-permute-start(bf16[4,64,256]{2,1,0:T(8,128)(2,1)S(1)} %pad_maximum_fusion), channel_id=1, source_target_pairs={{0,1},{1,0},{2,3},{3,2},{4,5},{5,4},{6,7},{7,6},{8,9},{9,8},{10,11... | collective-permute-start | bytes 393224 | tf_op jit(solution)/shard_map/ppermute | solution.py:167

commit v4 on v3

v4 whole, which is shorter than its diff:
```python
import jax
import jax.numpy as jnp
from jax import lax
from jax.experimental import pallas as pl
from jax.experimental.pallas import tpu as pltpu
from jax.sharding import PartitionSpec as P

STEPS = 4
CHIPS = 8
GROUPS = [[2 * chip + core for chip in range(CHIPS)] for core in range(2)]
PAIRS = [[2 * chip, 2 * chip + 1] for chip in range(CHIPS)]
SWAP = [(i, i ^ 1) for i in range(2 * CHIPS)]
PLANES = [
    [(16 * (y % 2) + z) * 16 + 8 * (y // 2) + 2 * x + core for y in range(4) for x in range(4)]
    for z in range(16)
    for core in range(2)
]
SHIFTED = [
    ((16 * low + z) * 16 + t, (16 * low + (z + t // 2 + 8 * (t % 2)) % 16) * 16 + t)
    for low in range(2)
    for z in range(16)
    for t in range(16)
]


def relay(part):
    pairs = []
    for z in range(16):
        for low in range(2):
            for block in range(16):
                shift = (z - block) % 16
                source = (16 * low + z) * 16 + 2 * (shift % 8) + shift // 8
                target = 16 * ((block % 4 // 2) ^ part) + z
                pairs.append((source, target * 16 + 8 * low + 2 * (block // 4) + block % 2))
    return pairs


VMEM = pl.BlockSpec(memory_space=pltpu.VMEM)
SMEM = pl.BlockSpec(memory_space=pltpu.SMEM)
ROOM = pltpu.CompilerParams(vmem_limit_bytes=16 * 1024 * 1024)


def spread(blocks):
    return lax.all_to_all(blocks, "tp", 0, 0, axis_index_groups=GROUPS)


def block_kernel(a_new_ref, a_old_ref, b_new_ref, b_old_ref, out_ref):
    half, cols = out_ref.shape[0] // 2, out_ref.shape[1]
    new = a_new_ref[0].astype(jnp.float32)
    old = a_old_ref[0].astype(jnp.float32)
    slices = []
    for i in range(new.shape[1] // cols):
        slices += [new[:, i * cols : (i + 1) * cols], old[:, i * cols : (i + 1) * cols]]
    out_ref[:half, :] = jnp.concatenate(slices, 0).astype(jnp.bfloat16)
    out_ref[half:, :] = jnp.concatenate([b_new_ref[0], -b_old_ref[0]], 1)


def merge_kernel(place_ref, own_ref, other_ref, ups_ref, base_ref, mate_ref, weight_ref, merged_ref, up_ref):
    core, low, z = place_ref[0], place_ref[1], place_ref[2]
    cols = base_ref.shape[1]
    for left in range(2):
        for part in range(2):
            up_ref[lax.rem(part + low + core, 2), left] = ups_ref[left, part]
    goes = lax.broadcasted_iota(jnp.int32, (cols, cols), 0)
    comes = lax.broadcasted_iota(jnp.int32, (cols, cols), 1)
    chip = comes // 8 % 16
    shift = chip // 8 * 4 + chip % 4 + 8 * ((comes // 128 + core) % 2)
    block = chip // 4 % 2 * 16 + (z + 32 - shift) % 16
    place = comes // 4 % 2 * 128 + block * 4 + comes % 4
    order = jnp.where(place == goes, 1.0, 0.0).astype(jnp.bfloat16)
    up = jnp.dot(up_ref[...].reshape(2 * cols, cols), order, preferred_element_type=jnp.float32).astype(jnp.bfloat16)
    for pair in range(CHIPS):
        parts = [
            ref[:, 16 * pair : 16 * pair + 16, :].astype(jnp.float32).reshape(16, 2, 8, cols)
            for ref in (own_ref, other_ref)
        ]
        for right in range(2):
            down = jnp.concatenate([part[:, right].reshape(128, cols) for part in parts], 0)
            down = down.T.astype(jnp.bfloat16)
            delta = lax.dot_general(down, up, (((1,), (1,)), ((), ())), preferred_element_type=jnp.float32)
            t = 2 * pair + right
            rows = slice(t * cols, (t + 1) * cols)
            mine = (base_ref[rows, :].astype(jnp.float32) + delta[:, :cols]).astype(jnp.bfloat16)
            theirs = (mate_ref[rows, :].astype(jnp.float32) + delta[:, cols:]).astype(jnp.bfloat16)
            merged_ref[rows, :] = mine
            which = 2 * pair + lax.rem(right + core, 2)
            weight_ref[which, :, :cols] = mine
            weight_ref[which, :, cols:] = theirs


def step_kernel(x_ref, weight_ref, gain_ref, mine_ref, out_ref, _):
    _, rows, cols = mine_ref.shape
    blocks = weight_ref.shape[0]
    part = lambda i: x_ref[i // 2, (i % 2) * rows : (i % 2 + 1) * rows, :].astype(jnp.float32)
    squares = part(0) * part(0)
    for i in range(1, blocks):
        squares += part(i) * part(i)
    mean = jnp.sum(squares, axis=1, keepdims=True) / (blocks * cols)
    scale = lax.rsqrt(mean + 1e-06)
    total = jnp.zeros((rows, 2 * cols), jnp.float32)
    for i in range(blocks):
        normed = (part(i) * scale * gain_ref[i]).astype(jnp.bfloat16)
        total += jnp.dot(normed, weight_ref[i], preferred_element_type=jnp.float32)
    for half in range(2):
        branch = total[:, half * cols : (half + 1) * cols]
        out_ref[half] = (mine_ref[half].astype(jnp.float32) + branch).astype(jnp.bfloat16)


def finish_kernel(core_ref, swapped_ref, *refs):
    core = core_ref[0]
    out_ref = refs[-1]
    half = swapped_ref.shape[1]
    mine = pl.ds(pl.multiple_of(core * half, half), half)
    theirs = pl.ds(pl.multiple_of((1 - core) * half, half), half)
    for step in range(STEPS):
        out_ref[step, mine, :] = refs[step][0]
        out_ref[step, theirs, :] = swapped_ref[step]


def shards(tokens, base_weight, a_old, a_new, b_old, b_new, gains):
    rows, cols = tokens.shape
    tp = lax.axis_size("tp")
    t = lax.axis_index("tp")
    core = lax.rem(t, 2)
    half = rows // 2

    block = pl.pallas_call(
        block_kernel,
        out_shape=jax.ShapeDtypeStruct((2 * b_old.shape[1], cols), jnp.bfloat16),
        in_specs=[VMEM] * 4,
        out_specs=VMEM,
        name="block",
        compiler_params=ROOM,
    )(a_new, a_old, b_new, b_old)
    block = lax.ppermute(block, ("fsdp", "tp"), SHIFTED)

    both = lax.all_gather(tokens, "tp", axis=0, axis_index_groups=PAIRS)
    both, base = lax.optimization_barrier((both, base_weight[0]))
    mate = lax.ppermute(base, "tp", SWAP)
    both = lax.dynamic_slice_in_dim(both, core * half, half, 1)
    stream = jnp.where(core == 0, both, both[::-1])
    x = spread(jnp.broadcast_to(stream.reshape(1, rows, cols), (CHIPS, rows, cols)))
    block, x = lax.optimization_barrier((block, x))

    down, up = block[: block.shape[0] // 2], block[block.shape[0] // 2 :]
    ups = [lax.ppermute(up, ("fsdp", "tp"), relay(part)) for part in range(2)]
    own = jnp.broadcast_to(down[None], (len(PLANES[0]),) + down.shape)
    own = lax.all_to_all(own, ("fsdp", "tp"), 0, 0, axis_index_groups=PLANES)
    own, *ups = lax.optimization_barrier((own, *ups))
    other = lax.ppermute(own, "tp", SWAP)
    ups = lax.all_gather(jnp.stack(ups), "tp", axis=0, axis_index_groups=PAIRS)
    f = lax.axis_index("fsdp")
    place = jnp.stack([core, f // 16, f % 16])
    weights, merged = pl.pallas_call(
        merge_kernel,
        out_shape=(
            jax.ShapeDtypeStruct((tp, cols, 2 * cols), jnp.bfloat16),
            jax.ShapeDtypeStruct((tp * cols, cols), jnp.bfloat16),
        ),
        in_specs=[SMEM] + [VMEM] * 5,
        out_specs=(VMEM, VMEM),
        scratch_shapes=[pltpu.VMEM((2, 2, cols // 2, cols), jnp.bfloat16)],
        name="merge",
        compiler_params=ROOM,
    )(place, own, other, ups, base_weight[0], mate)

    gain = gains[0].reshape(CHIPS, 2, 1, cols)
    gain = jnp.where(core == 0, gain, gain[:, ::-1]).reshape(tp, 1, cols)
    results = []
    for step in range(STEPS):
        if step:
            x = spread(jnp.broadcast_to(stream.reshape(1, rows, cols), (CHIPS, rows, cols)))
        stream, weights = pl.pallas_call(
            step_kernel,
            out_shape=(
                jax.ShapeDtypeStruct((2, half, cols), jnp.bfloat16),
                jax.ShapeDtypeStruct(weights.shape, weights.dtype),
            ),
            in_specs=[VMEM] * 4,
            out_specs=(VMEM, VMEM),
            input_output_aliases={1: 1},
            name="step",
            compiler_params=ROOM,
        )(x, weights, gain, stream)
        results.append(stream)

    swapped = lax.ppermute(jnp.stack([result[1] for result in results]), "tp", SWAP)
    ends = pl.pallas_call(
        finish_kernel,
        out_shape=jax.ShapeDtypeStruct((STEPS, rows, cols), jnp.bfloat16),
        in_specs=[SMEM] + [VMEM] * (STEPS + 1),
        out_specs=VMEM,
        name="finish",
        compiler_params=ROOM,
    )(core[None], swapped, *results)
    return ends, merged[None]


def solution(mesh):
    placed = (
        P("fsdp", "tp"),
        P(None, None, "tp"),
        P(None, "fsdp", None),
        P(None, "fsdp", None),
        P(None, "fsdp", None),
        P(None, "fsdp", None),
        P(),
    )
    return jax.shard_map(
        shards,
        mesh=mesh,
        in_specs=placed,
        out_specs=(P(None, "fsdp", "tp"), P(None, None, "tp")),
        check_vma=False,
    )
```

time: 135 us -> 132 us (0.978)
  the two profiles are of different devices: /device:TPU:1 before, /device:TPU:33 now
where the time goes in v4:
time: 132 us; the launch traced here: 131 us
  starting transfers between devices  50 us (38%)
  blocking collectives  32.4 us (25%)
  waiting for transfers between devices  27.4 us (21%)
  local copies, waits for them, and re-layouts  11.6 us (9%)
  Pallas kernels  9.07 us (7%)
    all_to_all x2, blocking collectives, spread(): return lax.all_to_all(blocks, 'tp', 0, 0, axis_index_groups=GROUPS)  27.3 us
    ppermute x1, starting transfers between devices, shards(): block = lax.ppermute(block, ('fsdp', 'tp'), SHIFTED)  14.5 us
    ppermute x2, waiting for transfers between devices, shards(): ups = [lax.ppermute(up, ('fsdp', 'tp'), relay(part)) for part in range(2)]  13.4 us
    all_to_all x2, waiting for transfers between devices, spread(): return lax.all_to_all(blocks, 'tp', 0, 0, axis_index_groups=GROUPS)  11 us
    all_to_all x2, starting transfers between devices, spread(): return lax.all_to_all(blocks, 'tp', 0, 0, axis_index_groups=GROUPS)  10.1 us
    ppermute x2, starting transfers between devices, shards(): ups = [lax.ppermute(up, ('fsdp', 'tp'), relay(part)) for part in range(2)]  9.37 us
    unnamed x16, local copies, waits for them, and re-layouts  8.75 us
    all_to_all x1, starting transfers between devices, shards(): own = lax.all_to_all(own, ('fsdp', 'tp'), 0, 0, axis_index_groups=PLANES)  8.72 us
  transfers between devices with their start and end apart: 9, of which 5 were waited for; matrix products, arithmetic and copies ran while one was open for 1% of the time, Pallas kernels for 0%

profile of v4, /device:TPU:33, one launch (start us, length us, event | category | flops | bytes accessed | tf_op | source)
XLA Modules:
  0.0 131.4 jit_solution(11723485316596498598)
XLA Ops:
  0.6 2.4 %all-gather = bf16[256,256]{1,0:T(8,128)(2,1)S(1)} all-gather(bf16[128,256]{1,0:T(8,128)(2,1)} %param.7), channel_id=2, replica_groups={{0,1},{2,3},{4,5},{6,7},{8,9},{10,11},{12,13},{14,15},{16,17},{18,19},{..., dimensions={0}, use_global_device_ids=true | all-gather | bytes 196608 | tf_op jit(solution)/shard_map/all_gather | solution.py:137
  3.1 0.8 broadcast_in_dim.42
  3.9 6.7 %all-to-all-start = ((bf16[8,128,256]{2,1,0:T(8,128)(2,1)}), bf16[8,128,256]{2,1,0:T(8,128)(2,1)S(1)}, u32[]{:S(2)}, u32[]{:S(2)}) async-start(bf16[8,128,256]{2,1,0:T(8,128)(2,1)} %broadcast_in_dim.42), calls=%async_computation | async-start | bytes 1048576 | tf_op jit(solution)/shard_map/all_to_all | solution.py:44
  11.3 0.8 copy-done.4
  12.1 0.8 copy-done.5
  12.9 0.8 copy-done.6
  13.6 14.5 %collective-permute-start = (bf16[256,256]{1,0:T(8,128)(2,1)S(1)}, bf16[256,256]{1,0:T(8,128)(2,1)S(1)}, u32[]{:S(2)}, u32[]{:S(2)}) collective-permute-start(bf16[256,256]{1,0:T(8,128)(2,1)S(1)} %block.1), channel_id=1, source_target_pairs={{0,0},{1,129},{2,18},{3,147},{4,36},{5,165},{6,54},{7,183},{8,72},... | collective-permute-start | bytes 393224 | tf_op jit(solution)/shard_map/ppermute | solution.py:135
  28.2 1.9 %collective-permute-start.4 = (bf16[4096,256]{1,0:T(8,128)(2,1)}, bf16[4096,256]{1,0:T(8,128)(2,1)}, u32[]{:S(2)}, u32[]{:S(2)}) collective-permute-start(bf16[4096,256]{1,0:T(8,128)(2,1)} %bitcast.15), channel_id=1, source_target_pairs={{0,1},{1,0},{2,3},{3,2},{4,5},{5,4},{6,7},{7,6},{8,9},{9,8},{10,11... | collective-permute-start | bytes 6291464 | tf_op jit(solution)/shard_map/ppermute | solution.py:139
  30.1 2.0 %collective-permute-done = bf16[256,256]{1,0:T(8,128)(2,1)S(1)} collective-permute-done((bf16[256,256]{1,0:T(8,128)(2,1)S(1)}, bf16[256,256]{1,0:T(8,128)(2,1)S(1)}, u32[]{:S(2)}, u32[]{:S(2)}) %collective-permute-start) | collective-permute-done | bytes 131104 | tf_op jit(solution)/shard_map/ppermute | solution.py:135
  32.2 1.1 broadcast_in_dim.43
  33.2 8.7 %all-to-all-start.1 = ((bf16[16,128,256]{2,1,0:T(8,128)(2,1)}), bf16[16,128,256]{2,1,0:T(8,128)(2,1)S(1)}, u32[]{:S(2)}, u32[]{:S(2)}) async-start(bf16[16,128,256]{2,1,0:T(8,128)(2,1)} %broadcast_in_dim.43), calls=%async_computation.1 | async-start | bytes 2097152 | tf_op jit(solution)/shard_map/all_to_all | solution.py:148
  42.0 4.8 %collective-permute-start.1 = (bf16[128,256]{1,0:T(8,128)(2,1)S(1)}, bf16[128,256]{1,0:T(8,128)(2,1)S(1)}, u32[]{:S(2)}, u32[]{:S(2)}) collective-permute-start(bf16[128,256]{1,0:T(8,128)(2,1)S(1)} %get-tuple-element.34), channel_id=1, source_target_pairs={{0,0},{15,1},{13,256},{11,257},{9,2},{7,3},{5,258},{3,259},{1,4},{... | collective-permute-start | bytes 196616 | tf_op jit(solution)/shard_map/ppermute | solution.py:146
  46.8 4.6 %collective-permute-start.2 = (bf16[128,256]{1,0:T(8,128)(2,1)S(1)}, bf16[128,256]{1,0:T(8,128)(2,1)S(1)}, u32[]{:S(2)}, u32[]{:S(2)}) collective-permute-start(bf16[128,256]{1,0:T(8,128)(2,1)S(1)} %get-tuple-element.34), channel_id=1, source_target_pairs={{0,256},{15,257},{13,0},{11,1},{9,258},{7,259},{5,2},{3,3},{1,260}... | collective-permute-start | bytes 196616 | tf_op jit(solution)/shard_map/ppermute | solution.py:146
  51.4 3.6 %collective-permute-done.1 = bf16[128,256]{1,0:T(8,128)(2,1)S(1)} collective-permute-done((bf16[128,256]{1,0:T(8,128)(2,1)S(1)}, bf16[128,256]{1,0:T(8,128)(2,1)S(1)}, u32[]{:S(2)}, u32[]{:S(2)}) %collective-permute-start.1) | collective-permute-done | bytes 65568 | tf_op jit(solution)/shard_map/ppermute | solution.py:146
  55.0 9.8 %collective-permute-done.2 = bf16[128,256]{1,0:T(8,128)(2,1)S(1)} collective-permute-done((bf16[128,256]{1,0:T(8,128)(2,1)S(1)}, bf16[128,256]{1,0:T(8,128)(2,1)S(1)}, u32[]{:S(2)}, u32[]{:S(2)}) %collective-permute-start.2) | collective-permute-done | bytes 65568 | tf_op jit(solution)/shard_map/ppermute | solution.py:146
  64.8 1.9 %collective-permute-start.3 = (bf16[16,128,256]{2,1,0:T(8,128)(2,1)S(1)}, bf16[16,128,256]{2,1,0:T(8,128)(2,1)S(1)}, u32[]{:S(2)}, u32[]{:S(2)}) collective-permute-start(bf16[16,128,256]{2,1,0:T(8,128)(2,1)S(1)} %all-to-all-done.1.own_ref), channel_id=1, source_target_pairs={{0,1},{1,0},{2,3},{3,2},{4,5},{5,4},{6,7},{7,6},{8,9},{9,8},{10,11... | collective-permute-start | bytes 3145736 | tf_op jit(solution)/shard_map/ppermute | solution.py:150
  66.8 2.7 %all-gather.1 = bf16[4,128,256]{2,1,0:T(8,128)(2,1)S(1)} all-gather(bf16[2,128,256]{2,1,0:T(8,128)(2,1)S(1)} %pad_maximum_fusion), channel_id=3, replica_groups={{0,1},{2,3},{4,5},{6,7},{8,9},{10,11},{12,13},{14,15},{16,17},{18,19},{..., dimensions={0}, use_global_device_ids=true | all-gather | bytes 393216 | tf_op jit(solution)/shard_map/all_gather | solution.py:151
  69.5 1.6 %copy-done.2 = bf16[1,4096,256]{2,1,0:T(8,128)(2,1)S(1)} copy-done((bf16[1,4096,256]{2,1,0:T(8,128)(2,1)S(1)}, bf16[1,4096,256]{2,1,0:T(8,128)(2,1)}, u32[]{:S(2)}) %copy-start.2) | copy-done | bytes 2097176
  71.1 4.4 %merge.1 = (bf16[16,256,512]{2,1,0:T(8,128)(2,1)S(1)}, bf16[4096,256]{1,0:T(8,128)(2,1)}) custom-call(s32[3]{0:T(128)S(1)} %pad_add_fusion.place_ref, bf16[16,128,256]{2,1,0:T(8,128)(2,1)S(1)} %all-to-all-done.1.own_ref, bf16[16,128,256]{2,1,0:T(8,128)(2,1)S(1)} %collective-permute-done.3.other_ref, bf16[2,2,128,256]{3,2,1,0:T(8,128)(2,1)S(1)} %bitcast.17, ...), custom_call_target="tpu_custom_call" | custom-call | tf_op jit(solution)/shard_map/merge/pallas_call | solution.py:154
  75.5 1.0 step.4
  76.5 14.2 %all_to_all.25.x_ref = bf16[8,128,256]{2,1,0:T(8,128)(2,1)S(1)} all-to-all(bf16[8,128,256]{2,1,0:T(8,128)(2,1)S(1)} %broadcast_in_dim.45), channel_id=1, replica_groups={{0,2,4,6,8,10,12,14},{1,3,5,7,9,11,13,15},{16,18,20,22,24,26,28,30},{17..., dimensions={0} | all-to-all | bytes 1048576 | tf_op jit(solution)/shard_map/all_to_all | solution.py:44
  90.8 1.0 step.5
  91.8 13.1 %all_to_all.26.x_ref = bf16[8,128,256]{2,1,0:T(8,128)(2,1)S(1)} all-to-all(bf16[8,128,256]{2,1,0:T(8,128)(2,1)S(1)} %broadcast_in_dim.47), channel_id=1, replica_groups={{0,2,4,6,8,10,12,14},{1,3,5,7,9,11,13,15},{16,18,20,22,24,26,28,30},{17..., dimensions={0} | all-to-all | bytes 1048576 | tf_op jit(solution)/shard_map/all_to_all | solution.py:44
  104.9 1.0 step.6
  105.9 1.9 %copy-done = bf16[16,256,512]{2,1,0:T(8,128)(2,1)} copy-done((bf16[16,256,512]{2,1,0:T(8,128)(2,1)}, bf16[16,256,512]{2,1,0:T(8,128)(2,1)S(1)}, u32[]{:S(2)}) %copy-start) | copy-done | bytes 4194328
  107.8 0.8 broadcast_in_dim.49
  108.7 3.5 %all-to-all-start.4 = ((bf16[8,128,256]{2,1,0:T(8,128)(2,1)}), bf16[8,128,256]{2,1,0:T(8,128)(2,1)S(1)}, u32[]{:S(2)}, u32[]{:S(2)}) async-start(bf16[8,128,256]{2,1,0:T(8,128)(2,1)} %broadcast_in_dim.49), calls=%async_computation.4 | async-start | bytes 1048576 | tf_op jit(solution)/shard_map/all_to_all | solution.py:44
  112.2 11.0 %all-to-all-done.4.x_ref = bf16[8,128,256]{2,1,0:T(8,128)(2,1)S(1)} async-done(((bf16[8,128,256]{2,1,0:T(8,128)(2,1)}), bf16[8,128,256]{2,1,0:T(8,128)(2,1)S(1)}, u32[]{:S(2)}, u32[]{:S(2)}) %all-to-all-start.4) | async-done | bytes 524320 | tf_op jit(solution)/shard_map/all_to_all | solution.py:44
  123.2 2.2 %copy-done.1 = bf16[16,256,512]{2,1,0:T(8,128)(2,1)S(1)} copy-done((bf16[16,256,512]{2,1,0:T(8,128)(2,1)S(1)}, bf16[16,256,512]{2,1,0:T(8,128)(2,1)}, u32[]{:S(2)}) %copy-start.1) | copy-done | bytes 4194328
  125.4 1.0 step.7
  126.4 3.4 %collective-permute-start.5 = (bf16[4,64,256]{2,1,0:T(8,128)(2,1)S(1)}, bf16[4,64,256]{2,1,0:T(8,128)(2,1)S(1)}, u32[]{:S(2)}, u32[]{:S(2)}) collective-permute-start(bf16[4,64,256]{2,1,0:T(8,128)(2,1)S(1)} %pad_maximum_fusion.1), channel_id=1, source_target_pairs={{0,1},{1,0},{2,3},{3,2},{4,5},{5,4},{6,7},{7,6},{8,9},{9,8},{10,11... | collective-permute-start | bytes 393224 | tf_op jit(solution)/shard_map/ppermute | solution.py:187
  129.8 1.0 collective-permute-done.5.swapped_ref
  (29 shorter events, 1.8 us)
Async XLA Ops:
  0.6 66.2 %copy-start.7 = (f32[1,4096]{1,0:T(1,128)S(1)}, f32[1,4096]{1,0:T(1,128)}, u32[]{:S(2)}) copy-start(f32[1,4096]{1,0:T(1,128)} %param.13) | copy-start | bytes 49156
  3.9 28.2 %all-to-all-start = ((bf16[8,128,256]{2,1,0:T(8,128)(2,1)}), bf16[8,128,256]{2,1,0:T(8,128)(2,1)S(1)}, u32[]{:S(2)}, u32[]{:S(2)}) async-start(bf16[8,128,256]{2,1,0:T(8,128)(2,1)} %broadcast_in_dim.42), calls=%async_computation | async-start | bytes 1048576 | tf_op jit(solution)/shard_map/all_to_all | solution.py:44
  10.6 0.8 copy-start.3
  11.3 0.8 copy-start.4
  12.1 0.8 copy-start.5
  12.9 0.8 copy-start.6
  13.6 18.5 %collective-permute-start = (bf16[256,256]{1,0:T(8,128)(2,1)S(1)}, bf16[256,256]{1,0:T(8,128)(2,1)S(1)}, u32[]{:S(2)}, u32[]{:S(2)}) collective-permute-start(bf16[256,256]{1,0:T(8,128)(2,1)S(1)} %block.1), channel_id=1, source_target_pairs={{0,0},{1,129},{2,18},{3,147},{4,36},{5,165},{6,54},{7,183},{8,72},... | collective-permute-start | bytes 393224 | tf_op jit(solution)/shard_map/ppermute | solution.py:135
  28.2 41.3 %collective-permute-start.4 = (bf16[4096,256]{1,0:T(8,128)(2,1)}, bf16[4096,256]{1,0:T(8,128)(2,1)}, u32[]{:S(2)}, u32[]{:S(2)}) collective-permute-start(bf16[4096,256]{1,0:T(8,128)(2,1)} %bitcast.15), channel_id=1, source_target_pairs={{0,1},{1,0},{2,3},{3,2},{4,5},{5,4},{6,7},{7,6},{8,9},{9,8},{10,11... | collective-permute-start | bytes 6291464 | tf_op jit(solution)/shard_map/ppermute | solution.py:139
  33.2 31.5 %all-to-all-start.1 = ((bf16[16,128,256]{2,1,0:T(8,128)(2,1)}), bf16[16,128,256]{2,1,0:T(8,128)(2,1)S(1)}, u32[]{:S(2)}, u32[]{:S(2)}) async-start(bf16[16,128,256]{2,1,0:T(8,128)(2,1)} %broadcast_in_dim.43), calls=%async_computation.1 | async-start | bytes 2097152 | tf_op jit(solution)/shard_map/all_to_all | solution.py:148
  42.0 13.0 %collective-permute-start.1 = (bf16[128,256]{1,0:T(8,128)(2,1)S(1)}, bf16[128,256]{1,0:T(8,128)(2,1)S(1)}, u32[]{:S(2)}, u32[]{:S(2)}) collective-permute-start(bf16[128,256]{1,0:T(8,128)(2,1)S(1)} %get-tuple-element.34), channel_id=1, source_target_pairs={{0,0},{15,1},{13,256},{11,257},{9,2},{7,3},{5,258},{3,259},{1,4},{... | collective-permute-start | bytes 196616 | tf_op jit(solution)/shard_map/ppermute | solution.py:146
  46.8 18.0 %collective-permute-start.2 = (bf16[128,256]{1,0:T(8,128)(2,1)S(1)}, bf16[128,256]{1,0:T(8,128)(2,1)S(1)}, u32[]{:S(2)}, u32[]{:S(2)}) collective-permute-start(bf16[128,256]{1,0:T(8,128)(2,1)S(1)} %get-tuple-element.34), channel_id=1, source_target_pairs={{0,256},{15,257},{13,0},{11,1},{9,258},{7,259},{5,2},{3,3},{1,260}... | collective-permute-start | bytes 196616 | tf_op jit(solution)/shard_map/ppermute | solution.py:146
  64.8 4.7 %collective-permute-start.3 = (bf16[16,128,256]{2,1,0:T(8,128)(2,1)S(1)}, bf16[16,128,256]{2,1,0:T(8,128)(2,1)S(1)}, u32[]{:S(2)}, u32[]{:S(2)}) collective-permute-start(bf16[16,128,256]{2,1,0:T(8,128)(2,1)S(1)} %all-to-all-done.1.own_ref), channel_id=1, source_target_pairs={{0,1},{1,0},{2,3},{3,2},{4,5},{5,4},{6,7},{7,6},{8,9},{9,8},{10,11... | collective-permute-start | bytes 3145736 | tf_op jit(solution)/shard_map/ppermute | solution.py:150
  69.5 1.6 %copy-start.2 = (bf16[1,4096,256]{2,1,0:T(8,128)(2,1)S(1)}, bf16[1,4096,256]{2,1,0:T(8,128)(2,1)}, u32[]{:S(2)}) copy-start(bf16[1,4096,256]{2,1,0:T(8,128)(2,1)} %param.8) | copy-start | bytes 6291460
  105.9 1.9 %copy-start = (bf16[16,256,512]{2,1,0:T(8,128)(2,1)}, bf16[16,256,512]{2,1,0:T(8,128)(2,1)S(1)}, u32[]{:S(2)}) copy-start(bf16[16,256,512]{2,1,0:T(8,128)(2,1)S(1)} %get-tuple-element.31.weight_ref) | copy-start | bytes 12582916
  108.7 14.5 %all-to-all-start.4 = ((bf16[8,128,256]{2,1,0:T(8,128)(2,1)}), bf16[8,128,256]{2,1,0:T(8,128)(2,1)S(1)}, u32[]{:S(2)}, u32[]{:S(2)}) async-start(bf16[8,128,256]{2,1,0:T(8,128)(2,1)} %broadcast_in_dim.49), calls=%async_computation.4 | async-start | bytes 1048576 | tf_op jit(solution)/shard_map/all_to_all | solution.py:44
  123.2 2.2 %copy-start.1 = (bf16[16,256,512]{2,1,0:T(8,128)(2,1)S(1)}, bf16[16,256,512]{2,1,0:T(8,128)(2,1)}, u32[]{:S(2)}) copy-start(bf16[16,256,512]{2,1,0:T(8,128)(2,1)} %copy-done) | copy-start | bytes 12582916
  126.4 4.3 %collective-permute-start.5 = (bf16[4,64,256]{2,1,0:T(8,128)(2,1)S(1)}, bf16[4,64,256]{2,1,0:T(8,128)(2,1)S(1)}, u32[]{:S(2)}, u32[]{:S(2)}) collective-permute-start(bf16[4,64,256]{2,1,0:T(8,128)(2,1)S(1)} %pad_maximum_fusion.1), channel_id=1, source_target_pairs={{0,1},{1,0},{2,3},{3,2},{4,5},{5,4},{6,7},{7,6},{8,9},{9,8},{10,11... | collective-permute-start | bytes 393224 | tf_op jit(solution)/shard_map/ppermute | solution.py:187

commit v5 on v4

--- a/solution.py
+++ b/solution.py
@@ -37,6 +37,7 @@
 
 VMEM = pl.BlockSpec(memory_space=pltpu.VMEM)
 SMEM = pl.BlockSpec(memory_space=pltpu.SMEM)
+ANY = pl.BlockSpec(memory_space=pl.ANY)
 ROOM = pltpu.CompilerParams(vmem_limit_bytes=16 * 1024 * 1024)
 
 
@@ -44,20 +45,52 @@
     return lax.all_to_all(blocks, "tp", 0, 0, axis_index_groups=GROUPS)
 
 
-def block_kernel(a_new_ref, a_old_ref, b_new_ref, b_old_ref, out_ref):
+def block_kernel(a_new_ref, a_old_ref, b_new_ref, b_old_ref, out_ref, a_ref, b_ref, sems):
+    copies = [
+        pltpu.make_async_copy(source, target, sems.at[i])
+        for i, (source, target) in enumerate(
+            ((a_new_ref, a_ref.at[0]), (a_old_ref, a_ref.at[1]), (b_new_ref, b_ref.at[0]), (b_old_ref, b_ref.at[1]))
+        )
+    ]
+    for copy in copies:
+        copy.start()
+    for copy in copies:
+        copy.wait()
     half, cols = out_ref.shape[0] // 2, out_ref.shape[1]
-    new = a_new_ref[0].astype(jnp.float32)
-    old = a_old_ref[0].astype(jnp.float32)
+    new = a_ref[0, 0].astype(jnp.float32)
+    old = a_ref[1, 0].astype(jnp.float32)
     slices = []
     for i in range(new.shape[1] // cols):
         slices += [new[:, i * cols : (i + 1) * cols], old[:, i * cols : (i + 1) * cols]]
     out_ref[:half, :] = jnp.concatenate(slices, 0).astype(jnp.bfloat16)
-    out_ref[half:, :] = jnp.concatenate([b_new_ref[0], -b_old_ref[0]], 1)
-
-
-def merge_kernel(place_ref, own_ref, other_ref, ups_ref, base_ref, mate_ref, weight_ref, merged_ref, up_ref):
+    out_ref[half:, :] = jnp.concatenate([b_ref[0, 0], -b_ref[1, 0]], 1)
+
+
+def split_kernel(block_ref, down_ref, up_ref):
+    half = up_ref.shape[0]
+    for chip in range(down_ref.shape[0]):
+        down_ref[chip] = block_ref[:half, :]
+    up_ref[...] = block_ref[half:, :]
+
+
+def merge_kernel(
+    place_ref, own_ref, other_ref, ups_ref, base_ref, mate_ref, weight_ref, merged_ref, up_ref, old_ref, new_ref, in_sems, out_sems
+):
     core, low, z = place_ref[0], place_ref[1], place_ref[2]
     cols = base_ref.shape[1]
+    span = 2 * cols
+    loads = []
+    for pair in range(CHIPS):
+        rows = slice(pair * span, (pair + 1) * span)
+        loads.append(
+            [
+                pltpu.make_async_copy(ref.at[rows], old_ref.at[i, rows], in_sems.at[i, pair])
+                for i, ref in enumerate((base_ref, mate_ref))
+            ]
+        )
+        for load in loads[-1]:
+            load.start()
+    stores = []
     for left in range(2):
         for part in range(2):
             up_ref[lax.rem(part + low + core, 2), left] = ups_ref[left, part]
@@ -74,21 +107,28 @@
             ref[:, 16 * pair : 16 * pair + 16, :].astype(jnp.float32).reshape(16, 2, 8, cols)
             for ref in (own_ref, other_ref)
         ]
+        for load in loads[pair]:
+            load.wait()
         for right in range(2):
             down = jnp.concatenate([part[:, right].reshape(128, cols) for part in parts], 0)
             down = down.T.astype(jnp.bfloat16)
             delta = lax.dot_general(down, up, (((1,), (1,)), ((), ())), preferred_element_type=jnp.float32)
             t = 2 * pair + right
             rows = slice(t * cols, (t + 1) * cols)
-            mine = (base_ref[rows, :].astype(jnp.float32) + delta[:, :cols]).astype(jnp.bfloat16)
-            theirs = (mate_ref[rows, :].astype(jnp.float32) + delta[:, cols:]).astype(jnp.bfloat16)
-            merged_ref[rows, :] = mine
+            mine = (old_ref[0, rows, :].astype(jnp.float32) + delta[:, :cols]).astype(jnp.bfloat16)
+            theirs = (old_ref[1, rows, :].astype(jnp.float32) + delta[:, cols:]).astype(jnp.bfloat16)
+            new_ref[rows, :] = mine
             which = 2 * pair + lax.rem(right + core, 2)
             weight_ref[which, :, :cols] = mine
             weight_ref[which, :, cols:] = theirs
-
-
-def step_kernel(x_ref, weight_ref, gain_ref, mine_ref, out_ref, _):
+        rows = slice(pair * span, (pair + 1) * span)
+        stores.append(pltpu.make_async_copy(new_ref.at[rows], merged_ref.at[rows], out_sems.at[pair]))
+        stores[-1].start()
+    for store in stores:
+        store.wait()
+
+
+def step_kernel(x_ref, weight_ref, gain_ref, mine_ref, out_ref, give_ref, _):
     _, rows, cols = mine_ref.shape
     blocks = weight_ref.shape[0]
     part = lambda i: x_ref[i // 2, (i % 2) * rows : (i % 2 + 1) * rows, :].astype(jnp.float32)
@@ -104,6 +144,7 @@
     for half in range(2):
         branch = total[:, half * cols : (half + 1) * cols]
         out_ref[half] = (mine_ref[half].astype(jnp.float32) + branch).astype(jnp.bfloat16)
+    give_ref[...] = out_ref[1]
 
 
 def finish_kernel(core_ref, swapped_ref, *refs):
@@ -127,11 +168,16 @@
     block = pl.pallas_call(
         block_kernel,
         out_shape=jax.ShapeDtypeStruct((2 * b_old.shape[1], cols), jnp.bfloat16),
-        in_specs=[VMEM] * 4,
+        in_specs=[ANY] * 4,
         out_specs=VMEM,
+        scratch_shapes=[
+            pltpu.VMEM((2,) + a_new.shape, jnp.bfloat16),
+            pltpu.VMEM((2,) + b_new.shape, jnp.bfloat16),
+            pltpu.SemaphoreType.DMA((4,)),
+        ],
         name="block",
-        compiler_params=ROOM,
     )(a_new, a_old, b_new, b_old)
+    block, tokens = lax.optimization_barrier((block, tokens))
     block = lax.ppermute(block, ("fsdp", "tp"), SHIFTED)
 
     both = lax.all_gather(tokens, "tp", axis=0, axis_index_groups=PAIRS)
@@ -140,12 +186,23 @@
     both = lax.dynamic_slice_in_dim(both, core * half, half, 1)
     stream = jnp.where(core == 0, both, both[::-1])
     x = spread(jnp.broadcast_to(stream.reshape(1, rows, cols), (CHIPS, rows, cols)))
-    block, x = lax.optimization_barrier((block, x))
-
-    down, up = block[: block.shape[0] // 2], block[block.shape[0] // 2 :]
+
+    size = block.shape[0] // 2
+    down, up = pl.pallas_call(
+        split_kernel,
+        out_shape=(
+            jax.ShapeDtypeStruct((len(PLANES[0]), size, cols), jnp.bfloat16),
+            jax.ShapeDtypeStruct((size, cols), jnp.bfloat16),
+        ),
+        in_specs=[VMEM],
+        out_specs=(VMEM, VMEM),
+        cost_estimate=pl.CostEstimate(flops=3 * 10**10, bytes_accessed=2**20, transcendentals=0),
+        name="split",
+        compiler_params=ROOM,
+    )(block)
+    down, up, x = lax.optimization_barrier((down, up, x))
     ups = [lax.ppermute(up, ("fsdp", "tp"), relay(part)) for part in range(2)]
-    own = jnp.broadcast_to(down[None], (len(PLANES[0]),) + down.shape)
-    own = lax.all_to_all(own, ("fsdp", "tp"), 0, 0, axis_index_groups=PLANES)
+    own = lax.all_to_all(down, ("fsdp", "tp"), 0, 0, axis_index_groups=PLANES)
     own, *ups = lax.optimization_barrier((own, *ups))
     other = lax.ppermute(own, "tp", SWAP)
     ups = lax.all_gather(jnp.stack(ups), "tp", axis=0, axis_index_groups=PAIRS)
@@ -157,34 +214,42 @@
             jax.ShapeDtypeStruct((tp, cols, 2 * cols), jnp.bfloat16),
             jax.ShapeDtypeStruct((tp * cols, cols), jnp.bfloat16),
         ),
-        in_specs=[SMEM] + [VMEM] * 5,
-        out_specs=(VMEM, VMEM),
-        scratch_shapes=[pltpu.VMEM((2, 2, cols // 2, cols), jnp.bfloat16)],
+        in_specs=[SMEM] + [VMEM] * 3 + [ANY] * 2,
+        out_specs=(VMEM, ANY),
+        scratch_shapes=[
+            pltpu.VMEM((2, 2, cols // 2, cols), jnp.bfloat16),
+            pltpu.VMEM((2, tp * cols, cols), jnp.bfloat16),
+            pltpu.VMEM((tp * cols, cols), jnp.bfloat16),
+            pltpu.SemaphoreType.DMA((2, CHIPS)),
+            pltpu.SemaphoreType.DMA((CHIPS,)),
+        ],
         name="merge",
         compiler_params=ROOM,
     )(place, own, other, ups, base_weight[0], mate)
 
     gain = gains[0].reshape(CHIPS, 2, 1, cols)
     gain = jnp.where(core == 0, gain, gain[:, ::-1]).reshape(tp, 1, cols)
-    results = []
+    results, gives = [], []
     for step in range(STEPS):
         if step:
             x = spread(jnp.broadcast_to(stream.reshape(1, rows, cols), (CHIPS, rows, cols)))
-        stream, weights = pl.pallas_call(
+        stream, give, weights = pl.pallas_call(
             step_kernel,
             out_shape=(
                 jax.ShapeDtypeStruct((2, half, cols), jnp.bfloat16),
+                jax.ShapeDtypeStruct((half, cols), jnp.bfloat16),
                 jax.ShapeDtypeStruct(weights.shape, weights.dtype),
             ),
             in_specs=[VMEM] * 4,
-            out_specs=(VMEM, VMEM),
-            input_output_aliases={1: 1},
+            out_specs=(VMEM, VMEM, VMEM),
+            input_output_aliases={1: 2},
             name="step",
             compiler_params=ROOM,
         )(x, weights, gain, stream)
         results.append(stream)
-
-    swapped = lax.ppermute(jnp.stack([result[1] for result in results]), "tp", SWAP)
+        gives.append(give)
+
+    swapped = lax.ppermute(jnp.stack(gives), "tp", SWAP)
     ends = pl.pallas_call(
         finish_kernel,
         out_shape=jax.ShapeDtypeStruct((STEPS, rows, cols), jnp.bfloat16),

time: 132 us -> 124 us (0.939)
  the two profiles are of different devices: /device:TPU:33 before, /device:TPU:1 now
where the time goes in v5:
time: 124 us; the launch traced here: 123 us
  blocking collectives  44.8 us (36%)
  starting transfers between devices  41.6 us (34%)
  waiting for transfers between devices  20.5 us (17%)
  Pallas kernels  12.5 us (10%)
  local copies, waits for them, and re-layouts  2.56 us (2%)
    all_to_all x3, blocking collectives, spread(): return lax.all_to_all(blocks, 'tp', 0, 0, axis_index_groups=GROUPS)  40.1 us
    ppermute x1, starting transfers between devices, shards(): block = lax.ppermute(block, ('fsdp', 'tp'), SHIFTED)  16.3 us
    ppermute x2, waiting for transfers between devices, shards(): ups = [lax.ppermute(up, ('fsdp', 'tp'), relay(part)) for part in range(2)]  11.4 us
    ppermute x2, starting transfers between devices, shards(): ups = [lax.ppermute(up, ('fsdp', 'tp'), relay(part)) for part in range(2)]  8.7 us
    all_to_all x1, waiting for transfers between devices, spread(): return lax.all_to_all(blocks, 'tp', 0, 0, axis_index_groups=GROUPS)  8.13 us
    pallas_call x1, Pallas kernels, shards(): pl.pallas_call(merge_kernel, out_shape=(jax.ShapeDtypeStruct((tp, cols, 2...  5.3 us
    all_to_all x1, starting transfers between devices, spread(): return lax.all_to_all(blocks, 'tp', 0, 0, axis_index_groups=GROUPS)  4.42 us
    ppermute x1, starting transfers between devices, shards(): swapped = lax.ppermute(jnp.stack(gives), 'tp', SWAP)  4.12 us
  transfers between devices with their start and end apart: 8, of which 4 were waited for; matrix products, arithmetic and copies ran while one was open for 1% of the time, Pallas kernels for 1%

profile of v5, /device:TPU:1, one launch (start us, length us, event | category | flops | bytes accessed | tf_op | source)
XLA Modules:
  0.0 123.0 jit_solution(1265372122520508416)
XLA Ops:
  0.6 1.5 %block.1 = bf16[256,256]{1,0:T(8,128)(2,1)} custom-call(bf16[1,4,4096]{2,1,0:T(4,128)(2,1)} %a_new_ref.1, bf16[1,4,4096]{2,1,0:T(4,128)(2,1)} %a_old_ref.1, bf16[1,128,128]{2,1,0:T(8,128)(2,1)} %b_new_ref.1, bf16[1,128,128]{2,1,0:T(8,128)(2,1)} %b_old_ref.1), custom_call_target="tpu_custom_call" | custom-call | tf_op jit(solution)/shard_map/block/pallas_call | solution.py:168
  2.2 16.3 %collective-permute-start = (bf16[256,256]{1,0:T(8,128)(2,1)}, bf16[256,256]{1,0:T(8,128)(2,1)S(1)}, u32[]{:S(2)}, u32[]{:S(2)}) collective-permute-start(bf16[256,256]{1,0:T(8,128)(2,1)} %block.1), channel_id=1, source_target_pairs={{0,0},{1,129},{2,18},{3,147},{4,36},{5,165},{6,54},{7,183},{8,72},... | collective-permute-start | bytes 393224 | tf_op jit(solution)/shard_map/ppermute | solution.py:181
  18.4 2.1 %all-gather = bf16[256,256]{1,0:T(8,128)(2,1)S(1)} all-gather(bf16[128,256]{1,0:T(8,128)(2,1)} %param.7), channel_id=2, replica_groups={{0,1},{2,3},{4,5},{6,7},{8,9},{10,11},{12,13},{14,15},{16,17},{18,19},{..., dimensions={0}, use_global_device_ids=true | all-gather | bytes 196608 | tf_op jit(solution)/shard_map/all_gather | solution.py:183
  20.6 0.8 broadcast_in_dim.36
  21.4 4.4 %all-to-all-start = ((bf16[8,128,256]{2,1,0:T(8,128)(2,1)}), bf16[8,128,256]{2,1,0:T(8,128)(2,1)S(1)}, u32[]{:S(2)}, u32[]{:S(2)}) async-start(bf16[8,128,256]{2,1,0:T(8,128)(2,1)} %broadcast_in_dim.36), calls=%async_computation | async-start | bytes 1048576 | tf_op jit(solution)/shard_map/all_to_all | solution.py:45
  25.9 2.5 %collective-permute-start.4 = (bf16[4096,256]{1,0:T(8,128)(2,1)}, bf16[4096,256]{1,0:T(8,128)(2,1)}, u32[]{:S(2)}, u32[]{:S(2)}) collective-permute-start(bf16[4096,256]{1,0:T(8,128)(2,1)} %bitcast.19), channel_id=1, source_target_pairs={{0,1},{1,0},{2,3},{3,2},{4,5},{5,4},{6,7},{7,6},{8,9},{9,8},{10,11... | collective-permute-start | bytes 6291464 | tf_op jit(solution)/shard_map/ppermute | solution.py:185
  28.4 0.0 collective-permute-done.block_ref
  28.4 1.0 split.1
  29.5 8.1 %all-to-all-done.x_ref = bf16[8,128,256]{2,1,0:T(8,128)(2,1)S(1)} async-done(((bf16[8,128,256]{2,1,0:T(8,128)(2,1)}), bf16[8,128,256]{2,1,0:T(8,128)(2,1)S(1)}, u32[]{:S(2)}, u32[]{:S(2)}) %all-to-all-start) | async-done | bytes 524320 | tf_op jit(solution)/shard_map/all_to_all | solution.py:45
  37.6 3.7 %all-to-all-start.1 = ((bf16[16,128,256]{2,1,0:T(8,128)(2,1)}), bf16[16,128,256]{2,1,0:T(8,128)(2,1)S(1)}, u32[]{:S(2)}, u32[]{:S(2)}) async-start(bf16[16,128,256]{2,1,0:T(8,128)(2,1)} %get-tuple-element.33), calls=%async_computation.1 | async-start | bytes 2097152 | tf_op jit(solution)/shard_map/all_to_all | solution.py:205
  41.3 6.5 %collective-permute-start.2 = (bf16[128,256]{1,0:T(8,128)(2,1)S(1)}, bf16[128,256]{1,0:T(8,128)(2,1)S(1)}, u32[]{:S(2)}, u32[]{:S(2)}) collective-permute-start(bf16[128,256]{1,0:T(8,128)(2,1)S(1)} %get-tuple-element.34), channel_id=1, source_target_pairs={{0,256},{15,257},{13,0},{11,1},{9,258},{7,259},{5,2},{3,3},{1,260}... | collective-permute-start | bytes 196616 | tf_op jit(solution)/shard_map/ppermute | solution.py:204
  47.8 2.2 %collective-permute-start.1 = (bf16[128,256]{1,0:T(8,128)(2,1)S(1)}, bf16[128,256]{1,0:T(8,128)(2,1)S(1)}, u32[]{:S(2)}, u32[]{:S(2)}) collective-permute-start(bf16[128,256]{1,0:T(8,128)(2,1)S(1)} %get-tuple-element.34), channel_id=1, source_target_pairs={{0,0},{15,1},{13,256},{11,257},{9,2},{7,3},{5,258},{3,259},{1,4},{... | collective-permute-start | bytes 196616 | tf_op jit(solution)/shard_map/ppermute | solution.py:204
  50.0 7.6 %collective-permute-done.2 = bf16[128,256]{1,0:T(8,128)(2,1)S(1)} collective-permute-done((bf16[128,256]{1,0:T(8,128)(2,1)S(1)}, bf16[128,256]{1,0:T(8,128)(2,1)S(1)}, u32[]{:S(2)}, u32[]{:S(2)}) %collective-permute-start.2) | collective-permute-done | bytes 65568 | tf_op jit(solution)/shard_map/ppermute | solution.py:204
  57.6 3.8 %collective-permute-done.1 = bf16[128,256]{1,0:T(8,128)(2,1)S(1)} collective-permute-done((bf16[128,256]{1,0:T(8,128)(2,1)S(1)}, bf16[128,256]{1,0:T(8,128)(2,1)S(1)}, u32[]{:S(2)}, u32[]{:S(2)}) %collective-permute-start.1) | collective-permute-done | bytes 65568 | tf_op jit(solution)/shard_map/ppermute | solution.py:204
  61.4 0.0 all-to-all-done.1.own_ref
  61.4 1.9 %collective-permute-start.3 = (bf16[16,128,256]{2,1,0:T(8,128)(2,1)S(1)}, bf16[16,128,256]{2,1,0:T(8,128)(2,1)S(1)}, u32[]{:S(2)}, u32[]{:S(2)}) collective-permute-start(bf16[16,128,256]{2,1,0:T(8,128)(2,1)S(1)} %all-to-all-done.1.own_ref), channel_id=1, source_target_pairs={{0,1},{1,0},{2,3},{3,2},{4,5},{5,4},{6,7},{7,6},{8,9},{9,8},{10,11... | collective-permute-start | bytes 3145736 | tf_op jit(solution)/shard_map/ppermute | solution.py:207
  63.3 0.1 pad_add_fusion.place_ref
  63.5 2.7 %all-gather.1 = bf16[4,128,256]{2,1,0:T(8,128)(2,1)S(1)} all-gather(bf16[2,128,256]{2,1,0:T(8,128)(2,1)S(1)} %pad_maximum_fusion), channel_id=3, replica_groups={{0,1},{2,3},{4,5},{6,7},{8,9},{10,11},{12,13},{14,15},{16,17},{18,19},{..., dimensions={0}, use_global_device_ids=true | all-gather | bytes 393216 | tf_op jit(solution)/shard_map/all_gather | solution.py:208
  66.1 0.0 collective-permute-done.4.mate_ref
  66.1 0.0 collective-permute-done.3.other_ref
  66.1 1.6 %copy-done = bf16[1,4096,256]{2,1,0:T(8,128)(2,1)S(1)} copy-done((bf16[1,4096,256]{2,1,0:T(8,128)(2,1)S(1)}, bf16[1,4096,256]{2,1,0:T(8,128)(2,1)}, u32[]{:S(2)}) %copy-start) | copy-done | bytes 2097176
  67.7 5.3 %merge.1 = (bf16[16,256,512]{2,1,0:T(8,128)(2,1)S(1)}, bf16[4096,256]{1,0:T(8,128)(2,1)}) custom-call(s32[3]{0:T(128)S(1)} %pad_add_fusion.place_ref, bf16[16,128,256]{2,1,0:T(8,128)(2,1)S(1)} %all-to-all-done.1.own_ref, bf16[16,128,256]{2,1,0:T(8,128)(2,1)S(1)} %collective-permute-done.3.other_ref, bf16[2,2,128,256]{3,2,1,0:T(8,128)(2,1)S(1)} %bitcast.21, ...), custom_call_target="tpu_custom_call" | custom-call | tf_op jit(solution)/shard_map/merge/pallas_call | solution.py:211
  73.0 1.0 step.4
  74.1 14.2 %all_to_all.25.x_ref = bf16[8,128,256]{2,1,0:T(8,128)(2,1)S(1)} all-to-all(bf16[8,128,256]{2,1,0:T(8,128)(2,1)S(1)} %broadcast_in_dim.38), channel_id=1, replica_groups={{0,2,4,6,8,10,12,14},{1,3,5,7,9,11,13,15},{16,18,20,22,24,26,28,30},{17..., dimensions={0} | all-to-all | bytes 1048576 | tf_op jit(solution)/shard_map/all_to_all | solution.py:45
  88.3 1.0 step.5
  89.3 13.1 %all_to_all.26.x_ref = bf16[8,128,256]{2,1,0:T(8,128)(2,1)S(1)} all-to-all(bf16[8,128,256]{2,1,0:T(8,128)(2,1)S(1)} %broadcast_in_dim.40), channel_id=1, replica_groups={{0,2,4,6,8,10,12,14},{1,3,5,7,9,11,13,15},{16,18,20,22,24,26,28,30},{17..., dimensions={0} | all-to-all | bytes 1048576 | tf_op jit(solution)/shard_map/all_to_all | solution.py:45
  102.4 1.0 step.6
  103.4 12.7 %all_to_all.27.x_ref = bf16[8,128,256]{2,1,0:T(8,128)(2,1)S(1)} all-to-all(bf16[8,128,256]{2,1,0:T(8,128)(2,1)S(1)} %broadcast_in_dim.42), channel_id=1, replica_groups={{0,2,4,6,8,10,12,14},{1,3,5,7,9,11,13,15},{16,18,20,22,24,26,28,30},{17..., dimensions={0} | all-to-all | bytes 1048576 | tf_op jit(solution)/shard_map/all_to_all | solution.py:45
  116.2 1.0 step.7
  117.2 4.1 %collective-permute-start.5 = (bf16[4,64,256]{2,1,0:T(8,128)(2,1)S(1)}, bf16[4,64,256]{2,1,0:T(8,128)(2,1)S(1)}, u32[]{:S(2)}, u32[]{:S(2)}) collective-permute-start(bf16[4,64,256]{2,1,0:T(8,128)(2,1)S(1)} %pad_maximum_fusion.1), channel_id=1, source_target_pairs={{0,1},{1,0},{2,3},{3,2},{4,5},{5,4},{6,7},{7,6},{8,9},{9,8},{10,11... | collective-permute-start | bytes 393224 | tf_op jit(solution)/shard_map/ppermute | solution.py:252
  121.3 1.0 collective-permute-done.5.swapped_ref
  122.3 0.7 finish.1
  (11 shorter events, 0.2 us)
Async XLA Ops:
  2.2 26.3 %collective-permute-start = (bf16[256,256]{1,0:T(8,128)(2,1)}, bf16[256,256]{1,0:T(8,128)(2,1)S(1)}, u32[]{:S(2)}, u32[]{:S(2)}) collective-permute-start(bf16[256,256]{1,0:T(8,128)(2,1)} %block.1), channel_id=1, source_target_pairs={{0,0},{1,129},{2,18},{3,147},{4,36},{5,165},{6,54},{7,183},{8,72},... | collective-permute-start | bytes 393224 | tf_op jit(solution)/shard_map/ppermute | solution.py:181
  21.4 16.2 %all-to-all-start = ((bf16[8,128,256]{2,1,0:T(8,128)(2,1)}), bf16[8,128,256]{2,1,0:T(8,128)(2,1)S(1)}, u32[]{:S(2)}, u32[]{:S(2)}) async-start(bf16[8,128,256]{2,1,0:T(8,128)(2,1)} %broadcast_in_dim.36), calls=%async_computation | async-start | bytes 1048576 | tf_op jit(solution)/shard_map/all_to_all | solution.py:45
  25.9 37.6 %copy-start.1 = (f32[1,4096]{1,0:T(1,128)S(1)}, f32[1,4096]{1,0:T(1,128)}, u32[]{:S(2)}) copy-start(f32[1,4096]{1,0:T(1,128)} %param.13) | copy-start | bytes 49156
  25.9 40.3 %collective-permute-start.4 = (bf16[4096,256]{1,0:T(8,128)(2,1)}, bf16[4096,256]{1,0:T(8,128)(2,1)}, u32[]{:S(2)}, u32[]{:S(2)}) collective-permute-start(bf16[4096,256]{1,0:T(8,128)(2,1)} %bitcast.19), channel_id=1, source_target_pairs={{0,1},{1,0},{2,3},{3,2},{4,5},{5,4},{6,7},{7,6},{8,9},{9,8},{10,11... | collective-permute-start | bytes 6291464 | tf_op jit(solution)/shard_map/ppermute | solution.py:185
  37.6 23.8 %all-to-all-start.1 = ((bf16[16,128,256]{2,1,0:T(8,128)(2,1)}), bf16[16,128,256]{2,1,0:T(8,128)(2,1)S(1)}, u32[]{:S(2)}, u32[]{:S(2)}) async-start(bf16[16,128,256]{2,1,0:T(8,128)(2,1)} %get-tuple-element.33), calls=%async_computation.1 | async-start | bytes 2097152 | tf_op jit(solution)/shard_map/all_to_all | solution.py:205
  41.3 16.3 %collective-permute-start.2 = (bf16[128,256]{1,0:T(8,128)(2,1)S(1)}, bf16[128,256]{1,0:T(8,128)(2,1)S(1)}, u32[]{:S(2)}, u32[]{:S(2)}) collective-permute-start(bf16[128,256]{1,0:T(8,128)(2,1)S(1)} %get-tuple-element.34), channel_id=1, source_target_pairs={{0,256},{15,257},{13,0},{11,1},{9,258},{7,259},{5,2},{3,3},{1,260}... | collective-permute-start | bytes 196616 | tf_op jit(solution)/shard_map/ppermute | solution.py:204
  47.8 13.6 %collective-permute-start.1 = (bf16[128,256]{1,0:T(8,128)(2,1)S(1)}, bf16[128,256]{1,0:T(8,128)(2,1)S(1)}, u32[]{:S(2)}, u32[]{:S(2)}) collective-permute-start(bf16[128,256]{1,0:T(8,128)(2,1)S(1)} %get-tuple-element.34), channel_id=1, source_target_pairs={{0,0},{15,1},{13,256},{11,257},{9,2},{7,3},{5,258},{3,259},{1,4},{... | collective-permute-start | bytes 196616 | tf_op jit(solution)/shard_map/ppermute | solution.py:204
  61.4 4.7 %collective-permute-start.3 = (bf16[16,128,256]{2,1,0:T(8,128)(2,1)S(1)}, bf16[16,128,256]{2,1,0:T(8,128)(2,1)S(1)}, u32[]{:S(2)}, u32[]{:S(2)}) collective-permute-start(bf16[16,128,256]{2,1,0:T(8,128)(2,1)S(1)} %all-to-all-done.1.own_ref), channel_id=1, source_target_pairs={{0,1},{1,0},{2,3},{3,2},{4,5},{5,4},{6,7},{7,6},{8,9},{9,8},{10,11... | collective-permute-start | bytes 3145736 | tf_op jit(solution)/shard_map/ppermute | solution.py:207
  66.1 1.6 %copy-start = (bf16[1,4096,256]{2,1,0:T(8,128)(2,1)S(1)}, bf16[1,4096,256]{2,1,0:T(8,128)(2,1)}, u32[]{:S(2)}) copy-start(bf16[1,4096,256]{2,1,0:T(8,128)(2,1)} %param.8) | copy-start | bytes 6291460
  117.2 5.1 %collective-permute-start.5 = (bf16[4,64,256]{2,1,0:T(8,128)(2,1)S(1)}, bf16[4,64,256]{2,1,0:T(8,128)(2,1)S(1)}, u32[]{:S(2)}, u32[]{:S(2)}) collective-permute-start(bf16[4,64,256]{2,1,0:T(8,128)(2,1)S(1)} %pad_maximum_fusion.1), channel_id=1, source_target_pairs={{0,1},{1,0},{2,3},{3,2},{4,5},{5,4},{6,7},{7,6},{8,9},{9,8},{10,11... | collective-permute-start | bytes 393224 | tf_op jit(solution)/shard_map/ppermute | solution.py:252

commit v6 on v5

--- a/solution.py
+++ b/solution.py
@@ -37,7 +37,8 @@
 
 VMEM = pl.BlockSpec(memory_space=pltpu.VMEM)
 SMEM = pl.BlockSpec(memory_space=pltpu.SMEM)
-ANY = pl.BlockSpec(memory_space=pl.ANY)
+HBM = pl.BlockSpec(memory_space=pltpu.HBM)
+WIDE = pltpu.CompilerParams(vmem_limit_bytes=32 * 1024 * 1024)
 ROOM = pltpu.CompilerParams(vmem_limit_bytes=16 * 1024 * 1024)
 
 
@@ -74,7 +75,7 @@
 
 
 def merge_kernel(
-    place_ref, own_ref, other_ref, ups_ref, base_ref, mate_ref, weight_ref, merged_ref, up_ref, old_ref, new_ref, in_sems, out_sems
+    place_ref, own_ref, other_ref, ups_ref, base_ref, mate_ref, weight_ref, merged_ref, up_ref, old_ref, new_ref, out_ref, in_sems, out_sems
 ):
     core, low, z = place_ref[0], place_ref[1], place_ref[2]
     cols = base_ref.shape[1]
@@ -119,16 +120,18 @@
             theirs = (old_ref[1, rows, :].astype(jnp.float32) + delta[:, cols:]).astype(jnp.bfloat16)
             new_ref[rows, :] = mine
             which = 2 * pair + lax.rem(right + core, 2)
-            weight_ref[which, :, :cols] = mine
-            weight_ref[which, :, cols:] = theirs
-        rows = slice(pair * span, (pair + 1) * span)
-        stores.append(pltpu.make_async_copy(new_ref.at[rows], merged_ref.at[rows], out_sems.at[pair]))
-        stores[-1].start()
+            out_ref[which, :, :cols] = mine
+            out_ref[which, :, cols:] = theirs
+        rows, both = slice(pair * span, (pair + 1) * span), slice(2 * pair, 2 * pair + 2)
+        stores.append(pltpu.make_async_copy(new_ref.at[rows], merged_ref.at[rows], out_sems.at[0, pair]))
+        stores.append(pltpu.make_async_copy(out_ref.at[both], weight_ref.at[both], out_sems.at[1, pair]))
+        for store in stores[-2:]:
+            store.start()
     for store in stores:
         store.wait()
 
 
-def step_kernel(x_ref, weight_ref, gain_ref, mine_ref, out_ref, give_ref, _):
+def decode(x_ref, weight_ref, gain_ref, mine_ref, out_ref, give_ref, arrive):
     _, rows, cols = mine_ref.shape
     blocks = weight_ref.shape[0]
     part = lambda i: x_ref[i // 2, (i % 2) * rows : (i % 2 + 1) * rows, :].astype(jnp.float32)
@@ -140,11 +143,31 @@
     total = jnp.zeros((rows, 2 * cols), jnp.float32)
     for i in range(blocks):
         normed = (part(i) * scale * gain_ref[i]).astype(jnp.bfloat16)
+        arrive(i)
         total += jnp.dot(normed, weight_ref[i], preferred_element_type=jnp.float32)
     for half in range(2):
         branch = total[:, half * cols : (half + 1) * cols]
         out_ref[half] = (mine_ref[half].astype(jnp.float32) + branch).astype(jnp.bfloat16)
     give_ref[...] = out_ref[1]
+
+
+def first_kernel(x_ref, stored_ref, gain_ref, mine_ref, out_ref, give_ref, weight_ref, sems):
+    loads = [
+        pltpu.make_async_copy(stored_ref.at[2 * i : 2 * i + 2], weight_ref.at[2 * i : 2 * i + 2], sems.at[i])
+        for i in range(CHIPS)
+    ]
+    for load in loads:
+        load.start()
+
+    def arrive(i):
+        if i % 2 == 0:
+            loads[i // 2].wait()
+
+    decode(x_ref, weight_ref, gain_ref, mine_ref, out_ref, give_ref, arrive)
+
+
+def step_kernel(x_ref, weight_ref, gain_ref, mine_ref, out_ref, give_ref, _):
+    decode(x_ref, weight_ref, gain_ref, mine_ref, out_ref, give_ref, lambda i: None)
 
 
 def finish_kernel(core_ref, swapped_ref, *refs):
@@ -168,7 +191,7 @@
     block = pl.pallas_call(
         block_kernel,
         out_shape=jax.ShapeDtypeStruct((2 * b_old.shape[1], cols), jnp.bfloat16),
-        in_specs=[ANY] * 4,
+        in_specs=[HBM] * 4,
         out_specs=VMEM,
         scratch_shapes=[
             pltpu.VMEM((2,) + a_new.shape, jnp.bfloat16),
@@ -185,7 +208,6 @@
     mate = lax.ppermute(base, "tp", SWAP)
     both = lax.dynamic_slice_in_dim(both, core * half, half, 1)
     stream = jnp.where(core == 0, both, both[::-1])
-    x = spread(jnp.broadcast_to(stream.reshape(1, rows, cols), (CHIPS, rows, cols)))
 
     size = block.shape[0] // 2
     down, up = pl.pallas_call(
@@ -196,14 +218,14 @@
         ),
         in_specs=[VMEM],
         out_specs=(VMEM, VMEM),
-        cost_estimate=pl.CostEstimate(flops=3 * 10**10, bytes_accessed=2**20, transcendentals=0),
         name="split",
         compiler_params=ROOM,
     )(block)
-    down, up, x = lax.optimization_barrier((down, up, x))
+    down, up, stream = lax.optimization_barrier((down, up, stream))
     ups = [lax.ppermute(up, ("fsdp", "tp"), relay(part)) for part in range(2)]
     own = lax.all_to_all(down, ("fsdp", "tp"), 0, 0, axis_index_groups=PLANES)
-    own, *ups = lax.optimization_barrier((own, *ups))
+    own, stream, *ups = lax.optimization_barrier((own, stream, *ups))
+    x = spread(jnp.broadcast_to(stream.reshape(1, rows, cols), (CHIPS, rows, cols)))
     other = lax.ppermute(own, "tp", SWAP)
     ups = lax.all_gather(jnp.stack(ups), "tp", axis=0, axis_index_groups=PAIRS)
     f = lax.axis_index("fsdp")
@@ -214,17 +236,18 @@
             jax.ShapeDtypeStruct((tp, cols, 2 * cols), jnp.bfloat16),
             jax.ShapeDtypeStruct((tp * cols, cols), jnp.bfloat16),
         ),
-        in_specs=[SMEM] + [VMEM] * 3 + [ANY] * 2,
-        out_specs=(VMEM, ANY),
+        in_specs=[SMEM] + [VMEM] * 3 + [HBM] * 2,
+        out_specs=(HBM, HBM),
         scratch_shapes=[
             pltpu.VMEM((2, 2, cols // 2, cols), jnp.bfloat16),
             pltpu.VMEM((2, tp * cols, cols), jnp.bfloat16),
             pltpu.VMEM((tp * cols, cols), jnp.bfloat16),
+            pltpu.VMEM((tp, cols, 2 * cols), jnp.bfloat16),
             pltpu.SemaphoreType.DMA((2, CHIPS)),
-            pltpu.SemaphoreType.DMA((CHIPS,)),
+            pltpu.SemaphoreType.DMA((2, CHIPS)),
         ],
         name="merge",
-        compiler_params=ROOM,
+        compiler_params=WIDE,
     )(place, own, other, ups, base_weight[0], mate)
 
     gain = gains[0].reshape(CHIPS, 2, 1, cols)
@@ -234,17 +257,18 @@
         if step:
             x = spread(jnp.broadcast_to(stream.reshape(1, rows, cols), (CHIPS, rows, cols)))
         stream, give, weights = pl.pallas_call(
-            step_kernel,
+            step_kernel if step else first_kernel,
             out_shape=(
                 jax.ShapeDtypeStruct((2, half, cols), jnp.bfloat16),
                 jax.ShapeDtypeStruct((half, cols), jnp.bfloat16),
                 jax.ShapeDtypeStruct(weights.shape, weights.dtype),
             ),
-            in_specs=[VMEM] * 4,
+            in_specs=[VMEM, VMEM if step else HBM, VMEM, VMEM],
             out_specs=(VMEM, VMEM, VMEM),
-            input_output_aliases={1: 2},
-            name="step",
-            compiler_params=ROOM,
+            scratch_shapes=[] if step else [pltpu.SemaphoreType.DMA((CHIPS,))],
+            input_output_aliases={1: 2} if step else {},
+            name="step" if step else "first",
+            compiler_params=ROOM if step else pltpu.CompilerParams(vmem_limit_bytes=46 * 1024 * 1024),
         )(x, weights, gain, stream)
         results.append(stream)
         gives.append(give)

time: 124 us -> 124 us (level)
  waiting for transfers between devices: 20.5 us -> 13.7 us
  local copies, waits for them, and re-layouts: 2.56 us -> 4.51 us
  Pallas kernels: 12.5 us -> 14.4 us
  starting transfers between devices: 41.6 us -> 43.5 us
  blocking collectives: 44.8 us -> 46.4 us
    all_to_all x1, waiting for transfers between devices: 8.13 us -> 0.13 us  [spread(): return lax.all_to_all(blocks, 'tp', 0, 0, axis_index_groups=GROUPS)]
    all_to_all x1, starting transfers between devices: 3.66 us -> 9.58 us  [shards(): own = lax.all_to_all(down, ('fsdp', 'tp'), 0, 0, axis_index_groups=PLANES)]
    ppermute x2, starting transfers between devices: 8.7 us -> 5 us  [shards(): ups = [lax.ppermute(up, ('fsdp', 'tp'), relay(part)) for part in range(2)]]
    all_to_all x3, blocking collectives: 40.1 us -> 42.2 us  [spread(): return lax.all_to_all(blocks, 'tp', 0, 0, axis_index_groups=GROUPS)]
    unnamed x4 -> x6, local copies, waits for them, and re-layouts: 1.59 us -> 3.55 us
    pallas_call x4, Pallas kernels: 3.91 us -> 5.37 us  [shards(): pl.pallas_call(step_kernel if step else first_kernel, out_shape=(jax.Shap...]
  transfers between devices with their start and end apart: 8 -> 8, of which waited for: 4 -> 4; matrix products, arithmetic and copies ran while one was open for 1% -> 1% of each run, Pallas kernels for 1% -> 5%
where the time goes in v6:
time: 124 us
  blocking collectives  46.4 us (37%)
  starting transfers between devices  43.5 us (35%)
  Pallas kernels  14.4 us (12%)
  waiting for transfers between devices  13.7 us (11%)
  local copies, waits for them, and re-layouts  4.51 us (4%)
    all_to_all x3, blocking collectives, spread(): return lax.all_to_all(blocks, 'tp', 0, 0, axis_index_groups=GROUPS)  42.2 us
    ppermute x1, starting transfers between devices, shards(): block = lax.ppermute(block, ('fsdp', 'tp'), SHIFTED)  16.3 us
    ppermute x2, waiting for transfers between devices, shards(): ups = [lax.ppermute(up, ('fsdp', 'tp'), relay(part)) for part in range(2)]  12.6 us
    all_to_all x1, starting transfers between devices, shards(): own = lax.all_to_all(down, ('fsdp', 'tp'), 0, 0, axis_index_groups=PLANES)  9.58 us
    pallas_call x1, Pallas kernels, shards(): pl.pallas_call(merge_kernel, out_shape=(jax.ShapeDtypeStruct((tp, cols, 2...  5.74 us
    pallas_call x4, Pallas kernels, shards(): pl.pallas_call(step_kernel if step else first_kernel, out_shape=(jax.Shap...  5.37 us
    ppermute x1, starting transfers between devices, shards(): swapped = lax.ppermute(jnp.stack(gives), 'tp', SWAP)  5.21 us
    ppermute x2, starting transfers between devices, shards(): ups = [lax.ppermute(up, ('fsdp', 'tp'), relay(part)) for part in range(2)]  5 us
  transfers between devices with their start and end apart: 8, of which 4 were waited for; matrix products, arithmetic and copies ran while one was open for 1% of the time, Pallas kernels for 5%

profile of v6, /device:TPU:1, one launch (start us, length us, event | category | flops | bytes accessed | tf_op | source)
XLA Modules:
  0.0 123.6 jit_solution(3529007687667146311)
XLA Ops:
  0.6 1.5 %block.1 = bf16[256,256]{1,0:T(8,128)(2,1)} custom-call(bf16[1,4,4096]{2,1,0:T(4,128)(2,1)} %a_new_ref.1, bf16[1,4,4096]{2,1,0:T(4,128)(2,1)} %a_old_ref.1, bf16[1,128,128]{2,1,0:T(8,128)(2,1)} %b_new_ref.1, bf16[1,128,128]{2,1,0:T(8,128)(2,1)} %b_old_ref.1), custom_call_target="tpu_custom_call" | custom-call | tf_op jit(solution)/shard_map/block/pallas_call | solution.py:191
  2.2 16.3 %collective-permute-start = (bf16[256,256]{1,0:T(8,128)(2,1)}, bf16[256,256]{1,0:T(8,128)(2,1)S(1)}, u32[]{:S(2)}, u32[]{:S(2)}) collective-permute-start(bf16[256,256]{1,0:T(8,128)(2,1)} %block.1), channel_id=1, source_target_pairs={{0,0},{1,129},{2,18},{3,147},{4,36},{5,165},{6,54},{7,183},{8,72},... | collective-permute-start | bytes 393224 | tf_op jit(solution)/shard_map/ppermute | solution.py:204
  18.4 2.1 %all-gather = bf16[256,256]{1,0:T(8,128)(2,1)S(1)} all-gather(bf16[128,256]{1,0:T(8,128)(2,1)} %param.7), channel_id=2, replica_groups={{0,1},{2,3},{4,5},{6,7},{8,9},{10,11},{12,13},{14,15},{16,17},{18,19},{..., dimensions={0}, use_global_device_ids=true | all-gather | bytes 196608 | tf_op jit(solution)/shard_map/all_gather | solution.py:206
  20.6 2.1 %collective-permute-start.4 = (bf16[4096,256]{1,0:T(8,128)(2,1)}, bf16[4096,256]{1,0:T(8,128)(2,1)}, u32[]{:S(2)}, u32[]{:S(2)}) collective-permute-start(bf16[4096,256]{1,0:T(8,128)(2,1)} %bitcast.19), channel_id=1, source_target_pairs={{0,1},{1,0},{2,3},{3,2},{4,5},{5,4},{6,7},{7,6},{8,9},{9,8},{10,11... | collective-permute-start | bytes 6291464 | tf_op jit(solution)/shard_map/ppermute | solution.py:208
  22.7 0.0 collective-permute-done.block_ref
  22.7 1.0 split.1
  23.7 9.6 %all-to-all-start = ((bf16[16,128,256]{2,1,0:T(8,128)(2,1)}), bf16[16,128,256]{2,1,0:T(8,128)(2,1)S(1)}, u32[]{:S(2)}, u32[]{:S(2)}) async-start(bf16[16,128,256]{2,1,0:T(8,128)(2,1)} %get-tuple-element.33), calls=%async_computation | async-start | bytes 2097152 | tf_op jit(solution)/shard_map/all_to_all | solution.py:226
  33.3 2.8 %collective-permute-start.2 = (bf16[128,256]{1,0:T(8,128)(2,1)S(1)}, bf16[128,256]{1,0:T(8,128)(2,1)S(1)}, u32[]{:S(2)}, u32[]{:S(2)}) collective-permute-start(bf16[128,256]{1,0:T(8,128)(2,1)S(1)} %get-tuple-element.35), channel_id=1, source_target_pairs={{0,256},{15,257},{13,0},{11,1},{9,258},{7,259},{5,2},{3,3},{1,260}... | collective-permute-start | bytes 196616 | tf_op jit(solution)/shard_map/ppermute | solution.py:225
  36.2 2.2 %collective-permute-start.1 = (bf16[128,256]{1,0:T(8,128)(2,1)S(1)}, bf16[128,256]{1,0:T(8,128)(2,1)S(1)}, u32[]{:S(2)}, u32[]{:S(2)}) collective-permute-start(bf16[128,256]{1,0:T(8,128)(2,1)S(1)} %get-tuple-element.35), channel_id=1, source_target_pairs={{0,0},{15,1},{13,256},{11,257},{9,2},{7,3},{5,258},{3,259},{1,4},{... | collective-permute-start | bytes 196616 | tf_op jit(solution)/shard_map/ppermute | solution.py:225
  38.3 9.4 %collective-permute-done.2 = bf16[128,256]{1,0:T(8,128)(2,1)S(1)} collective-permute-done((bf16[128,256]{1,0:T(8,128)(2,1)S(1)}, bf16[128,256]{1,0:T(8,128)(2,1)S(1)}, u32[]{:S(2)}, u32[]{:S(2)}) %collective-permute-start.2) | collective-permute-done | bytes 65568 | tf_op jit(solution)/shard_map/ppermute | solution.py:225
  47.7 3.3 %collective-permute-done.1 = bf16[128,256]{1,0:T(8,128)(2,1)S(1)} collective-permute-done((bf16[128,256]{1,0:T(8,128)(2,1)S(1)}, bf16[128,256]{1,0:T(8,128)(2,1)S(1)}, u32[]{:S(2)}, u32[]{:S(2)}) %collective-permute-start.1) | collective-permute-done | bytes 65568 | tf_op jit(solution)/shard_map/ppermute | solution.py:225
  51.0 0.0 all-to-all-done.own_ref
  51.0 1.9 %collective-permute-start.3 = (bf16[16,128,256]{2,1,0:T(8,128)(2,1)S(1)}, bf16[16,128,256]{2,1,0:T(8,128)(2,1)S(1)}, u32[]{:S(2)}, u32[]{:S(2)}) collective-permute-start(bf16[16,128,256]{2,1,0:T(8,128)(2,1)S(1)} %all-to-all-done.own_ref), channel_id=1, source_target_pairs={{0,1},{1,0},{2,3},{3,2},{4,5},{5,4},{6,7},{7,6},{8,9},{9,8},{10,11... | collective-permute-start | bytes 3145736 | tf_op jit(solution)/shard_map/ppermute | solution.py:229
  52.9 0.8 broadcast_in_dim.36
  53.7 3.5 %all-to-all-start.1 = ((bf16[8,128,256]{2,1,0:T(8,128)(2,1)}), bf16[8,128,256]{2,1,0:T(8,128)(2,1)S(1)}, u32[]{:S(2)}, u32[]{:S(2)}) async-start(bf16[8,128,256]{2,1,0:T(8,128)(2,1)} %broadcast_in_dim.36), calls=%async_computation.1 | async-start | bytes 1048576 | tf_op jit(solution)/shard_map/all_to_all | solution.py:46
  57.2 0.1 pad_add_fusion.place_ref
  57.4 2.1 %all-gather.1 = bf16[4,128,256]{2,1,0:T(8,128)(2,1)S(1)} all-gather(bf16[2,128,256]{2,1,0:T(8,128)(2,1)S(1)} %pad_maximum_fusion), channel_id=3, replica_groups={{0,1},{2,3},{4,5},{6,7},{8,9},{10,11},{12,13},{14,15},{16,17},{18,19},{..., dimensions={0}, use_global_device_ids=true | all-gather | bytes 393216 | tf_op jit(solution)/shard_map/all_gather | solution.py:230
  59.5 0.0 collective-permute-done.4.mate_ref
  59.5 1.6 %copy-done.1 = bf16[1,4096,256]{2,1,0:T(8,128)(2,1)S(1)} copy-done((bf16[1,4096,256]{2,1,0:T(8,128)(2,1)S(1)}, bf16[1,4096,256]{2,1,0:T(8,128)(2,1)}, u32[]{:S(2)}) %copy-start.1) | copy-done | bytes 2097176
  61.1 5.7 %merge.1 = (bf16[16,256,512]{2,1,0:T(8,128)(2,1)S(1)}, bf16[4096,256]{1,0:T(8,128)(2,1)}) custom-call(s32[3]{0:T(128)S(1)} %pad_add_fusion.place_ref, bf16[16,128,256]{2,1,0:T(8,128)(2,1)S(1)} %all-to-all-done.own_ref, bf16[16,128,256]{2,1,0:T(8,128)(2,1)S(1)} %collective-permute-done.3.other_ref, bf16[2,2,128,256]{3,2,1,0:T(8,128)(2,1)S(1)} %bitcast.21, ...), custom_call_target="tpu_custom_call" | custom-call | tf_op jit(solution)/shard_map/merge/pallas_call | solution.py:233
  66.9 1.9 %copy-done = bf16[16,256,512]{2,1,0:T(8,128)(2,1)} copy-done((bf16[16,256,512]{2,1,0:T(8,128)(2,1)}, bf16[16,256,512]{2,1,0:T(8,128)(2,1)S(1)}, u32[]{:S(2)}) %copy-start) | copy-done | bytes 4194328
  68.8 0.1 all-to-all-done.1.x_ref
  68.9 2.4 %first.1 = (bf16[2,64,256]{2,1,0:T(8,128)(2,1)S(1)}, bf16[64,256]{1,0:T(8,128)(2,1)S(1)}, bf16[16,256,512]{2,1,0:T(8,128)(2,1)S(1)}) custom-call(bf16[8,128,256]{2,1,0:T(8,128)(2,1)S(1)} %all-to-all-done.1.x_ref, bf16[16,256,512]{2,1,0:T(8,128)(2,1)} %copy-done, f32[16,1,256]{2,1,0:T(1,128)S(1)} %bitcast.26, bf16[2,64,256]{2,1,0:T(8,128)(2,1)S(1)} %reverse_select_fusion.mine_ref), custom_call_target="tpu_custom_call" | custom-call | tf_op jit(solution)/shard_map/first/pallas_call | solution.py:259
  71.4 17.8 %all_to_all.25.x_ref = bf16[8,128,256]{2,1,0:T(8,128)(2,1)S(1)} all-to-all(bf16[8,128,256]{2,1,0:T(8,128)(2,1)S(1)} %broadcast_in_dim.38), channel_id=1, replica_groups={{0,2,4,6,8,10,12,14},{1,3,5,7,9,11,13,15},{16,18,20,22,24,26,28,30},{17..., dimensions={0} | all-to-all | bytes 1048576 | tf_op jit(solution)/shard_map/all_to_all | solution.py:46
  89.3 1.0 step.3
  90.3 12.7 %all_to_all.26.x_ref = bf16[8,128,256]{2,1,0:T(8,128)(2,1)S(1)} all-to-all(bf16[8,128,256]{2,1,0:T(8,128)(2,1)S(1)} %broadcast_in_dim.40), channel_id=1, replica_groups={{0,2,4,6,8,10,12,14},{1,3,5,7,9,11,13,15},{16,18,20,22,24,26,28,30},{17..., dimensions={0} | all-to-all | bytes 1048576 | tf_op jit(solution)/shard_map/all_to_all | solution.py:46
  102.9 1.0 step.4
  104.0 11.7 %all_to_all.27.x_ref = bf16[8,128,256]{2,1,0:T(8,128)(2,1)S(1)} all-to-all(bf16[8,128,256]{2,1,0:T(8,128)(2,1)S(1)} %broadcast_in_dim.42), channel_id=1, replica_groups={{0,2,4,6,8,10,12,14},{1,3,5,7,9,11,13,15},{16,18,20,22,24,26,28,30},{17..., dimensions={0} | all-to-all | bytes 1048576 | tf_op jit(solution)/shard_map/all_to_all | solution.py:46
  115.7 1.0 step.5
  116.7 5.2 %collective-permute-start.5 = (bf16[4,64,256]{2,1,0:T(8,128)(2,1)S(1)}, bf16[4,64,256]{2,1,0:T(8,128)(2,1)S(1)}, u32[]{:S(2)}, u32[]{:S(2)}) collective-permute-start(bf16[4,64,256]{2,1,0:T(8,128)(2,1)S(1)} %pad_maximum_fusion.1), channel_id=1, source_target_pairs={{0,1},{1,0},{2,3},{3,2},{4,5},{5,4},{6,7},{7,6},{8,9},{9,8},{10,11... | collective-permute-start | bytes 393224 | tf_op jit(solution)/shard_map/ppermute | solution.py:276
  121.9 1.0 collective-permute-done.5.swapped_ref
  122.9 0.7 finish.1
  (13 shorter events, 0.2 us)
Async XLA Ops:
  0.6 56.7 %copy-start.2 = (f32[1,4096]{1,0:T(1,128)S(1)}, f32[1,4096]{1,0:T(1,128)}, u32[]{:S(2)}) copy-start(f32[1,4096]{1,0:T(1,128)} %param.13) | copy-start | bytes 49156
  2.2 20.5 %collective-permute-start = (bf16[256,256]{1,0:T(8,128)(2,1)}, bf16[256,256]{1,0:T(8,128)(2,1)S(1)}, u32[]{:S(2)}, u32[]{:S(2)}) collective-permute-start(bf16[256,256]{1,0:T(8,128)(2,1)} %block.1), channel_id=1, source_target_pairs={{0,0},{1,129},{2,18},{3,147},{4,36},{5,165},{6,54},{7,183},{8,72},... | collective-permute-start | bytes 393224 | tf_op jit(solution)/shard_map/ppermute | solution.py:204
  20.6 38.9 %collective-permute-start.4 = (bf16[4096,256]{1,0:T(8,128)(2,1)}, bf16[4096,256]{1,0:T(8,128)(2,1)}, u32[]{:S(2)}, u32[]{:S(2)}) collective-permute-start(bf16[4096,256]{1,0:T(8,128)(2,1)} %bitcast.19), channel_id=1, source_target_pairs={{0,1},{1,0},{2,3},{3,2},{4,5},{5,4},{6,7},{7,6},{8,9},{9,8},{10,11... | collective-permute-start | bytes 6291464 | tf_op jit(solution)/shard_map/ppermute | solution.py:208
  23.7 27.2 %all-to-all-start = ((bf16[16,128,256]{2,1,0:T(8,128)(2,1)}), bf16[16,128,256]{2,1,0:T(8,128)(2,1)S(1)}, u32[]{:S(2)}, u32[]{:S(2)}) async-start(bf16[16,128,256]{2,1,0:T(8,128)(2,1)} %get-tuple-element.33), calls=%async_computation | async-start | bytes 2097152 | tf_op jit(solution)/shard_map/all_to_all | solution.py:226
  33.3 14.4 %collective-permute-start.2 = (bf16[128,256]{1,0:T(8,128)(2,1)S(1)}, bf16[128,256]{1,0:T(8,128)(2,1)S(1)}, u32[]{:S(2)}, u32[]{:S(2)}) collective-permute-start(bf16[128,256]{1,0:T(8,128)(2,1)S(1)} %get-tuple-element.35), channel_id=1, source_target_pairs={{0,256},{15,257},{13,0},{11,1},{9,258},{7,259},{5,2},{3,3},{1,260}... | collective-permute-start | bytes 196616 | tf_op jit(solution)/shard_map/ppermute | solution.py:225
  36.2 14.8 %collective-permute-start.1 = (bf16[128,256]{1,0:T(8,128)(2,1)S(1)}, bf16[128,256]{1,0:T(8,128)(2,1)S(1)}, u32[]{:S(2)}, u32[]{:S(2)}) collective-permute-start(bf16[128,256]{1,0:T(8,128)(2,1)S(1)} %get-tuple-element.35), channel_id=1, source_target_pairs={{0,0},{15,1},{13,256},{11,257},{9,2},{7,3},{5,258},{3,259},{1,4},{... | collective-permute-start | bytes 196616 | tf_op jit(solution)/shard_map/ppermute | solution.py:225
  51.0 8.5 %collective-permute-start.3 = (bf16[16,128,256]{2,1,0:T(8,128)(2,1)S(1)}, bf16[16,128,256]{2,1,0:T(8,128)(2,1)S(1)}, u32[]{:S(2)}, u32[]{:S(2)}) collective-permute-start(bf16[16,128,256]{2,1,0:T(8,128)(2,1)S(1)} %all-to-all-done.own_ref), channel_id=1, source_target_pairs={{0,1},{1,0},{2,3},{3,2},{4,5},{5,4},{6,7},{7,6},{8,9},{9,8},{10,11... | collective-permute-start | bytes 3145736 | tf_op jit(solution)/shard_map/ppermute | solution.py:229
  53.7 15.2 %all-to-all-start.1 = ((bf16[8,128,256]{2,1,0:T(8,128)(2,1)}), bf16[8,128,256]{2,1,0:T(8,128)(2,1)S(1)}, u32[]{:S(2)}, u32[]{:S(2)}) async-start(bf16[8,128,256]{2,1,0:T(8,128)(2,1)} %broadcast_in_dim.36), calls=%async_computation.1 | async-start | bytes 1048576 | tf_op jit(solution)/shard_map/all_to_all | solution.py:46
  59.5 1.6 %copy-start.1 = (bf16[1,4096,256]{2,1,0:T(8,128)(2,1)S(1)}, bf16[1,4096,256]{2,1,0:T(8,128)(2,1)}, u32[]{:S(2)}) copy-start(bf16[1,4096,256]{2,1,0:T(8,128)(2,1)} %param.8) | copy-start | bytes 6291460
  66.9 2.0 %copy-start = (bf16[16,256,512]{2,1,0:T(8,128)(2,1)}, bf16[16,256,512]{2,1,0:T(8,128)(2,1)S(1)}, u32[]{:S(2)}) copy-start(bf16[16,256,512]{2,1,0:T(8,128)(2,1)S(1)} %get-tuple-element.41.stored_ref) | copy-start | bytes 12582916
  116.7 6.2 %collective-permute-start.5 = (bf16[4,64,256]{2,1,0:T(8,128)(2,1)S(1)}, bf16[4,64,256]{2,1,0:T(8,128)(2,1)S(1)}, u32[]{:S(2)}, u32[]{:S(2)}) collective-permute-start(bf16[4,64,256]{2,1,0:T(8,128)(2,1)S(1)} %pad_maximum_fusion.1), channel_id=1, source_target_pairs={{0,1},{1,0},{2,3},{3,2},{4,5},{5,4},{6,7},{7,6},{8,9},{9,8},{10,11... | collective-permute-start | bytes 393224 | tf_op jit(solution)/shard_map/ppermute | solution.py:276

commit v7 on v6

--- a/solution.py
+++ b/solution.py
@@ -38,7 +38,7 @@
 VMEM = pl.BlockSpec(memory_space=pltpu.VMEM)
 SMEM = pl.BlockSpec(memory_space=pltpu.SMEM)
 HBM = pl.BlockSpec(memory_space=pltpu.HBM)
-WIDE = pltpu.CompilerParams(vmem_limit_bytes=32 * 1024 * 1024)
+WIDE = pltpu.CompilerParams(vmem_limit_bytes=51 * 1024 * 1024)
 ROOM = pltpu.CompilerParams(vmem_limit_bytes=16 * 1024 * 1024)
 
 
@@ -112,7 +112,7 @@
             load.wait()
         for right in range(2):
             down = jnp.concatenate([part[:, right].reshape(128, cols) for part in parts], 0)
-            down = down.T.astype(jnp.bfloat16)
+            down = down.astype(jnp.bfloat16).T
             delta = lax.dot_general(down, up, (((1,), (1,)), ((), ())), preferred_element_type=jnp.float32)
             t = 2 * pair + right
             rows = slice(t * cols, (t + 1) * cols)

time: 124 us -> 121 us (0.976)
  waiting for transfers between devices: 13.7 us -> 17.4 us
  blocking collectives: 46.4 us -> 42.8 us
  local copies, waits for them, and re-layouts: 4.51 us -> 0.97 us
    all_to_all x1, waiting for transfers between devices: 0.13 us -> 3.83 us  [spread(): return lax.all_to_all(blocks, 'tp', 0, 0, axis_index_groups=GROUPS)]
    all_to_all x3, blocking collectives: 42.2 us -> 38.5 us  [spread(): return lax.all_to_all(blocks, 'tp', 0, 0, axis_index_groups=GROUPS)]
    unnamed x6 -> x2, local copies, waits for them, and re-layouts: 3.55 us -> 0.01 us
  transfers between devices with their start and end apart: 8 -> 8, of which waited for: 4 -> 4; matrix products, arithmetic and copies ran while one was open for 1% -> 1% of each run, Pallas kernels for 5% -> 6%
where the time goes in v7:
time: 121 us; the launch traced here: 120 us
  starting transfers between devices  43.5 us (36%)
  blocking collectives  42.8 us (35%)
  waiting for transfers between devices  17.4 us (14%)
  Pallas kernels  14.3 us (12%)
    all_to_all x3, blocking collectives, spread(): return lax.all_to_all(blocks, 'tp', 0, 0, axis_index_groups=GROUPS)  38.5 us
    ppermute x1, starting transfers between devices, shards(): block = lax.ppermute(block, ('fsdp', 'tp'), SHIFTED)  16.3 us
    ppermute x2, waiting for transfers between devices, shards(): ups = [lax.ppermute(up, ('fsdp', 'tp'), relay(part)) for part in range(2)]  12.6 us
    all_to_all x1, starting transfers between devices, shards(): own = lax.all_to_all(down, ('fsdp', 'tp'), 0, 0, axis_index_groups=PLANES)  9.58 us
    pallas_call x1, Pallas kernels, shards(): pl.pallas_call(merge_kernel, out_shape=(jax.ShapeDtypeStruct((tp, cols, 2...  5.6 us
    pallas_call x4, Pallas kernels, shards(): pl.pallas_call(step_kernel if step else first_kernel, out_shape=(jax.Shap...  5.37 us
    ppermute x1, starting transfers between devices, shards(): swapped = lax.ppermute(jnp.stack(gives), 'tp', SWAP)  5.21 us
    ppermute x2, starting transfers between devices, shards(): ups = [lax.ppermute(up, ('fsdp', 'tp'), relay(part)) for part in range(2)]  5 us
  transfers between devices with their start and end apart: 8, of which 4 were waited for; matrix products, arithmetic and copies ran while one was open for 1% of the time, Pallas kernels for 6%

profile of v7, /device:TPU:1, one launch (start us, length us, event | category | flops | bytes accessed | tf_op | source)
XLA Modules:
  0.0 119.9 jit_solution(3402848576637663320)
XLA Ops:
  0.6 0.0 copy-start
  0.6 1.5 %block.1 = bf16[256,256]{1,0:T(8,128)(2,1)} custom-call(bf16[1,4,4096]{2,1,0:T(4,128)(2,1)} %a_new_ref.1, bf16[1,4,4096]{2,1,0:T(4,128)(2,1)} %a_old_ref.1, bf16[1,128,128]{2,1,0:T(8,128)(2,1)} %b_new_ref.1, bf16[1,128,128]{2,1,0:T(8,128)(2,1)} %b_old_ref.1), custom_call_target="tpu_custom_call" | custom-call | tf_op jit(solution)/shard_map/block/pallas_call | solution.py:191
  2.2 16.3 %collective-permute-start = (bf16[256,256]{1,0:T(8,128)(2,1)}, bf16[256,256]{1,0:T(8,128)(2,1)S(1)}, u32[]{:S(2)}, u32[]{:S(2)}) collective-permute-start(bf16[256,256]{1,0:T(8,128)(2,1)} %block.1), channel_id=1, source_target_pairs={{0,0},{1,129},{2,18},{3,147},{4,36},{5,165},{6,54},{7,183},{8,72},... | collective-permute-start | bytes 393224 | tf_op jit(solution)/shard_map/ppermute | solution.py:204
  18.4 2.1 %all-gather = bf16[256,256]{1,0:T(8,128)(2,1)S(1)} all-gather(bf16[128,256]{1,0:T(8,128)(2,1)} %param.7), channel_id=2, replica_groups={{0,1},{2,3},{4,5},{6,7},{8,9},{10,11},{12,13},{14,15},{16,17},{18,19},{..., dimensions={0}, use_global_device_ids=true | all-gather | bytes 196608 | tf_op jit(solution)/shard_map/all_gather | solution.py:206
  20.6 2.1 %collective-permute-start.4 = (bf16[4096,256]{1,0:T(8,128)(2,1)}, bf16[4096,256]{1,0:T(8,128)(2,1)}, u32[]{:S(2)}, u32[]{:S(2)}) collective-permute-start(bf16[4096,256]{1,0:T(8,128)(2,1)} %bitcast.32), channel_id=1, source_target_pairs={{0,1},{1,0},{2,3},{3,2},{4,5},{5,4},{6,7},{7,6},{8,9},{9,8},{10,11... | collective-permute-start | bytes 6291464 | tf_op jit(solution)/shard_map/ppermute | solution.py:208
  22.7 0.0 collective-permute-done.block_ref
  22.7 1.0 split.1
  23.7 9.6 %all-to-all-start = ((bf16[16,128,256]{2,1,0:T(8,128)(2,1)}), bf16[16,128,256]{2,1,0:T(8,128)(2,1)S(1)}, u32[]{:S(2)}, u32[]{:S(2)}) async-start(bf16[16,128,256]{2,1,0:T(8,128)(2,1)} %get-tuple-element.33), calls=%async_computation | async-start | bytes 2097152 | tf_op jit(solution)/shard_map/all_to_all | solution.py:226
  33.3 2.8 %collective-permute-start.2 = (bf16[128,256]{1,0:T(8,128)(2,1)S(1)}, bf16[128,256]{1,0:T(8,128)(2,1)S(1)}, u32[]{:S(2)}, u32[]{:S(2)}) collective-permute-start(bf16[128,256]{1,0:T(8,128)(2,1)S(1)} %get-tuple-element.35), channel_id=1, source_target_pairs={{0,256},{15,257},{13,0},{11,1},{9,258},{7,259},{5,2},{3,3},{1,260}... | collective-permute-start | bytes 196616 | tf_op jit(solution)/shard_map/ppermute | solution.py:225
  36.2 2.2 %collective-permute-start.1 = (bf16[128,256]{1,0:T(8,128)(2,1)S(1)}, bf16[128,256]{1,0:T(8,128)(2,1)S(1)}, u32[]{:S(2)}, u32[]{:S(2)}) collective-permute-start(bf16[128,256]{1,0:T(8,128)(2,1)S(1)} %get-tuple-element.35), channel_id=1, source_target_pairs={{0,0},{15,1},{13,256},{11,257},{9,2},{7,3},{5,258},{3,259},{1,4},{... | collective-permute-start | bytes 196616 | tf_op jit(solution)/shard_map/ppermute | solution.py:225
  38.3 9.4 %collective-permute-done.2 = bf16[128,256]{1,0:T(8,128)(2,1)S(1)} collective-permute-done((bf16[128,256]{1,0:T(8,128)(2,1)S(1)}, bf16[128,256]{1,0:T(8,128)(2,1)S(1)}, u32[]{:S(2)}, u32[]{:S(2)}) %collective-permute-start.2) | collective-permute-done | bytes 65568 | tf_op jit(solution)/shard_map/ppermute | solution.py:225
  47.7 3.3 %collective-permute-done.1 = bf16[128,256]{1,0:T(8,128)(2,1)S(1)} collective-permute-done((bf16[128,256]{1,0:T(8,128)(2,1)S(1)}, bf16[128,256]{1,0:T(8,128)(2,1)S(1)}, u32[]{:S(2)}, u32[]{:S(2)}) %collective-permute-start.1) | collective-permute-done | bytes 65568 | tf_op jit(solution)/shard_map/ppermute | solution.py:225
  51.0 0.0 all-to-all-done.own_ref
  51.0 1.9 %collective-permute-start.3 = (bf16[16,128,256]{2,1,0:T(8,128)(2,1)S(1)}, bf16[16,128,256]{2,1,0:T(8,128)(2,1)S(1)}, u32[]{:S(2)}, u32[]{:S(2)}) collective-permute-start(bf16[16,128,256]{2,1,0:T(8,128)(2,1)S(1)} %all-to-all-done.own_ref), channel_id=1, source_target_pairs={{0,1},{1,0},{2,3},{3,2},{4,5},{5,4},{6,7},{7,6},{8,9},{9,8},{10,11... | collective-permute-start | bytes 3145736 | tf_op jit(solution)/shard_map/ppermute | solution.py:229
  52.9 0.8 broadcast_in_dim.36
  53.8 3.5 %all-to-all-start.1 = ((bf16[8,128,256]{2,1,0:T(8,128)(2,1)}), bf16[8,128,256]{2,1,0:T(8,128)(2,1)S(1)}, u32[]{:S(2)}, u32[]{:S(2)}) async-start(bf16[8,128,256]{2,1,0:T(8,128)(2,1)} %broadcast_in_dim.36), calls=%async_computation.1 | async-start | bytes 1048576 | tf_op jit(solution)/shard_map/all_to_all | solution.py:46
  57.3 0.1 pad_add_fusion.place_ref
  57.4 2.1 %all-gather.1 = bf16[4,128,256]{2,1,0:T(8,128)(2,1)S(1)} all-gather(bf16[2,128,256]{2,1,0:T(8,128)(2,1)S(1)} %pad_maximum_fusion), channel_id=3, replica_groups={{0,1},{2,3},{4,5},{6,7},{8,9},{10,11},{12,13},{14,15},{16,17},{18,19},{..., dimensions={0}, use_global_device_ids=true | all-gather | bytes 393216 | tf_op jit(solution)/shard_map/all_gather | solution.py:230
  59.5 0.0 collective-permute-done.4.mate_ref
  59.5 0.0 collective-permute-done.3.other_ref
  59.5 5.6 %merge.1 = (bf16[16,256,512]{2,1,0:T(8,128)(2,1)}, bf16[4096,256]{1,0:T(8,128)(2,1)}) custom-call(s32[3]{0:T(128)S(1)} %pad_add_fusion.place_ref, bf16[16,128,256]{2,1,0:T(8,128)(2,1)S(1)} %all-to-all-done.own_ref, bf16[16,128,256]{2,1,0:T(8,128)(2,1)S(1)} %collective-permute-done.3.other_ref, bf16[2,2,128,256]{3,2,1,0:T(8,128)(2,1)S(1)} %bitcast.19, ...), custom_call_target="tpu_custom_call" | custom-call | tf_op jit(solution)/shard_map/merge/pallas_call | solution.py:233
  65.1 3.8 %all-to-all-done.1.x_ref = bf16[8,128,256]{2,1,0:T(8,128)(2,1)S(1)} async-done(((bf16[8,128,256]{2,1,0:T(8,128)(2,1)}), bf16[8,128,256]{2,1,0:T(8,128)(2,1)S(1)}, u32[]{:S(2)}, u32[]{:S(2)}) %all-to-all-start.1) | async-done | bytes 524320 | tf_op jit(solution)/shard_map/all_to_all | solution.py:46
  69.0 2.4 %first.1 = (bf16[2,64,256]{2,1,0:T(8,128)(2,1)S(1)}, bf16[64,256]{1,0:T(8,128)(2,1)S(1)}, bf16[16,256,512]{2,1,0:T(8,128)(2,1)S(1)}) custom-call(bf16[8,128,256]{2,1,0:T(8,128)(2,1)S(1)} %all-to-all-done.1.x_ref, bf16[16,256,512]{2,1,0:T(8,128)(2,1)} %get-tuple-element.41.stored_ref, f32[16,1,256]{2,1,0:T(1,128)S(1)} %bitcast.24, ...), custom_call_target="tpu_custom_call" | custom-call | tf_op jit(solution)/shard_map/first/pallas_call | solution.py:259
  71.4 14.2 %all_to_all.25.x_ref = bf16[8,128,256]{2,1,0:T(8,128)(2,1)S(1)} all-to-all(bf16[8,128,256]{2,1,0:T(8,128)(2,1)S(1)} %broadcast_in_dim.38), channel_id=1, replica_groups={{0,2,4,6,8,10,12,14},{1,3,5,7,9,11,13,15},{16,18,20,22,24,26,28,30},{17..., dimensions={0} | all-to-all | bytes 1048576 | tf_op jit(solution)/shard_map/all_to_all | solution.py:46
  85.6 1.0 step.3
  86.6 12.7 %all_to_all.26.x_ref = bf16[8,128,256]{2,1,0:T(8,128)(2,1)S(1)} all-to-all(bf16[8,128,256]{2,1,0:T(8,128)(2,1)S(1)} %broadcast_in_dim.40), channel_id=1, replica_groups={{0,2,4,6,8,10,12,14},{1,3,5,7,9,11,13,15},{16,18,20,22,24,26,28,30},{17..., dimensions={0} | all-to-all | bytes 1048576 | tf_op jit(solution)/shard_map/all_to_all | solution.py:46
  99.3 1.0 step.4
  100.3 11.7 %all_to_all.27.x_ref = bf16[8,128,256]{2,1,0:T(8,128)(2,1)S(1)} all-to-all(bf16[8,128,256]{2,1,0:T(8,128)(2,1)S(1)} %broadcast_in_dim.42), channel_id=1, replica_groups={{0,2,4,6,8,10,12,14},{1,3,5,7,9,11,13,15},{16,18,20,22,24,26,28,30},{17..., dimensions={0} | all-to-all | bytes 1048576 | tf_op jit(solution)/shard_map/all_to_all | solution.py:46
  112.0 1.0 step.5
  113.0 5.2 %collective-permute-start.5 = (bf16[4,64,256]{2,1,0:T(8,128)(2,1)S(1)}, bf16[4,64,256]{2,1,0:T(8,128)(2,1)S(1)}, u32[]{:S(2)}, u32[]{:S(2)}) collective-permute-start(bf16[4,64,256]{2,1,0:T(8,128)(2,1)S(1)} %pad_maximum_fusion.1), channel_id=1, source_target_pairs={{0,1},{1,0},{2,3},{3,2},{4,5},{5,4},{6,7},{7,6},{8,9},{9,8},{10,11... | collective-permute-start | bytes 393224 | tf_op jit(solution)/shard_map/ppermute | solution.py:276
  118.2 1.0 collective-permute-done.5.swapped_ref
  119.2 0.7 finish.1
  (9 shorter events, 0.2 us)
Async XLA Ops:
  0.6 56.7 %copy-start = (f32[1,4096]{1,0:T(1,128)S(1)}, f32[1,4096]{1,0:T(1,128)}, u32[]{:S(2)}) copy-start(f32[1,4096]{1,0:T(1,128)} %param.13) | copy-start | bytes 49156
  2.2 20.5 %collective-permute-start = (bf16[256,256]{1,0:T(8,128)(2,1)}, bf16[256,256]{1,0:T(8,128)(2,1)S(1)}, u32[]{:S(2)}, u32[]{:S(2)}) collective-permute-start(bf16[256,256]{1,0:T(8,128)(2,1)} %block.1), channel_id=1, source_target_pairs={{0,0},{1,129},{2,18},{3,147},{4,36},{5,165},{6,54},{7,183},{8,72},... | collective-permute-start | bytes 393224 | tf_op jit(solution)/shard_map/ppermute | solution.py:204
  20.6 38.9 %collective-permute-start.4 = (bf16[4096,256]{1,0:T(8,128)(2,1)}, bf16[4096,256]{1,0:T(8,128)(2,1)}, u32[]{:S(2)}, u32[]{:S(2)}) collective-permute-start(bf16[4096,256]{1,0:T(8,128)(2,1)} %bitcast.32), channel_id=1, source_target_pairs={{0,1},{1,0},{2,3},{3,2},{4,5},{5,4},{6,7},{7,6},{8,9},{9,8},{10,11... | collective-permute-start | bytes 6291464 | tf_op jit(solution)/shard_map/ppermute | solution.py:208
  23.7 27.2 %all-to-all-start = ((bf16[16,128,256]{2,1,0:T(8,128)(2,1)}), bf16[16,128,256]{2,1,0:T(8,128)(2,1)S(1)}, u32[]{:S(2)}, u32[]{:S(2)}) async-start(bf16[16,128,256]{2,1,0:T(8,128)(2,1)} %get-tuple-element.33), calls=%async_computation | async-start | bytes 2097152 | tf_op jit(solution)/shard_map/all_to_all | solution.py:226
  33.3 14.4 %collective-permute-start.2 = (bf16[128,256]{1,0:T(8,128)(2,1)S(1)}, bf16[128,256]{1,0:T(8,128)(2,1)S(1)}, u32[]{:S(2)}, u32[]{:S(2)}) collective-permute-start(bf16[128,256]{1,0:T(8,128)(2,1)S(1)} %get-tuple-element.35), channel_id=1, source_target_pairs={{0,256},{15,257},{13,0},{11,1},{9,258},{7,259},{5,2},{3,3},{1,260}... | collective-permute-start | bytes 196616 | tf_op jit(solution)/shard_map/ppermute | solution.py:225
  36.2 14.8 %collective-permute-start.1 = (bf16[128,256]{1,0:T(8,128)(2,1)S(1)}, bf16[128,256]{1,0:T(8,128)(2,1)S(1)}, u32[]{:S(2)}, u32[]{:S(2)}) collective-permute-start(bf16[128,256]{1,0:T(8,128)(2,1)S(1)} %get-tuple-element.35), channel_id=1, source_target_pairs={{0,0},{15,1},{13,256},{11,257},{9,2},{7,3},{5,258},{3,259},{1,4},{... | collective-permute-start | bytes 196616 | tf_op jit(solution)/shard_map/ppermute | solution.py:225
  51.0 8.5 %collective-permute-start.3 = (bf16[16,128,256]{2,1,0:T(8,128)(2,1)S(1)}, bf16[16,128,256]{2,1,0:T(8,128)(2,1)S(1)}, u32[]{:S(2)}, u32[]{:S(2)}) collective-permute-start(bf16[16,128,256]{2,1,0:T(8,128)(2,1)S(1)} %all-to-all-done.own_ref), channel_id=1, source_target_pairs={{0,1},{1,0},{2,3},{3,2},{4,5},{5,4},{6,7},{7,6},{8,9},{9,8},{10,11... | collective-permute-start | bytes 3145736 | tf_op jit(solution)/shard_map/ppermute | solution.py:229
  53.8 15.2 %all-to-all-start.1 = ((bf16[8,128,256]{2,1,0:T(8,128)(2,1)}), bf16[8,128,256]{2,1,0:T(8,128)(2,1)S(1)}, u32[]{:S(2)}, u32[]{:S(2)}) async-start(bf16[8,128,256]{2,1,0:T(8,128)(2,1)} %broadcast_in_dim.36), calls=%async_computation.1 | async-start | bytes 1048576 | tf_op jit(solution)/shard_map/all_to_all | solution.py:46
  113.0 6.2 %collective-permute-start.5 = (bf16[4,64,256]{2,1,0:T(8,128)(2,1)S(1)}, bf16[4,64,256]{2,1,0:T(8,128)(2,1)S(1)}, u32[]{:S(2)}, u32[]{:S(2)}) collective-permute-start(bf16[4,64,256]{2,1,0:T(8,128)(2,1)S(1)} %pad_maximum_fusion.1), channel_id=1, source_target_pairs={{0,1},{1,0},{2,3},{3,2},{4,5},{5,4},{6,7},{7,6},{8,9},{9,8},{10,11... | collective-permute-start | bytes 393224 | tf_op jit(solution)/shard_map/ppermute | solution.py:276

commit v8 on v7

--- a/solution.py
+++ b/solution.py
@@ -15,12 +15,17 @@
     for z in range(16)
     for core in range(2)
 ]
-SHIFTED = [
-    ((16 * low + z) * 16 + t, (16 * low + (z + t // 2 + 8 * (t % 2)) % 16) * 16 + t)
-    for low in range(2)
-    for z in range(16)
-    for t in range(16)
-]
+DOWN_SHIFTS = [(t // 2 + 8 * (t % 2)) % 16 for t in range(16)]
+UP_SHIFTS = [(8 * (t % 2) - t // 2) % 16 for t in range(16)]
+
+
+def shifted(shifts):
+    return [
+        ((16 * low + z) * 16 + t, (16 * low + (z + shifts[t]) % 16) * 16 + t)
+        for low in range(2)
+        for z in range(16)
+        for t in range(16)
+    ]
 
 
 def relay(part):
@@ -28,8 +33,7 @@
     for z in range(16):
         for low in range(2):
             for block in range(16):
-                shift = (z - block) % 16
-                source = (16 * low + z) * 16 + 2 * (shift % 8) + shift // 8
+                source = (16 * low + z) * 16 + UP_SHIFTS.index((z - block) % 16)
                 target = 16 * ((block % 4 // 2) ^ part) + z
                 pairs.append((source, target * 16 + 8 * low + 2 * (block // 4) + block % 2))
     return pairs
@@ -46,7 +50,7 @@
     return lax.all_to_all(blocks, "tp", 0, 0, axis_index_groups=GROUPS)
 
 
-def block_kernel(a_new_ref, a_old_ref, b_new_ref, b_old_ref, out_ref, a_ref, b_ref, sems):
+def block_kernel(a_new_ref, a_old_ref, b_new_ref, b_old_ref, down_ref, up_ref, a_ref, b_ref, sems):
     copies = [
         pltpu.make_async_copy(source, target, sems.at[i])
         for i, (source, target) in enumerate(
@@ -57,21 +61,14 @@
         copy.start()
     for copy in copies:
         copy.wait()
-    half, cols = out_ref.shape[0] // 2, out_ref.shape[1]
+    cols = down_ref.shape[1]
     new = a_ref[0, 0].astype(jnp.float32)
     old = a_ref[1, 0].astype(jnp.float32)
     slices = []
     for i in range(new.shape[1] // cols):
         slices += [new[:, i * cols : (i + 1) * cols], old[:, i * cols : (i + 1) * cols]]
-    out_ref[:half, :] = jnp.concatenate(slices, 0).astype(jnp.bfloat16)
-    out_ref[half:, :] = jnp.concatenate([b_ref[0, 0], -b_ref[1, 0]], 1)
-
-
-def split_kernel(block_ref, down_ref, up_ref):
-    half = up_ref.shape[0]
-    for chip in range(down_ref.shape[0]):
-        down_ref[chip] = block_ref[:half, :]
-    up_ref[...] = block_ref[half:, :]
+    down_ref[...] = jnp.concatenate(slices, 0).astype(jnp.bfloat16)
+    up_ref[...] = jnp.concatenate([b_ref[0, 0], -b_ref[1, 0]], 1)
 
 
 def merge_kernel(
@@ -188,11 +185,12 @@
     core = lax.rem(t, 2)
     half = rows // 2
 
-    block = pl.pallas_call(
+    size = b_old.shape[1]
+    down, up = pl.pallas_call(
         block_kernel,
-        out_shape=jax.ShapeDtypeStruct((2 * b_old.shape[1], cols), jnp.bfloat16),
+        out_shape=(jax.ShapeDtypeStruct((size, cols), jnp.bfloat16),) * 2,
         in_specs=[HBM] * 4,
-        out_specs=VMEM,
+        out_specs=(VMEM, VMEM),
         scratch_shapes=[
             pltpu.VMEM((2,) + a_new.shape, jnp.bfloat16),
             pltpu.VMEM((2,) + b_new.shape, jnp.bfloat16),
@@ -200,8 +198,9 @@
         ],
         name="block",
     )(a_new, a_old, b_new, b_old)
-    block, tokens = lax.optimization_barrier((block, tokens))
-    block = lax.ppermute(block, ("fsdp", "tp"), SHIFTED)
+    down, up, tokens = lax.optimization_barrier((down, up, tokens))
+    down = lax.ppermute(down, ("fsdp", "tp"), shifted(DOWN_SHIFTS))
+    up = lax.ppermute(up, ("fsdp", "tp"), shifted(UP_SHIFTS))
 
     both = lax.all_gather(tokens, "tp", axis=0, axis_index_groups=PAIRS)
     both, base = lax.optimization_barrier((both, base_weight[0]))
@@ -209,19 +208,8 @@
     both = lax.dynamic_slice_in_dim(both, core * half, half, 1)
     stream = jnp.where(core == 0, both, both[::-1])
 
-    size = block.shape[0] // 2
-    down, up = pl.pallas_call(
-        split_kernel,
-        out_shape=(
-            jax.ShapeDtypeStruct((len(PLANES[0]), size, cols), jnp.bfloat16),
-            jax.ShapeDtypeStruct((size, cols), jnp.bfloat16),
-        ),
-        in_specs=[VMEM],
-        out_specs=(VMEM, VMEM),
-        name="split",
-        compiler_params=ROOM,
-    )(block)
     down, up, stream = lax.optimization_barrier((down, up, stream))
+    down = jnp.broadcast_to(down[None], (len(PLANES[0]), size, cols))
     ups = [lax.ppermute(up, ("fsdp", "tp"), relay(part)) for part in range(2)]
     own = lax.all_to_all(down, ("fsdp", "tp"), 0, 0, axis_index_groups=PLANES)
     own, stream, *ups = lax.optimization_barrier((own, stream, *ups))

time: 121 us -> 129 us (1.066)
  waiting for transfers between devices: 17.4 us -> 24.9 us
    ppermute x1 -> x2, waiting for transfers between devices: 0.01 us -> 7.78 us  [the longest x1 7.78 us: shards(): up = lax.ppermute(up, ('fsdp', 'tp'), shifted(UP_SHIFTS))]
    ppermute x2, waiting for transfers between devices: 12.6 us -> 8.04 us  [shards(): ups = [lax.ppermute(up, ('fsdp', 'tp'), relay(part)) for part in range(2)]]
    all_to_all x1, starting transfers between devices: 9.58 us -> 5.06 us  [shards(): own = lax.all_to_all(down, ('fsdp', 'tp'), 0, 0, axis_index_groups=PLANES)]
    all_to_all x1, waiting for transfers between devices: 0.01 us -> 4.38 us  [shards(): own = lax.all_to_all(down, ('fsdp', 'tp'), 0, 0, axis_index_groups=PLANES)]
    ppermute x2, starting transfers between devices: 5 us -> 6.98 us  [shards(): ups = [lax.ppermute(up, ('fsdp', 'tp'), relay(part)) for part in range(2)]]
    ppermute x1 -> x2, starting transfers between devices: 16.3 us -> 18.2 us  [the longest x1 16.3 us: shards(): down = lax.ppermute(down, ('fsdp', 'tp'), shifted(DOWN_SHIFTS))]
  transfers between devices with their start and end apart: 8 -> 9, of which waited for: 4 -> 6; matrix products, arithmetic and copies ran while one was open for 1% -> 2% of each run, Pallas kernels for 6% -> 4%
where the time goes in v8:
time: 129 us; the launch traced here: 128 us
  starting transfers between devices  43.8 us (34%)
  blocking collectives  43 us (33%)
  waiting for transfers between devices  24.9 us (19%)
  Pallas kernels  13.2 us (10%)
  local copies, waits for them, and re-layouts  2.03 us (2%)
    all_to_all x3, blocking collectives, spread(): return lax.all_to_all(blocks, 'tp', 0, 0, axis_index_groups=GROUPS)  38.7 us
    ppermute x1, starting transfers between devices, shards(): down = lax.ppermute(down, ('fsdp', 'tp'), shifted(DOWN_SHIFTS))  16.3 us
    ppermute x2, waiting for transfers between devices, shards(): ups = [lax.ppermute(up, ('fsdp', 'tp'), relay(part)) for part in range(2)]  8.04 us
    ppermute x1, waiting for transfers between devices, shards(): up = lax.ppermute(up, ('fsdp', 'tp'), shifted(UP_SHIFTS))  7.78 us
    ppermute x2, starting transfers between devices, shards(): ups = [lax.ppermute(up, ('fsdp', 'tp'), relay(part)) for part in range(2)]  6.98 us
    pallas_call x1, Pallas kernels, shards(): pl.pallas_call(merge_kernel, out_shape=(jax.ShapeDtypeStruct((tp, cols, 2...  5.59 us
    pallas_call x4, Pallas kernels, shards(): pl.pallas_call(step_kernel if step else first_kernel, out_shape=(jax.Shap...  5.37 us
    ppermute x1, starting transfers between devices, shards(): swapped = lax.ppermute(jnp.stack(gives), 'tp', SWAP)  5.21 us
  transfers between devices with their start and end apart: 9, of which 6 were waited for; matrix products, arithmetic and copies ran while one was open for 2% of the time, Pallas kernels for 4%

profile of v8, /device:TPU:1, one launch (start us, length us, event | category | flops | bytes accessed | tf_op | source)
XLA Modules:
  0.0 128.0 jit_solution(7239139665963936132)
XLA Ops:
  0.6 1.5 %block.1 = (bf16[128,256]{1,0:T(8,128)(2,1)}, bf16[128,256]{1,0:T(8,128)(2,1)}) custom-call(bf16[1,4,4096]{2,1,0:T(4,128)(2,1)} %a_new_ref.1, bf16[1,4,4096]{2,1,0:T(4,128)(2,1)} %a_old_ref.1, bf16[1,128,128]{2,1,0:T(8,128)(2,1)} %b_new_ref.1, bf16[1,128,128]{2,1,0:T(8,128)(2,1)} %b_old_ref.1), custom_call_target="tpu_custom_call" | custom-call | tf_op jit(solution)/shard_map/block/pallas_call | solution.py:189
  2.2 16.3 %collective-permute-start = (bf16[128,256]{1,0:T(8,128)(2,1)}, bf16[128,256]{1,0:T(8,128)(2,1)S(1)}, u32[]{:S(2)}, u32[]{:S(2)}) collective-permute-start(bf16[128,256]{1,0:T(8,128)(2,1)} %get-tuple-element.31), channel_id=1, source_target_pairs={{0,0},{1,129},{2,18},{3,147},{4,36},{5,165},{6,54},{7,183},{8,72},... | collective-permute-start | bytes 196616 | tf_op jit(solution)/shard_map/ppermute | solution.py:202
  18.4 1.9 %collective-permute-start.1 = (bf16[128,256]{1,0:T(8,128)(2,1)}, bf16[128,256]{1,0:T(8,128)(2,1)S(1)}, u32[]{:S(2)}, u32[]{:S(2)}) collective-permute-start(bf16[128,256]{1,0:T(8,128)(2,1)} %get-tuple-element.32), channel_id=1, source_target_pairs={{0,0},{1,129},{2,242},{3,115},{4,228},{5,101},{6,214},{7,87},{8,20... | collective-permute-start | bytes 196616 | tf_op jit(solution)/shard_map/ppermute | solution.py:203
  20.4 2.1 %all-gather = bf16[256,256]{1,0:T(8,128)(2,1)S(1)} all-gather(bf16[128,256]{1,0:T(8,128)(2,1)} %param.7), channel_id=2, replica_groups={{0,1},{2,3},{4,5},{6,7},{8,9},{10,11},{12,13},{14,15},{16,17},{18,19},{..., dimensions={0}, use_global_device_ids=true | all-gather | bytes 196608 | tf_op jit(solution)/shard_map/all_gather | solution.py:205
  22.5 2.1 %collective-permute-start.5 = (bf16[4096,256]{1,0:T(8,128)(2,1)}, bf16[4096,256]{1,0:T(8,128)(2,1)}, u32[]{:S(2)}, u32[]{:S(2)}) collective-permute-start(bf16[4096,256]{1,0:T(8,128)(2,1)} %bitcast.32), channel_id=1, source_target_pairs={{0,1},{1,0},{2,3},{3,2},{4,5},{5,4},{6,7},{7,6},{8,9},{9,8},{10,11... | collective-permute-start | bytes 6291464 | tf_op jit(solution)/shard_map/ppermute | solution.py:207
  24.6 7.8 %collective-permute-done.1 = bf16[128,256]{1,0:T(8,128)(2,1)S(1)} collective-permute-done((bf16[128,256]{1,0:T(8,128)(2,1)}, bf16[128,256]{1,0:T(8,128)(2,1)S(1)}, u32[]{:S(2)}, u32[]{:S(2)}) %collective-permute-start.1) | collective-permute-done | bytes 65568 | tf_op jit(solution)/shard_map/ppermute | solution.py:203
  32.4 1.1 broadcast_in_dim.41
  33.5 5.1 %all-to-all-start = ((bf16[16,128,256]{2,1,0:T(8,128)(2,1)}), bf16[16,128,256]{2,1,0:T(8,128)(2,1)S(1)}, u32[]{:S(2)}, u32[]{:S(2)}) async-start(bf16[16,128,256]{2,1,0:T(8,128)(2,1)} %broadcast_in_dim.41), calls=%async_computation | async-start | bytes 2097152 | tf_op jit(solution)/shard_map/all_to_all | solution.py:214
  38.5 5.1 %collective-permute-start.3 = (bf16[128,256]{1,0:T(8,128)(2,1)S(1)}, bf16[128,256]{1,0:T(8,128)(2,1)S(1)}, u32[]{:S(2)}, u32[]{:S(2)}) collective-permute-start(bf16[128,256]{1,0:T(8,128)(2,1)S(1)} %collective-permute-done.1), channel_id=1, source_target_pairs={{0,256},{2,257},{4,0},{6,1},{8,258},{10,259},{12,2},{14,3},{1,260}... | collective-permute-start | bytes 196616 | tf_op jit(solution)/shard_map/ppermute | solution.py:213
  43.6 1.9 %collective-permute-start.2 = (bf16[128,256]{1,0:T(8,128)(2,1)S(1)}, bf16[128,256]{1,0:T(8,128)(2,1)S(1)}, u32[]{:S(2)}, u32[]{:S(2)}) collective-permute-start(bf16[128,256]{1,0:T(8,128)(2,1)S(1)} %collective-permute-done.1), channel_id=1, source_target_pairs={{0,0},{2,1},{4,256},{6,257},{8,2},{10,3},{12,258},{14,259},{1,4},{... | collective-permute-start | bytes 196616 | tf_op jit(solution)/shard_map/ppermute | solution.py:213
  45.5 7.0 %collective-permute-done.3 = bf16[128,256]{1,0:T(8,128)(2,1)S(1)} collective-permute-done((bf16[128,256]{1,0:T(8,128)(2,1)S(1)}, bf16[128,256]{1,0:T(8,128)(2,1)S(1)}, u32[]{:S(2)}, u32[]{:S(2)}) %collective-permute-start.3) | collective-permute-done | bytes 65568 | tf_op jit(solution)/shard_map/ppermute | solution.py:213
  52.5 1.1 collective-permute-done.2
  53.6 4.4 %all-to-all-done.own_ref = bf16[16,128,256]{2,1,0:T(8,128)(2,1)S(1)} async-done(((bf16[16,128,256]{2,1,0:T(8,128)(2,1)}), bf16[16,128,256]{2,1,0:T(8,128)(2,1)S(1)}, u32[]{:S(2)}, u32[]{:S(2)}) %all-to-all-start) | async-done | bytes 1048608 | tf_op jit(solution)/shard_map/all_to_all | solution.py:214
  58.0 2.3 %collective-permute-start.4 = (bf16[16,128,256]{2,1,0:T(8,128)(2,1)S(1)}, bf16[16,128,256]{2,1,0:T(8,128)(2,1)S(1)}, u32[]{:S(2)}, u32[]{:S(2)}) collective-permute-start(bf16[16,128,256]{2,1,0:T(8,128)(2,1)S(1)} %all-to-all-done.own_ref), channel_id=1, source_target_pairs={{0,1},{1,0},{2,3},{3,2},{4,5},{5,4},{6,7},{7,6},{8,9},{9,8},{10,11... | collective-permute-start | bytes 3145736 | tf_op jit(solution)/shard_map/ppermute | solution.py:217
  60.2 0.8 broadcast_in_dim.43
  61.1 4.1 %all-to-all-start.1 = ((bf16[8,128,256]{2,1,0:T(8,128)(2,1)}), bf16[8,128,256]{2,1,0:T(8,128)(2,1)S(1)}, u32[]{:S(2)}, u32[]{:S(2)}) async-start(bf16[8,128,256]{2,1,0:T(8,128)(2,1)} %broadcast_in_dim.43), calls=%async_computation.1 | async-start | bytes 1048576 | tf_op jit(solution)/shard_map/all_to_all | solution.py:50
  65.2 0.1 pad_add_fusion.place_ref
  65.3 2.2 %all-gather.1 = bf16[4,128,256]{2,1,0:T(8,128)(2,1)S(1)} all-gather(bf16[2,128,256]{2,1,0:T(8,128)(2,1)S(1)} %pad_maximum_fusion), channel_id=3, replica_groups={{0,1},{2,3},{4,5},{6,7},{8,9},{10,11},{12,13},{14,15},{16,17},{18,19},{..., dimensions={0}, use_global_device_ids=true | all-gather | bytes 393216 | tf_op jit(solution)/shard_map/all_gather | solution.py:218
  67.5 0.0 collective-permute-done.5.mate_ref
  67.5 0.0 collective-permute-done.4.other_ref
  67.5 5.6 %merge.1 = (bf16[16,256,512]{2,1,0:T(8,128)(2,1)}, bf16[4096,256]{1,0:T(8,128)(2,1)}) custom-call(s32[3]{0:T(128)S(1)} %pad_add_fusion.place_ref, bf16[16,128,256]{2,1,0:T(8,128)(2,1)S(1)} %all-to-all-done.own_ref, bf16[16,128,256]{2,1,0:T(8,128)(2,1)S(1)} %collective-permute-done.4.other_ref, bf16[2,2,128,256]{3,2,1,0:T(8,128)(2,1)S(1)} %bitcast.19, ...), custom_call_target="tpu_custom_call" | custom-call | tf_op jit(solution)/shard_map/merge/pallas_call | solution.py:221
  73.1 3.8 %all-to-all-done.1.x_ref = bf16[8,128,256]{2,1,0:T(8,128)(2,1)S(1)} async-done(((bf16[8,128,256]{2,1,0:T(8,128)(2,1)}), bf16[8,128,256]{2,1,0:T(8,128)(2,1)S(1)}, u32[]{:S(2)}, u32[]{:S(2)}) %all-to-all-start.1) | async-done | bytes 524320 | tf_op jit(solution)/shard_map/all_to_all | solution.py:50
  76.9 2.4 %first.1 = (bf16[2,64,256]{2,1,0:T(8,128)(2,1)S(1)}, bf16[64,256]{1,0:T(8,128)(2,1)S(1)}, bf16[16,256,512]{2,1,0:T(8,128)(2,1)S(1)}) custom-call(bf16[8,128,256]{2,1,0:T(8,128)(2,1)S(1)} %all-to-all-done.1.x_ref, bf16[16,256,512]{2,1,0:T(8,128)(2,1)} %get-tuple-element.43.stored_ref, f32[16,1,256]{2,1,0:T(1,128)S(1)} %bitcast.24, ...), custom_call_target="tpu_custom_call" | custom-call | tf_op jit(solution)/shard_map/first/pallas_call | solution.py:247
  79.4 14.3 %all_to_all.25.x_ref = bf16[8,128,256]{2,1,0:T(8,128)(2,1)S(1)} all-to-all(bf16[8,128,256]{2,1,0:T(8,128)(2,1)S(1)} %broadcast_in_dim.45), channel_id=1, replica_groups={{0,2,4,6,8,10,12,14},{1,3,5,7,9,11,13,15},{16,18,20,22,24,26,28,30},{17..., dimensions={0} | all-to-all | bytes 1048576 | tf_op jit(solution)/shard_map/all_to_all | solution.py:50
  93.7 1.0 step.3
  94.7 12.7 %all_to_all.26.x_ref = bf16[8,128,256]{2,1,0:T(8,128)(2,1)S(1)} all-to-all(bf16[8,128,256]{2,1,0:T(8,128)(2,1)S(1)} %broadcast_in_dim.47), channel_id=1, replica_groups={{0,2,4,6,8,10,12,14},{1,3,5,7,9,11,13,15},{16,18,20,22,24,26,28,30},{17..., dimensions={0} | all-to-all | bytes 1048576 | tf_op jit(solution)/shard_map/all_to_all | solution.py:50
  107.4 1.0 step.4
  108.4 11.7 %all_to_all.27.x_ref = bf16[8,128,256]{2,1,0:T(8,128)(2,1)S(1)} all-to-all(bf16[8,128,256]{2,1,0:T(8,128)(2,1)S(1)} %broadcast_in_dim.49), channel_id=1, replica_groups={{0,2,4,6,8,10,12,14},{1,3,5,7,9,11,13,15},{16,18,20,22,24,26,28,30},{17..., dimensions={0} | all-to-all | bytes 1048576 | tf_op jit(solution)/shard_map/all_to_all | solution.py:50
  120.1 1.0 step.5
  121.1 5.2 %collective-permute-start.6 = (bf16[4,64,256]{2,1,0:T(8,128)(2,1)S(1)}, bf16[4,64,256]{2,1,0:T(8,128)(2,1)S(1)}, u32[]{:S(2)}, u32[]{:S(2)}) collective-permute-start(bf16[4,64,256]{2,1,0:T(8,128)(2,1)S(1)} %pad_maximum_fusion.1), channel_id=1, source_target_pairs={{0,1},{1,0},{2,3},{3,2},{4,5},{5,4},{6,7},{7,6},{8,9},{9,8},{10,11... | collective-permute-start | bytes 393224 | tf_op jit(solution)/shard_map/ppermute | solution.py:264
  126.3 1.0 collective-permute-done.6.swapped_ref
  127.3 0.7 finish.1
  (11 shorter events, 0.2 us)
Async XLA Ops:
  0.6 64.6 %copy-start = (f32[1,4096]{1,0:T(1,128)S(1)}, f32[1,4096]{1,0:T(1,128)}, u32[]{:S(2)}) copy-start(f32[1,4096]{1,0:T(1,128)} %param.13) | copy-start | bytes 49156
  2.2 22.4 %collective-permute-start = (bf16[128,256]{1,0:T(8,128)(2,1)}, bf16[128,256]{1,0:T(8,128)(2,1)S(1)}, u32[]{:S(2)}, u32[]{:S(2)}) collective-permute-start(bf16[128,256]{1,0:T(8,128)(2,1)} %get-tuple-element.31), channel_id=1, source_target_pairs={{0,0},{1,129},{2,18},{3,147},{4,36},{5,165},{6,54},{7,183},{8,72},... | collective-permute-start | bytes 196616 | tf_op jit(solution)/shard_map/ppermute | solution.py:202
  18.4 14.0 %collective-permute-start.1 = (bf16[128,256]{1,0:T(8,128)(2,1)}, bf16[128,256]{1,0:T(8,128)(2,1)S(1)}, u32[]{:S(2)}, u32[]{:S(2)}) collective-permute-start(bf16[128,256]{1,0:T(8,128)(2,1)} %get-tuple-element.32), channel_id=1, source_target_pairs={{0,0},{1,129},{2,242},{3,115},{4,228},{5,101},{6,214},{7,87},{8,20... | collective-permute-start | bytes 196616 | tf_op jit(solution)/shard_map/ppermute | solution.py:203
  22.5 45.0 %collective-permute-start.5 = (bf16[4096,256]{1,0:T(8,128)(2,1)}, bf16[4096,256]{1,0:T(8,128)(2,1)}, u32[]{:S(2)}, u32[]{:S(2)}) collective-permute-start(bf16[4096,256]{1,0:T(8,128)(2,1)} %bitcast.32), channel_id=1, source_target_pairs={{0,1},{1,0},{2,3},{3,2},{4,5},{5,4},{6,7},{7,6},{8,9},{9,8},{10,11... | collective-permute-start | bytes 6291464 | tf_op jit(solution)/shard_map/ppermute | solution.py:207
  33.5 24.5 %all-to-all-start = ((bf16[16,128,256]{2,1,0:T(8,128)(2,1)}), bf16[16,128,256]{2,1,0:T(8,128)(2,1)S(1)}, u32[]{:S(2)}, u32[]{:S(2)}) async-start(bf16[16,128,256]{2,1,0:T(8,128)(2,1)} %broadcast_in_dim.41), calls=%async_computation | async-start | bytes 2097152 | tf_op jit(solution)/shard_map/all_to_all | solution.py:214
  38.5 14.0 %collective-permute-start.3 = (bf16[128,256]{1,0:T(8,128)(2,1)S(1)}, bf16[128,256]{1,0:T(8,128)(2,1)S(1)}, u32[]{:S(2)}, u32[]{:S(2)}) collective-permute-start(bf16[128,256]{1,0:T(8,128)(2,1)S(1)} %collective-permute-done.1), channel_id=1, source_target_pairs={{0,256},{2,257},{4,0},{6,1},{8,258},{10,259},{12,2},{14,3},{1,260}... | collective-permute-start | bytes 196616 | tf_op jit(solution)/shard_map/ppermute | solution.py:213
  43.6 10.0 %collective-permute-start.2 = (bf16[128,256]{1,0:T(8,128)(2,1)S(1)}, bf16[128,256]{1,0:T(8,128)(2,1)S(1)}, u32[]{:S(2)}, u32[]{:S(2)}) collective-permute-start(bf16[128,256]{1,0:T(8,128)(2,1)S(1)} %collective-permute-done.1), channel_id=1, source_target_pairs={{0,0},{2,1},{4,256},{6,257},{8,2},{10,3},{12,258},{14,259},{1,4},{... | collective-permute-start | bytes 196616 | tf_op jit(solution)/shard_map/ppermute | solution.py:213
  58.0 9.6 %collective-permute-start.4 = (bf16[16,128,256]{2,1,0:T(8,128)(2,1)S(1)}, bf16[16,128,256]{2,1,0:T(8,128)(2,1)S(1)}, u32[]{:S(2)}, u32[]{:S(2)}) collective-permute-start(bf16[16,128,256]{2,1,0:T(8,128)(2,1)S(1)} %all-to-all-done.own_ref), channel_id=1, source_target_pairs={{0,1},{1,0},{2,3},{3,2},{4,5},{5,4},{6,7},{7,6},{8,9},{9,8},{10,11... | collective-permute-start | bytes 3145736 | tf_op jit(solution)/shard_map/ppermute | solution.py:217
  61.1 15.8 %all-to-all-start.1 = ((bf16[8,128,256]{2,1,0:T(8,128)(2,1)}), bf16[8,128,256]{2,1,0:T(8,128)(2,1)S(1)}, u32[]{:S(2)}, u32[]{:S(2)}) async-start(bf16[8,128,256]{2,1,0:T(8,128)(2,1)} %broadcast_in_dim.43), calls=%async_computation.1 | async-start | bytes 1048576 | tf_op jit(solution)/shard_map/all_to_all | solution.py:50
  121.1 6.2 %collective-permute-start.6 = (bf16[4,64,256]{2,1,0:T(8,128)(2,1)S(1)}, bf16[4,64,256]{2,1,0:T(8,128)(2,1)S(1)}, u32[]{:S(2)}, u32[]{:S(2)}) collective-permute-start(bf16[4,64,256]{2,1,0:T(8,128)(2,1)S(1)} %pad_maximum_fusion.1), channel_id=1, source_target_pairs={{0,1},{1,0},{2,3},{3,2},{4,5},{5,4},{6,7},{7,6},{8,9},{9,8},{10,11... | collective-permute-start | bytes 393224 | tf_op jit(solution)/shard_map/ppermute | solution.py:264

commit v9 on v7

--- a/solution.py
+++ b/solution.py
@@ -75,22 +75,15 @@
 
 
 def merge_kernel(
-    place_ref, own_ref, other_ref, ups_ref, base_ref, mate_ref, weight_ref, merged_ref, up_ref, old_ref, new_ref, out_ref, in_sems, out_sems
+    place_ref, own_ref, other_ref, ups_ref, base_ref, mate_ref, weight_ref, merged_ref, up_ref, old_ref, new_ref, out_ref, turned_ref, in_sems, out_sems
 ):
     core, low, z = place_ref[0], place_ref[1], place_ref[2]
     cols = base_ref.shape[1]
-    span = 2 * cols
-    loads = []
-    for pair in range(CHIPS):
-        rows = slice(pair * span, (pair + 1) * span)
-        loads.append(
-            [
-                pltpu.make_async_copy(ref.at[rows], old_ref.at[i, rows], in_sems.at[i, pair])
-                for i, ref in enumerate((base_ref, mate_ref))
-            ]
-        )
-        for load in loads[-1]:
-            load.start()
+    loads = [
+        pltpu.make_async_copy(ref, old_ref.at[i], in_sems.at[i]) for i, ref in enumerate((base_ref, mate_ref))
+    ]
+    for load in loads:
+        load.start()
     stores = []
     for left in range(2):
         for part in range(2):
@@ -108,23 +101,24 @@
             ref[:, 16 * pair : 16 * pair + 16, :].astype(jnp.float32).reshape(16, 2, 8, cols)
             for ref in (own_ref, other_ref)
         ]
-        for load in loads[pair]:
-            load.wait()
         for right in range(2):
             down = jnp.concatenate([part[:, right].reshape(128, cols) for part in parts], 0)
-            down = down.astype(jnp.bfloat16).T
-            delta = lax.dot_general(down, up, (((1,), (1,)), ((), ())), preferred_element_type=jnp.float32)
-            t = 2 * pair + right
+            turned_ref[2 * pair + right] = down.astype(jnp.bfloat16).T
+    for load in loads:
+        load.wait()
+    for quarter in range(4):
+        for t in range(4 * quarter, 4 * quarter + 4):
+            delta = lax.dot_general(turned_ref[t], up, (((1,), (1,)), ((), ())), preferred_element_type=jnp.float32)
             rows = slice(t * cols, (t + 1) * cols)
             mine = (old_ref[0, rows, :].astype(jnp.float32) + delta[:, :cols]).astype(jnp.bfloat16)
             theirs = (old_ref[1, rows, :].astype(jnp.float32) + delta[:, cols:]).astype(jnp.bfloat16)
             new_ref[rows, :] = mine
-            which = 2 * pair + lax.rem(right + core, 2)
+            which = t // 2 * 2 + lax.rem(t + core, 2)
             out_ref[which, :, :cols] = mine
             out_ref[which, :, cols:] = theirs
-        rows, both = slice(pair * span, (pair + 1) * span), slice(2 * pair, 2 * pair + 2)
-        stores.append(pltpu.make_async_copy(new_ref.at[rows], merged_ref.at[rows], out_sems.at[0, pair]))
-        stores.append(pltpu.make_async_copy(out_ref.at[both], weight_ref.at[both], out_sems.at[1, pair]))
+        rows, blocks = slice(4 * quarter * cols, (4 * quarter + 4) * cols), slice(4 * quarter, 4 * quarter + 4)
+        stores.append(pltpu.make_async_copy(new_ref.at[rows], merged_ref.at[rows], out_sems.at[0, quarter]))
+        stores.append(pltpu.make_async_copy(out_ref.at[blocks], weight_ref.at[blocks], out_sems.at[1, quarter]))
         for store in stores[-2:]:
             store.start()
     for store in stores:
@@ -204,10 +198,11 @@
     block = lax.ppermute(block, ("fsdp", "tp"), SHIFTED)
 
     both = lax.all_gather(tokens, "tp", axis=0, axis_index_groups=PAIRS)
-    both, base = lax.optimization_barrier((both, base_weight[0]))
-    mate = lax.ppermute(base, "tp", SWAP)
     both = lax.dynamic_slice_in_dim(both, core * half, half, 1)
     stream = jnp.where(core == 0, both, both[::-1])
+    copies = jnp.broadcast_to(stream.reshape(1, rows, cols), (CHIPS, rows, cols))
+    copies, base = lax.optimization_barrier((copies, base_weight[0]))
+    mate = lax.ppermute(base, "tp", SWAP)
 
     size = block.shape[0] // 2
     down, up = pl.pallas_call(
@@ -221,11 +216,11 @@
         name="split",
         compiler_params=ROOM,
     )(block)
-    down, up, stream = lax.optimization_barrier((down, up, stream))
+    down, up = lax.optimization_barrier((down, up))
     ups = [lax.ppermute(up, ("fsdp", "tp"), relay(part)) for part in range(2)]
     own = lax.all_to_all(down, ("fsdp", "tp"), 0, 0, axis_index_groups=PLANES)
-    own, stream, *ups = lax.optimization_barrier((own, stream, *ups))
-    x = spread(jnp.broadcast_to(stream.reshape(1, rows, cols), (CHIPS, rows, cols)))
+    own, copies, *ups = lax.optimization_barrier((own, copies, *ups))
+    x = spread(copies)
     other = lax.ppermute(own, "tp", SWAP)
     ups = lax.all_gather(jnp.stack(ups), "tp", axis=0, axis_index_groups=PAIRS)
     f = lax.axis_index("fsdp")
@@ -243,8 +238,9 @@
             pltpu.VMEM((2, tp * cols, cols), jnp.bfloat16),
             pltpu.VMEM((tp * cols, cols), jnp.bfloat16),
             pltpu.VMEM((tp, cols, 2 * cols), jnp.bfloat16),
-            pltpu.SemaphoreType.DMA((2, CHIPS)),
-            pltpu.SemaphoreType.DMA((2, CHIPS)),
+            pltpu.VMEM((tp, cols, cols), jnp.bfloat16),
+            pltpu.SemaphoreType.DMA((2,)),
+            pltpu.SemaphoreType.DMA((2, 4)),
         ],
         name="merge",
         compiler_params=WIDE,

time: 121 us -> 120 us (level)
  no operation moved by 1% of the time
where the time goes in v9:
time: 120 us
  blocking collectives  43.2 us (36%)
  starting transfers between devices  42.7 us (36%)
  waiting for transfers between devices  17 us (14%)
  Pallas kernels  14.7 us (12%)
    all_to_all x3, blocking collectives, spread(): return lax.all_to_all(blocks, 'tp', 0, 0, axis_index_groups=GROUPS)  38.9 us
    ppermute x1, starting transfers between devices, shards(): block = lax.ppermute(block, ('fsdp', 'tp'), SHIFTED)  16.3 us
    ppermute x2, waiting for transfers between devices, shards(): ups = [lax.ppermute(up, ('fsdp', 'tp'), relay(part)) for part in range(2)]  12.6 us
    all_to_all x1, starting transfers between devices, shards(): own = lax.all_to_all(down, ('fsdp', 'tp'), 0, 0, axis_index_groups=PLANES)  8.76 us
    pallas_call x1, Pallas kernels, shards(): pl.pallas_call(merge_kernel, out_shape=(jax.ShapeDtypeStruct((tp, cols, 2...  6 us
    pallas_call x4, Pallas kernels, shards(): pl.pallas_call(step_kernel if step else first_kernel, out_shape=(jax.Shap...  5.37 us
    ppermute x1, starting transfers between devices, shards(): swapped = lax.ppermute(jnp.stack(gives), 'tp', SWAP)  5.21 us
    ppermute x2, starting transfers between devices, shards(): ups = [lax.ppermute(up, ('fsdp', 'tp'), relay(part)) for part in range(2)]  5 us
  transfers between devices with their start and end apart: 8, of which 4 were waited for; matrix products, arithmetic and copies ran while one was open for 1% of the time, Pallas kernels for 6%

profile of v9, /device:TPU:1, one launch (start us, length us, event | category | flops | bytes accessed | tf_op | source)
XLA Modules:
  0.0 119.5 jit_solution(631042991397362281)
XLA Ops:
  0.6 0.0 copy-start
  0.6 1.5 %block.1 = bf16[256,256]{1,0:T(8,128)(2,1)} custom-call(bf16[1,4,4096]{2,1,0:T(4,128)(2,1)} %a_new_ref.1, bf16[1,4,4096]{2,1,0:T(4,128)(2,1)} %a_old_ref.1, bf16[1,128,128]{2,1,0:T(8,128)(2,1)} %b_new_ref.1, bf16[1,128,128]{2,1,0:T(8,128)(2,1)} %b_old_ref.1), custom_call_target="tpu_custom_call" | custom-call | tf_op jit(solution)/shard_map/block/pallas_call | solution.py:185
  2.2 16.3 %collective-permute-start = (bf16[256,256]{1,0:T(8,128)(2,1)}, bf16[256,256]{1,0:T(8,128)(2,1)S(1)}, u32[]{:S(2)}, u32[]{:S(2)}) collective-permute-start(bf16[256,256]{1,0:T(8,128)(2,1)} %block.1), channel_id=1, source_target_pairs={{0,0},{1,129},{2,18},{3,147},{4,36},{5,165},{6,54},{7,183},{8,72},... | collective-permute-start | bytes 393224 | tf_op jit(solution)/shard_map/ppermute | solution.py:198
  18.5 2.1 %all-gather = bf16[256,256]{1,0:T(8,128)(2,1)S(1)} all-gather(bf16[128,256]{1,0:T(8,128)(2,1)} %param.7), channel_id=2, replica_groups={{0,1},{2,3},{4,5},{6,7},{8,9},{10,11},{12,13},{14,15},{16,17},{18,19},{..., dimensions={0}, use_global_device_ids=true | all-gather | bytes 196608 | tf_op jit(solution)/shard_map/all_gather | solution.py:200
  20.6 0.8 broadcast_in_dim.36
  21.4 2.1 %collective-permute-start.4 = (bf16[4096,256]{1,0:T(8,128)(2,1)}, bf16[4096,256]{1,0:T(8,128)(2,1)}, u32[]{:S(2)}, u32[]{:S(2)}) collective-permute-start(bf16[4096,256]{1,0:T(8,128)(2,1)} %bitcast.32), channel_id=1, source_target_pairs={{0,1},{1,0},{2,3},{3,2},{4,5},{5,4},{6,7},{7,6},{8,9},{9,8},{10,11... | collective-permute-start | bytes 6291464 | tf_op jit(solution)/shard_map/ppermute | solution.py:205
  23.5 0.0 collective-permute-done.block_ref
  23.5 1.0 split.1
  24.6 8.8 %all-to-all-start = ((bf16[16,128,256]{2,1,0:T(8,128)(2,1)}), bf16[16,128,256]{2,1,0:T(8,128)(2,1)S(1)}, u32[]{:S(2)}, u32[]{:S(2)}) async-start(bf16[16,128,256]{2,1,0:T(8,128)(2,1)} %get-tuple-element.26), calls=%async_computation | async-start | bytes 2097152 | tf_op jit(solution)/shard_map/all_to_all | solution.py:221
  33.3 2.8 %collective-permute-start.2 = (bf16[128,256]{1,0:T(8,128)(2,1)S(1)}, bf16[128,256]{1,0:T(8,128)(2,1)S(1)}, u32[]{:S(2)}, u32[]{:S(2)}) collective-permute-start(bf16[128,256]{1,0:T(8,128)(2,1)S(1)} %get-tuple-element.29), channel_id=1, source_target_pairs={{0,256},{15,257},{13,0},{11,1},{9,258},{7,259},{5,2},{3,3},{1,260}... | collective-permute-start | bytes 196616 | tf_op jit(solution)/shard_map/ppermute | solution.py:220
  36.2 2.2 %collective-permute-start.1 = (bf16[128,256]{1,0:T(8,128)(2,1)S(1)}, bf16[128,256]{1,0:T(8,128)(2,1)S(1)}, u32[]{:S(2)}, u32[]{:S(2)}) collective-permute-start(bf16[128,256]{1,0:T(8,128)(2,1)S(1)} %get-tuple-element.29), channel_id=1, source_target_pairs={{0,0},{15,1},{13,256},{11,257},{9,2},{7,3},{5,258},{3,259},{1,4},{... | collective-permute-start | bytes 196616 | tf_op jit(solution)/shard_map/ppermute | solution.py:220
  38.3 9.4 %collective-permute-done.2 = bf16[128,256]{1,0:T(8,128)(2,1)S(1)} collective-permute-done((bf16[128,256]{1,0:T(8,128)(2,1)S(1)}, bf16[128,256]{1,0:T(8,128)(2,1)S(1)}, u32[]{:S(2)}, u32[]{:S(2)}) %collective-permute-start.2) | collective-permute-done | bytes 65568 | tf_op jit(solution)/shard_map/ppermute | solution.py:220
  47.7 3.3 %collective-permute-done.1 = bf16[128,256]{1,0:T(8,128)(2,1)S(1)} collective-permute-done((bf16[128,256]{1,0:T(8,128)(2,1)S(1)}, bf16[128,256]{1,0:T(8,128)(2,1)S(1)}, u32[]{:S(2)}, u32[]{:S(2)}) %collective-permute-start.1) | collective-permute-done | bytes 65568 | tf_op jit(solution)/shard_map/ppermute | solution.py:220
  51.0 0.0 all-to-all-done.own_ref
  51.0 1.9 %collective-permute-start.3 = (bf16[16,128,256]{2,1,0:T(8,128)(2,1)S(1)}, bf16[16,128,256]{2,1,0:T(8,128)(2,1)S(1)}, u32[]{:S(2)}, u32[]{:S(2)}) collective-permute-start(bf16[16,128,256]{2,1,0:T(8,128)(2,1)S(1)} %all-to-all-done.own_ref), channel_id=1, source_target_pairs={{0,1},{1,0},{2,3},{3,2},{4,5},{5,4},{6,7},{7,6},{8,9},{9,8},{10,11... | collective-permute-start | bytes 3145736 | tf_op jit(solution)/shard_map/ppermute | solution.py:224
  52.9 3.5 %all-to-all-start.1 = ((bf16[8,128,256]{2,1,0:T(8,128)(2,1)}), bf16[8,128,256]{2,1,0:T(8,128)(2,1)S(1)}, u32[]{:S(2)}, u32[]{:S(2)}) async-start(bf16[8,128,256]{2,1,0:T(8,128)(2,1)} %broadcast_in_dim.36), calls=%async_computation.1 | async-start | bytes 1048576 | tf_op jit(solution)/shard_map/all_to_all | solution.py:46
  56.4 0.1 pad_add_fusion.place_ref
  56.5 2.1 %all-gather.1 = bf16[4,128,256]{2,1,0:T(8,128)(2,1)S(1)} all-gather(bf16[2,128,256]{2,1,0:T(8,128)(2,1)S(1)} %pad_maximum_fusion), channel_id=3, replica_groups={{0,1},{2,3},{4,5},{6,7},{8,9},{10,11},{12,13},{14,15},{16,17},{18,19},{..., dimensions={0}, use_global_device_ids=true | all-gather | bytes 393216 | tf_op jit(solution)/shard_map/all_gather | solution.py:225
  58.7 0.0 collective-permute-done.4.mate_ref
  58.7 0.0 collective-permute-done.3.other_ref
  58.7 6.0 %merge.1 = (bf16[16,256,512]{2,1,0:T(8,128)(2,1)}, bf16[4096,256]{1,0:T(8,128)(2,1)}) custom-call(s32[3]{0:T(128)S(1)} %pad_add_fusion.place_ref, bf16[16,128,256]{2,1,0:T(8,128)(2,1)S(1)} %all-to-all-done.own_ref, bf16[16,128,256]{2,1,0:T(8,128)(2,1)S(1)} %collective-permute-done.3.other_ref, bf16[2,2,128,256]{3,2,1,0:T(8,128)(2,1)S(1)} %bitcast.19, ...), custom_call_target="tpu_custom_call" | custom-call | tf_op jit(solution)/shard_map/merge/pallas_call | solution.py:228
  64.7 3.4 %all-to-all-done.1.x_ref = bf16[8,128,256]{2,1,0:T(8,128)(2,1)S(1)} async-done(((bf16[8,128,256]{2,1,0:T(8,128)(2,1)}), bf16[8,128,256]{2,1,0:T(8,128)(2,1)S(1)}, u32[]{:S(2)}, u32[]{:S(2)}) %all-to-all-start.1) | async-done | bytes 524320 | tf_op jit(solution)/shard_map/all_to_all | solution.py:46
  68.1 2.4 %first.1 = (bf16[2,64,256]{2,1,0:T(8,128)(2,1)S(1)}, bf16[64,256]{1,0:T(8,128)(2,1)S(1)}, bf16[16,256,512]{2,1,0:T(8,128)(2,1)S(1)}) custom-call(bf16[8,128,256]{2,1,0:T(8,128)(2,1)S(1)} %all-to-all-done.1.x_ref, bf16[16,256,512]{2,1,0:T(8,128)(2,1)} %get-tuple-element.35.stored_ref, f32[16,1,256]{2,1,0:T(1,128)S(1)} %bitcast.24, ...), custom_call_target="tpu_custom_call" | custom-call | tf_op jit(solution)/shard_map/first/pallas_call | solution.py:255
  70.6 14.6 %all_to_all.25.x_ref = bf16[8,128,256]{2,1,0:T(8,128)(2,1)S(1)} all-to-all(bf16[8,128,256]{2,1,0:T(8,128)(2,1)S(1)} %broadcast_in_dim.38), channel_id=1, replica_groups={{0,2,4,6,8,10,12,14},{1,3,5,7,9,11,13,15},{16,18,20,22,24,26,28,30},{17..., dimensions={0} | all-to-all | bytes 1048576 | tf_op jit(solution)/shard_map/all_to_all | solution.py:46
  85.2 1.0 step.3
  86.2 12.7 %all_to_all.26.x_ref = bf16[8,128,256]{2,1,0:T(8,128)(2,1)S(1)} all-to-all(bf16[8,128,256]{2,1,0:T(8,128)(2,1)S(1)} %broadcast_in_dim.40), channel_id=1, replica_groups={{0,2,4,6,8,10,12,14},{1,3,5,7,9,11,13,15},{16,18,20,22,24,26,28,30},{17..., dimensions={0} | all-to-all | bytes 1048576 | tf_op jit(solution)/shard_map/all_to_all | solution.py:46
  98.8 1.0 step.4
  99.9 11.7 %all_to_all.27.x_ref = bf16[8,128,256]{2,1,0:T(8,128)(2,1)S(1)} all-to-all(bf16[8,128,256]{2,1,0:T(8,128)(2,1)S(1)} %broadcast_in_dim.42), channel_id=1, replica_groups={{0,2,4,6,8,10,12,14},{1,3,5,7,9,11,13,15},{16,18,20,22,24,26,28,30},{17..., dimensions={0} | all-to-all | bytes 1048576 | tf_op jit(solution)/shard_map/all_to_all | solution.py:46
  111.6 1.0 step.5
  112.6 5.2 %collective-permute-start.5 = (bf16[4,64,256]{2,1,0:T(8,128)(2,1)S(1)}, bf16[4,64,256]{2,1,0:T(8,128)(2,1)S(1)}, u32[]{:S(2)}, u32[]{:S(2)}) collective-permute-start(bf16[4,64,256]{2,1,0:T(8,128)(2,1)S(1)} %pad_maximum_fusion.1), channel_id=1, source_target_pairs={{0,1},{1,0},{2,3},{3,2},{4,5},{5,4},{6,7},{7,6},{8,9},{9,8},{10,11... | collective-permute-start | bytes 393224 | tf_op jit(solution)/shard_map/ppermute | solution.py:272
  117.8 1.0 collective-permute-done.5.swapped_ref
  118.8 0.7 finish.1
  (9 shorter events, 0.2 us)
Async XLA Ops:
  0.6 55.9 %copy-start = (f32[1,4096]{1,0:T(1,128)S(1)}, f32[1,4096]{1,0:T(1,128)}, u32[]{:S(2)}) copy-start(f32[1,4096]{1,0:T(1,128)} %param.13) | copy-start | bytes 49156
  2.2 21.3 %collective-permute-start = (bf16[256,256]{1,0:T(8,128)(2,1)}, bf16[256,256]{1,0:T(8,128)(2,1)S(1)}, u32[]{:S(2)}, u32[]{:S(2)}) collective-permute-start(bf16[256,256]{1,0:T(8,128)(2,1)} %block.1), channel_id=1, source_target_pairs={{0,0},{1,129},{2,18},{3,147},{4,36},{5,165},{6,54},{7,183},{8,72},... | collective-permute-start | bytes 393224 | tf_op jit(solution)/shard_map/ppermute | solution.py:198
  21.4 37.2 %collective-permute-start.4 = (bf16[4096,256]{1,0:T(8,128)(2,1)}, bf16[4096,256]{1,0:T(8,128)(2,1)}, u32[]{:S(2)}, u32[]{:S(2)}) collective-permute-start(bf16[4096,256]{1,0:T(8,128)(2,1)} %bitcast.32), channel_id=1, source_target_pairs={{0,1},{1,0},{2,3},{3,2},{4,5},{5,4},{6,7},{7,6},{8,9},{9,8},{10,11... | collective-permute-start | bytes 6291464 | tf_op jit(solution)/shard_map/ppermute | solution.py:205
  24.6 26.4 %all-to-all-start = ((bf16[16,128,256]{2,1,0:T(8,128)(2,1)}), bf16[16,128,256]{2,1,0:T(8,128)(2,1)S(1)}, u32[]{:S(2)}, u32[]{:S(2)}) async-start(bf16[16,128,256]{2,1,0:T(8,128)(2,1)} %get-tuple-element.26), calls=%async_computation | async-start | bytes 2097152 | tf_op jit(solution)/shard_map/all_to_all | solution.py:221
  33.3 14.4 %collective-permute-start.2 = (bf16[128,256]{1,0:T(8,128)(2,1)S(1)}, bf16[128,256]{1,0:T(8,128)(2,1)S(1)}, u32[]{:S(2)}, u32[]{:S(2)}) collective-permute-start(bf16[128,256]{1,0:T(8,128)(2,1)S(1)} %get-tuple-element.29), channel_id=1, source_target_pairs={{0,256},{15,257},{13,0},{11,1},{9,258},{7,259},{5,2},{3,3},{1,260}... | collective-permute-start | bytes 196616 | tf_op jit(solution)/shard_map/ppermute | solution.py:220
  36.2 14.8 %collective-permute-start.1 = (bf16[128,256]{1,0:T(8,128)(2,1)S(1)}, bf16[128,256]{1,0:T(8,128)(2,1)S(1)}, u32[]{:S(2)}, u32[]{:S(2)}) collective-permute-start(bf16[128,256]{1,0:T(8,128)(2,1)S(1)} %get-tuple-element.29), channel_id=1, source_target_pairs={{0,0},{15,1},{13,256},{11,257},{9,2},{7,3},{5,258},{3,259},{1,4},{... | collective-permute-start | bytes 196616 | tf_op jit(solution)/shard_map/ppermute | solution.py:220
  51.0 7.7 %collective-permute-start.3 = (bf16[16,128,256]{2,1,0:T(8,128)(2,1)S(1)}, bf16[16,128,256]{2,1,0:T(8,128)(2,1)S(1)}, u32[]{:S(2)}, u32[]{:S(2)}) collective-permute-start(bf16[16,128,256]{2,1,0:T(8,128)(2,1)S(1)} %all-to-all-done.own_ref), channel_id=1, source_target_pairs={{0,1},{1,0},{2,3},{3,2},{4,5},{5,4},{6,7},{7,6},{8,9},{9,8},{10,11... | collective-permute-start | bytes 3145736 | tf_op jit(solution)/shard_map/ppermute | solution.py:224
  52.9 15.2 %all-to-all-start.1 = ((bf16[8,128,256]{2,1,0:T(8,128)(2,1)}), bf16[8,128,256]{2,1,0:T(8,128)(2,1)S(1)}, u32[]{:S(2)}, u32[]{:S(2)}) async-start(bf16[8,128,256]{2,1,0:T(8,128)(2,1)} %broadcast_in_dim.36), calls=%async_computation.1 | async-start | bytes 1048576 | tf_op jit(solution)/shard_map/all_to_all | solution.py:46
  112.6 6.2 %collective-permute-start.5 = (bf16[4,64,256]{2,1,0:T(8,128)(2,1)S(1)}, bf16[4,64,256]{2,1,0:T(8,128)(2,1)S(1)}, u32[]{:S(2)}, u32[]{:S(2)}) collective-permute-start(bf16[4,64,256]{2,1,0:T(8,128)(2,1)S(1)} %pad_maximum_fusion.1), channel_id=1, source_target_pairs={{0,1},{1,0},{2,3},{3,2},{4,5},{5,4},{6,7},{7,6},{8,9},{9,8},{10,11... | collective-permute-start | bytes 393224 | tf_op jit(solution)/shard_map/ppermute | solution.py:272

commit v10 on v7

--- a/solution.py
+++ b/solution.py
@@ -140,11 +140,11 @@
         squares += part(i) * part(i)
     mean = jnp.sum(squares, axis=1, keepdims=True) / (blocks * cols)
     scale = lax.rsqrt(mean + 1e-06)
+    normed = [(part(i) * scale * gain_ref[i]).astype(jnp.bfloat16) for i in range(blocks)]
     total = jnp.zeros((rows, 2 * cols), jnp.float32)
     for i in range(blocks):
-        normed = (part(i) * scale * gain_ref[i]).astype(jnp.bfloat16)
         arrive(i)
-        total += jnp.dot(normed, weight_ref[i], preferred_element_type=jnp.float32)
+        total += jnp.dot(normed[i], weight_ref[i], preferred_element_type=jnp.float32)
     for half in range(2):
         branch = total[:, half * cols : (half + 1) * cols]
         out_ref[half] = (mine_ref[half].astype(jnp.float32) + branch).astype(jnp.bfloat16)
@@ -204,10 +204,11 @@
     block = lax.ppermute(block, ("fsdp", "tp"), SHIFTED)
 
     both = lax.all_gather(tokens, "tp", axis=0, axis_index_groups=PAIRS)
-    both, base = lax.optimization_barrier((both, base_weight[0]))
-    mate = lax.ppermute(base, "tp", SWAP)
     both = lax.dynamic_slice_in_dim(both, core * half, half, 1)
     stream = jnp.where(core == 0, both, both[::-1])
+    copies = jnp.broadcast_to(stream.reshape(1, rows, cols), (CHIPS, rows, cols))
+    copies, base = lax.optimization_barrier((copies, base_weight[0]))
+    mate = lax.ppermute(base, "tp", SWAP)
 
     size = block.shape[0] // 2
     down, up = pl.pallas_call(
@@ -221,11 +222,11 @@
         name="split",
         compiler_params=ROOM,
     )(block)
-    down, up, stream = lax.optimization_barrier((down, up, stream))
+    down, up = lax.optimization_barrier((down, up))
     ups = [lax.ppermute(up, ("fsdp", "tp"), relay(part)) for part in range(2)]
     own = lax.all_to_all(down, ("fsdp", "tp"), 0, 0, axis_index_groups=PLANES)
-    own, stream, *ups = lax.optimization_barrier((own, stream, *ups))
-    x = spread(jnp.broadcast_to(stream.reshape(1, rows, cols), (CHIPS, rows, cols)))
+    own, copies, *ups = lax.optimization_barrier((own, copies, *ups))
+    x = spread(copies)
     other = lax.ppermute(own, "tp", SWAP)
     ups = lax.all_gather(jnp.stack(ups), "tp", axis=0, axis_index_groups=PAIRS)
     f = lax.axis_index("fsdp")

time: 121 us -> 120 us (level)
  no operation moved by 1% of the time
where the time goes in v10:
time: 120 us; the launch traced here: 119 us
  blocking collectives  42.8 us (36%)
  starting transfers between devices  42.7 us (36%)
  waiting for transfers between devices  17.4 us (14%)
  Pallas kernels  14.2 us (12%)
    all_to_all x3, blocking collectives, spread(): return lax.all_to_all(blocks, 'tp', 0, 0, axis_index_groups=GROUPS)  38.5 us
    ppermute x1, starting transfers between devices, shards(): block = lax.ppermute(block, ('fsdp', 'tp'), SHIFTED)  16.3 us
    ppermute x2, waiting for transfers between devices, shards(): ups = [lax.ppermute(up, ('fsdp', 'tp'), relay(part)) for part in range(2)]  12.6 us
    all_to_all x1, starting transfers between devices, shards(): own = lax.all_to_all(down, ('fsdp', 'tp'), 0, 0, axis_index_groups=PLANES)  8.76 us
    pallas_call x1, Pallas kernels, shards(): pl.pallas_call(merge_kernel, out_shape=(jax.ShapeDtypeStruct((tp, cols, 2...  5.58 us
    pallas_call x4, Pallas kernels, shards(): pl.pallas_call(step_kernel if step else first_kernel, out_shape=(jax.Shap...  5.37 us
    ppermute x1, starting transfers between devices, shards(): swapped = lax.ppermute(jnp.stack(gives), 'tp', SWAP)  5.21 us
    ppermute x2, starting transfers between devices, shards(): ups = [lax.ppermute(up, ('fsdp', 'tp'), relay(part)) for part in range(2)]  5 us
  transfers between devices with their start and end apart: 8, of which 4 were waited for; matrix products, arithmetic and copies ran while one was open for 1% of the time, Pallas kernels for 6%

profile of v10, /device:TPU:1, one launch (start us, length us, event | category | flops | bytes accessed | tf_op | source)
XLA Modules:
  0.0 119.1 jit_solution(5362072900430953299)
XLA Ops:
  0.6 0.0 copy-start
  0.6 1.5 %block.1 = bf16[256,256]{1,0:T(8,128)(2,1)} custom-call(bf16[1,4,4096]{2,1,0:T(4,128)(2,1)} %a_new_ref.1, bf16[1,4,4096]{2,1,0:T(4,128)(2,1)} %a_old_ref.1, bf16[1,128,128]{2,1,0:T(8,128)(2,1)} %b_new_ref.1, bf16[1,128,128]{2,1,0:T(8,128)(2,1)} %b_old_ref.1), custom_call_target="tpu_custom_call" | custom-call | tf_op jit(solution)/shard_map/block/pallas_call | solution.py:191
  2.2 16.3 %collective-permute-start = (bf16[256,256]{1,0:T(8,128)(2,1)}, bf16[256,256]{1,0:T(8,128)(2,1)S(1)}, u32[]{:S(2)}, u32[]{:S(2)}) collective-permute-start(bf16[256,256]{1,0:T(8,128)(2,1)} %block.1), channel_id=1, source_target_pairs={{0,0},{1,129},{2,18},{3,147},{4,36},{5,165},{6,54},{7,183},{8,72},... | collective-permute-start | bytes 393224 | tf_op jit(solution)/shard_map/ppermute | solution.py:204
  18.5 2.1 %all-gather = bf16[256,256]{1,0:T(8,128)(2,1)S(1)} all-gather(bf16[128,256]{1,0:T(8,128)(2,1)} %param.7), channel_id=2, replica_groups={{0,1},{2,3},{4,5},{6,7},{8,9},{10,11},{12,13},{14,15},{16,17},{18,19},{..., dimensions={0}, use_global_device_ids=true | all-gather | bytes 196608 | tf_op jit(solution)/shard_map/all_gather | solution.py:206
  20.6 0.8 broadcast_in_dim.36
  21.4 2.1 %collective-permute-start.4 = (bf16[4096,256]{1,0:T(8,128)(2,1)}, bf16[4096,256]{1,0:T(8,128)(2,1)}, u32[]{:S(2)}, u32[]{:S(2)}) collective-permute-start(bf16[4096,256]{1,0:T(8,128)(2,1)} %bitcast.32), channel_id=1, source_target_pairs={{0,1},{1,0},{2,3},{3,2},{4,5},{5,4},{6,7},{7,6},{8,9},{9,8},{10,11... | collective-permute-start | bytes 6291464 | tf_op jit(solution)/shard_map/ppermute | solution.py:211
  23.5 0.0 collective-permute-done.block_ref
  23.5 1.0 split.1
  24.6 8.8 %all-to-all-start = ((bf16[16,128,256]{2,1,0:T(8,128)(2,1)}), bf16[16,128,256]{2,1,0:T(8,128)(2,1)S(1)}, u32[]{:S(2)}, u32[]{:S(2)}) async-start(bf16[16,128,256]{2,1,0:T(8,128)(2,1)} %get-tuple-element.26), calls=%async_computation | async-start | bytes 2097152 | tf_op jit(solution)/shard_map/all_to_all | solution.py:227
  33.3 2.8 %collective-permute-start.2 = (bf16[128,256]{1,0:T(8,128)(2,1)S(1)}, bf16[128,256]{1,0:T(8,128)(2,1)S(1)}, u32[]{:S(2)}, u32[]{:S(2)}) collective-permute-start(bf16[128,256]{1,0:T(8,128)(2,1)S(1)} %get-tuple-element.29), channel_id=1, source_target_pairs={{0,256},{15,257},{13,0},{11,1},{9,258},{7,259},{5,2},{3,3},{1,260}... | collective-permute-start | bytes 196616 | tf_op jit(solution)/shard_map/ppermute | solution.py:226
  36.2 2.2 %collective-permute-start.1 = (bf16[128,256]{1,0:T(8,128)(2,1)S(1)}, bf16[128,256]{1,0:T(8,128)(2,1)S(1)}, u32[]{:S(2)}, u32[]{:S(2)}) collective-permute-start(bf16[128,256]{1,0:T(8,128)(2,1)S(1)} %get-tuple-element.29), channel_id=1, source_target_pairs={{0,0},{15,1},{13,256},{11,257},{9,2},{7,3},{5,258},{3,259},{1,4},{... | collective-permute-start | bytes 196616 | tf_op jit(solution)/shard_map/ppermute | solution.py:226
  38.3 9.4 %collective-permute-done.2 = bf16[128,256]{1,0:T(8,128)(2,1)S(1)} collective-permute-done((bf16[128,256]{1,0:T(8,128)(2,1)S(1)}, bf16[128,256]{1,0:T(8,128)(2,1)S(1)}, u32[]{:S(2)}, u32[]{:S(2)}) %collective-permute-start.2) | collective-permute-done | bytes 65568 | tf_op jit(solution)/shard_map/ppermute | solution.py:226
  47.7 3.3 %collective-permute-done.1 = bf16[128,256]{1,0:T(8,128)(2,1)S(1)} collective-permute-done((bf16[128,256]{1,0:T(8,128)(2,1)S(1)}, bf16[128,256]{1,0:T(8,128)(2,1)S(1)}, u32[]{:S(2)}, u32[]{:S(2)}) %collective-permute-start.1) | collective-permute-done | bytes 65568 | tf_op jit(solution)/shard_map/ppermute | solution.py:226
  51.0 0.0 all-to-all-done.own_ref
  51.0 1.9 %collective-permute-start.3 = (bf16[16,128,256]{2,1,0:T(8,128)(2,1)S(1)}, bf16[16,128,256]{2,1,0:T(8,128)(2,1)S(1)}, u32[]{:S(2)}, u32[]{:S(2)}) collective-permute-start(bf16[16,128,256]{2,1,0:T(8,128)(2,1)S(1)} %all-to-all-done.own_ref), channel_id=1, source_target_pairs={{0,1},{1,0},{2,3},{3,2},{4,5},{5,4},{6,7},{7,6},{8,9},{9,8},{10,11... | collective-permute-start | bytes 3145736 | tf_op jit(solution)/shard_map/ppermute | solution.py:230
  52.9 3.5 %all-to-all-start.1 = ((bf16[8,128,256]{2,1,0:T(8,128)(2,1)}), bf16[8,128,256]{2,1,0:T(8,128)(2,1)S(1)}, u32[]{:S(2)}, u32[]{:S(2)}) async-start(bf16[8,128,256]{2,1,0:T(8,128)(2,1)} %broadcast_in_dim.36), calls=%async_computation.1 | async-start | bytes 1048576 | tf_op jit(solution)/shard_map/all_to_all | solution.py:46
  56.4 0.1 pad_add_fusion.place_ref
  56.5 2.1 %all-gather.1 = bf16[4,128,256]{2,1,0:T(8,128)(2,1)S(1)} all-gather(bf16[2,128,256]{2,1,0:T(8,128)(2,1)S(1)} %pad_maximum_fusion), channel_id=3, replica_groups={{0,1},{2,3},{4,5},{6,7},{8,9},{10,11},{12,13},{14,15},{16,17},{18,19},{..., dimensions={0}, use_global_device_ids=true | all-gather | bytes 393216 | tf_op jit(solution)/shard_map/all_gather | solution.py:231
  58.7 0.0 collective-permute-done.4.mate_ref
  58.7 0.0 collective-permute-done.3.other_ref
  58.7 5.6 %merge.1 = (bf16[16,256,512]{2,1,0:T(8,128)(2,1)}, bf16[4096,256]{1,0:T(8,128)(2,1)}) custom-call(s32[3]{0:T(128)S(1)} %pad_add_fusion.place_ref, bf16[16,128,256]{2,1,0:T(8,128)(2,1)S(1)} %all-to-all-done.own_ref, bf16[16,128,256]{2,1,0:T(8,128)(2,1)S(1)} %collective-permute-done.3.other_ref, bf16[2,2,128,256]{3,2,1,0:T(8,128)(2,1)S(1)} %bitcast.19, ...), custom_call_target="tpu_custom_call" | custom-call | tf_op jit(solution)/shard_map/merge/pallas_call | solution.py:234
  64.3 3.9 %all-to-all-done.1.x_ref = bf16[8,128,256]{2,1,0:T(8,128)(2,1)S(1)} async-done(((bf16[8,128,256]{2,1,0:T(8,128)(2,1)}), bf16[8,128,256]{2,1,0:T(8,128)(2,1)S(1)}, u32[]{:S(2)}, u32[]{:S(2)}) %all-to-all-start.1) | async-done | bytes 524320 | tf_op jit(solution)/shard_map/all_to_all | solution.py:46
  68.1 2.4 %first.1 = (bf16[2,64,256]{2,1,0:T(8,128)(2,1)S(1)}, bf16[64,256]{1,0:T(8,128)(2,1)S(1)}, bf16[16,256,512]{2,1,0:T(8,128)(2,1)S(1)}) custom-call(bf16[8,128,256]{2,1,0:T(8,128)(2,1)S(1)} %all-to-all-done.1.x_ref, bf16[16,256,512]{2,1,0:T(8,128)(2,1)} %get-tuple-element.35.stored_ref, f32[16,1,256]{2,1,0:T(1,128)S(1)} %bitcast.24, ...), custom_call_target="tpu_custom_call" | custom-call | tf_op jit(solution)/shard_map/first/pallas_call | solution.py:260
  70.6 14.1 %all_to_all.25.x_ref = bf16[8,128,256]{2,1,0:T(8,128)(2,1)S(1)} all-to-all(bf16[8,128,256]{2,1,0:T(8,128)(2,1)S(1)} %broadcast_in_dim.38), channel_id=1, replica_groups={{0,2,4,6,8,10,12,14},{1,3,5,7,9,11,13,15},{16,18,20,22,24,26,28,30},{17..., dimensions={0} | all-to-all | bytes 1048576 | tf_op jit(solution)/shard_map/all_to_all | solution.py:46
  84.7 1.0 step.3
  85.8 12.7 %all_to_all.26.x_ref = bf16[8,128,256]{2,1,0:T(8,128)(2,1)S(1)} all-to-all(bf16[8,128,256]{2,1,0:T(8,128)(2,1)S(1)} %broadcast_in_dim.40), channel_id=1, replica_groups={{0,2,4,6,8,10,12,14},{1,3,5,7,9,11,13,15},{16,18,20,22,24,26,28,30},{17..., dimensions={0} | all-to-all | bytes 1048576 | tf_op jit(solution)/shard_map/all_to_all | solution.py:46
  98.4 1.0 step.4
  99.5 11.7 %all_to_all.27.x_ref = bf16[8,128,256]{2,1,0:T(8,128)(2,1)S(1)} all-to-all(bf16[8,128,256]{2,1,0:T(8,128)(2,1)S(1)} %broadcast_in_dim.42), channel_id=1, replica_groups={{0,2,4,6,8,10,12,14},{1,3,5,7,9,11,13,15},{16,18,20,22,24,26,28,30},{17..., dimensions={0} | all-to-all | bytes 1048576 | tf_op jit(solution)/shard_map/all_to_all | solution.py:46
  111.2 1.0 step.5
  112.2 5.2 %collective-permute-start.5 = (bf16[4,64,256]{2,1,0:T(8,128)(2,1)S(1)}, bf16[4,64,256]{2,1,0:T(8,128)(2,1)S(1)}, u32[]{:S(2)}, u32[]{:S(2)}) collective-permute-start(bf16[4,64,256]{2,1,0:T(8,128)(2,1)S(1)} %pad_maximum_fusion.1), channel_id=1, source_target_pairs={{0,1},{1,0},{2,3},{3,2},{4,5},{5,4},{6,7},{7,6},{8,9},{9,8},{10,11... | collective-permute-start | bytes 393224 | tf_op jit(solution)/shard_map/ppermute | solution.py:277
  117.4 1.0 collective-permute-done.5.swapped_ref
  118.4 0.7 finish.1
  (9 shorter events, 0.2 us)
Async XLA Ops:
  0.6 55.9 %copy-start = (f32[1,4096]{1,0:T(1,128)S(1)}, f32[1,4096]{1,0:T(1,128)}, u32[]{:S(2)}) copy-start(f32[1,4096]{1,0:T(1,128)} %param.13) | copy-start | bytes 49156
  2.2 21.3 %collective-permute-start = (bf16[256,256]{1,0:T(8,128)(2,1)}, bf16[256,256]{1,0:T(8,128)(2,1)S(1)}, u32[]{:S(2)}, u32[]{:S(2)}) collective-permute-start(bf16[256,256]{1,0:T(8,128)(2,1)} %block.1), channel_id=1, source_target_pairs={{0,0},{1,129},{2,18},{3,147},{4,36},{5,165},{6,54},{7,183},{8,72},... | collective-permute-start | bytes 393224 | tf_op jit(solution)/shard_map/ppermute | solution.py:204
  21.4 37.2 %collective-permute-start.4 = (bf16[4096,256]{1,0:T(8,128)(2,1)}, bf16[4096,256]{1,0:T(8,128)(2,1)}, u32[]{:S(2)}, u32[]{:S(2)}) collective-permute-start(bf16[4096,256]{1,0:T(8,128)(2,1)} %bitcast.32), channel_id=1, source_target_pairs={{0,1},{1,0},{2,3},{3,2},{4,5},{5,4},{6,7},{7,6},{8,9},{9,8},{10,11... | collective-permute-start | bytes 6291464 | tf_op jit(solution)/shard_map/ppermute | solution.py:211
  24.6 26.4 %all-to-all-start = ((bf16[16,128,256]{2,1,0:T(8,128)(2,1)}), bf16[16,128,256]{2,1,0:T(8,128)(2,1)S(1)}, u32[]{:S(2)}, u32[]{:S(2)}) async-start(bf16[16,128,256]{2,1,0:T(8,128)(2,1)} %get-tuple-element.26), calls=%async_computation | async-start | bytes 2097152 | tf_op jit(solution)/shard_map/all_to_all | solution.py:227
  33.3 14.4 %collective-permute-start.2 = (bf16[128,256]{1,0:T(8,128)(2,1)S(1)}, bf16[128,256]{1,0:T(8,128)(2,1)S(1)}, u32[]{:S(2)}, u32[]{:S(2)}) collective-permute-start(bf16[128,256]{1,0:T(8,128)(2,1)S(1)} %get-tuple-element.29), channel_id=1, source_target_pairs={{0,256},{15,257},{13,0},{11,1},{9,258},{7,259},{5,2},{3,3},{1,260}... | collective-permute-start | bytes 196616 | tf_op jit(solution)/shard_map/ppermute | solution.py:226
  36.2 14.8 %collective-permute-start.1 = (bf16[128,256]{1,0:T(8,128)(2,1)S(1)}, bf16[128,256]{1,0:T(8,128)(2,1)S(1)}, u32[]{:S(2)}, u32[]{:S(2)}) collective-permute-start(bf16[128,256]{1,0:T(8,128)(2,1)S(1)} %get-tuple-element.29), channel_id=1, source_target_pairs={{0,0},{15,1},{13,256},{11,257},{9,2},{7,3},{5,258},{3,259},{1,4},{... | collective-permute-start | bytes 196616 | tf_op jit(solution)/shard_map/ppermute | solution.py:226
  51.0 7.7 %collective-permute-start.3 = (bf16[16,128,256]{2,1,0:T(8,128)(2,1)S(1)}, bf16[16,128,256]{2,1,0:T(8,128)(2,1)S(1)}, u32[]{:S(2)}, u32[]{:S(2)}) collective-permute-start(bf16[16,128,256]{2,1,0:T(8,128)(2,1)S(1)} %all-to-all-done.own_ref), channel_id=1, source_target_pairs={{0,1},{1,0},{2,3},{3,2},{4,5},{5,4},{6,7},{7,6},{8,9},{9,8},{10,11... | collective-permute-start | bytes 3145736 | tf_op jit(solution)/shard_map/ppermute | solution.py:230
  52.9 15.2 %all-to-all-start.1 = ((bf16[8,128,256]{2,1,0:T(8,128)(2,1)}), bf16[8,128,256]{2,1,0:T(8,128)(2,1)S(1)}, u32[]{:S(2)}, u32[]{:S(2)}) async-start(bf16[8,128,256]{2,1,0:T(8,128)(2,1)} %broadcast_in_dim.36), calls=%async_computation.1 | async-start | bytes 1048576 | tf_op jit(solution)/shard_map/all_to_all | solution.py:46
  112.2 6.2 %collective-permute-start.5 = (bf16[4,64,256]{2,1,0:T(8,128)(2,1)S(1)}, bf16[4,64,256]{2,1,0:T(8,128)(2,1)S(1)}, u32[]{:S(2)}, u32[]{:S(2)}) collective-permute-start(bf16[4,64,256]{2,1,0:T(8,128)(2,1)S(1)} %pad_maximum_fusion.1), channel_id=1, source_target_pairs={{0,1},{1,0},{2,3},{3,2},{4,5},{5,4},{6,7},{7,6},{8,9},{9,8},{10,11... | collective-permute-start | bytes 393224 | tf_op jit(solution)/shard_map/ppermute | solution.py:277

commit v11 on v10

--- a/solution.py
+++ b/solution.py
@@ -72,6 +72,14 @@
     for chip in range(down_ref.shape[0]):
         down_ref[chip] = block_ref[:half, :]
     up_ref[...] = block_ref[half:, :]
+
+
+def turn_kernel(own_ref, turned_ref):
+    cols = own_ref.shape[2]
+    for pair in range(CHIPS):
+        part = own_ref[:, 16 * pair : 16 * pair + 16, :].astype(jnp.float32).reshape(16, 2, 8, cols)
+        for right in range(2):
+            turned_ref[2 * pair + right] = part[:, right].reshape(128, cols).astype(jnp.bfloat16).T
 
 
 def merge_kernel(
@@ -104,17 +112,12 @@
     order = jnp.where(place == goes, 1.0, 0.0).astype(jnp.bfloat16)
     up = jnp.dot(up_ref[...].reshape(2 * cols, cols), order, preferred_element_type=jnp.float32).astype(jnp.bfloat16)
     for pair in range(CHIPS):
-        parts = [
-            ref[:, 16 * pair : 16 * pair + 16, :].astype(jnp.float32).reshape(16, 2, 8, cols)
-            for ref in (own_ref, other_ref)
-        ]
         for load in loads[pair]:
             load.wait()
         for right in range(2):
-            down = jnp.concatenate([part[:, right].reshape(128, cols) for part in parts], 0)
-            down = down.astype(jnp.bfloat16).T
+            t = 2 * pair + right
+            down = jnp.concatenate([own_ref[t], other_ref[t]], 1)
             delta = lax.dot_general(down, up, (((1,), (1,)), ((), ())), preferred_element_type=jnp.float32)
-            t = 2 * pair + right
             rows = slice(t * cols, (t + 1) * cols)
             mine = (old_ref[0, rows, :].astype(jnp.float32) + delta[:, :cols]).astype(jnp.bfloat16)
             theirs = (old_ref[1, rows, :].astype(jnp.float32) + delta[:, cols:]).astype(jnp.bfloat16)
@@ -227,6 +230,14 @@
     own = lax.all_to_all(down, ("fsdp", "tp"), 0, 0, axis_index_groups=PLANES)
     own, copies, *ups = lax.optimization_barrier((own, copies, *ups))
     x = spread(copies)
+    own = pl.pallas_call(
+        turn_kernel,
+        out_shape=jax.ShapeDtypeStruct((tp, cols, size), jnp.bfloat16),
+        in_specs=[VMEM],
+        out_specs=VMEM,
+        name="turn",
+        compiler_params=ROOM,
+    )(own)
     other = lax.ppermute(own, "tp", SWAP)
     ups = lax.all_gather(jnp.stack(ups), "tp", axis=0, axis_index_groups=PAIRS)
     f = lax.axis_index("fsdp")

time: 120 us -> 120 us (level)
  no operation moved by 1% of the time
where the time goes in v11:
time: 120 us; the launch traced here: 119 us
  starting transfers between devices  42.7 us (36%)
  blocking collectives  42.7 us (36%)
  waiting for transfers between devices  17.5 us (15%)
  Pallas kernels  14.5 us (12%)
    all_to_all x3, blocking collectives, spread(): return lax.all_to_all(blocks, 'tp', 0, 0, axis_index_groups=GROUPS)  38.5 us
    ppermute x1, starting transfers between devices, shards(): block = lax.ppermute(block, ('fsdp', 'tp'), SHIFTED)  16.3 us
    ppermute x2, waiting for transfers between devices, shards(): ups = [lax.ppermute(up, ('fsdp', 'tp'), relay(part)) for part in range(2)]  12.6 us
    all_to_all x1, starting transfers between devices, shards(): own = lax.all_to_all(down, ('fsdp', 'tp'), 0, 0, axis_index_groups=PLANES)  8.76 us
    pallas_call x1, Pallas kernels, shards(): pl.pallas_call(merge_kernel, out_shape=(jax.ShapeDtypeStruct((tp, cols, 2...  5.54 us
    pallas_call x4, Pallas kernels, shards(): pl.pallas_call(step_kernel if step else first_kernel, out_shape=(jax.Shap...  5.37 us
    ppermute x1, starting transfers between devices, shards(): swapped = lax.ppermute(jnp.stack(gives), 'tp', SWAP)  5.21 us
    ppermute x2, starting transfers between devices, shards(): ups = [lax.ppermute(up, ('fsdp', 'tp'), relay(part)) for part in range(2)]  5 us
  transfers between devices with their start and end apart: 8, of which 4 were waited for; matrix products, arithmetic and copies ran while one was open for 1% of the time, Pallas kernels for 6%

profile of v11, /device:TPU:1, one launch (start us, length us, event | category | flops | bytes accessed | tf_op | source)
XLA Modules:
  0.0 119.4 jit_solution(13457578711787322974)
XLA Ops:
  0.6 1.5 %block.1 = bf16[256,256]{1,0:T(8,128)(2,1)} custom-call(bf16[1,4,4096]{2,1,0:T(4,128)(2,1)} %a_new_ref.1, bf16[1,4,4096]{2,1,0:T(4,128)(2,1)} %a_old_ref.1, bf16[1,128,128]{2,1,0:T(8,128)(2,1)} %b_new_ref.1, bf16[1,128,128]{2,1,0:T(8,128)(2,1)} %b_old_ref.1), custom_call_target="tpu_custom_call" | custom-call | tf_op jit(solution)/shard_map/block/pallas_call | solution.py:194
  2.2 16.3 %collective-permute-start = (bf16[256,256]{1,0:T(8,128)(2,1)}, bf16[256,256]{1,0:T(8,128)(2,1)S(1)}, u32[]{:S(2)}, u32[]{:S(2)}) collective-permute-start(bf16[256,256]{1,0:T(8,128)(2,1)} %block.1), channel_id=1, source_target_pairs={{0,0},{1,129},{2,18},{3,147},{4,36},{5,165},{6,54},{7,183},{8,72},... | collective-permute-start | bytes 393224 | tf_op jit(solution)/shard_map/ppermute | solution.py:207
  18.5 2.1 %all-gather = bf16[256,256]{1,0:T(8,128)(2,1)S(1)} all-gather(bf16[128,256]{1,0:T(8,128)(2,1)} %param.7), channel_id=2, replica_groups={{0,1},{2,3},{4,5},{6,7},{8,9},{10,11},{12,13},{14,15},{16,17},{18,19},{..., dimensions={0}, use_global_device_ids=true | all-gather | bytes 196608 | tf_op jit(solution)/shard_map/all_gather | solution.py:209
  20.6 0.8 broadcast_in_dim.36
  21.4 2.1 %collective-permute-start.4 = (bf16[4096,256]{1,0:T(8,128)(2,1)}, bf16[4096,256]{1,0:T(8,128)(2,1)}, u32[]{:S(2)}, u32[]{:S(2)}) collective-permute-start(bf16[4096,256]{1,0:T(8,128)(2,1)} %bitcast.32), channel_id=1, source_target_pairs={{0,1},{1,0},{2,3},{3,2},{4,5},{5,4},{6,7},{7,6},{8,9},{9,8},{10,11... | collective-permute-start | bytes 6291464 | tf_op jit(solution)/shard_map/ppermute | solution.py:214
  23.5 0.0 collective-permute-done.block_ref
  23.5 1.0 split.1
  24.6 8.8 %all-to-all-start = ((bf16[16,128,256]{2,1,0:T(8,128)(2,1)}), bf16[16,128,256]{2,1,0:T(8,128)(2,1)S(1)}, u32[]{:S(2)}, u32[]{:S(2)}) async-start(bf16[16,128,256]{2,1,0:T(8,128)(2,1)} %get-tuple-element.26), calls=%async_computation | async-start | bytes 2097152 | tf_op jit(solution)/shard_map/all_to_all | solution.py:230
  33.3 2.8 %collective-permute-start.2 = (bf16[128,256]{1,0:T(8,128)(2,1)S(1)}, bf16[128,256]{1,0:T(8,128)(2,1)S(1)}, u32[]{:S(2)}, u32[]{:S(2)}) collective-permute-start(bf16[128,256]{1,0:T(8,128)(2,1)S(1)} %get-tuple-element.29), channel_id=1, source_target_pairs={{0,256},{15,257},{13,0},{11,1},{9,258},{7,259},{5,2},{3,3},{1,260}... | collective-permute-start | bytes 196616 | tf_op jit(solution)/shard_map/ppermute | solution.py:229
  36.2 2.2 %collective-permute-start.1 = (bf16[128,256]{1,0:T(8,128)(2,1)S(1)}, bf16[128,256]{1,0:T(8,128)(2,1)S(1)}, u32[]{:S(2)}, u32[]{:S(2)}) collective-permute-start(bf16[128,256]{1,0:T(8,128)(2,1)S(1)} %get-tuple-element.29), channel_id=1, source_target_pairs={{0,0},{15,1},{13,256},{11,257},{9,2},{7,3},{5,258},{3,259},{1,4},{... | collective-permute-start | bytes 196616 | tf_op jit(solution)/shard_map/ppermute | solution.py:229
  38.3 9.4 %collective-permute-done.2 = bf16[128,256]{1,0:T(8,128)(2,1)S(1)} collective-permute-done((bf16[128,256]{1,0:T(8,128)(2,1)S(1)}, bf16[128,256]{1,0:T(8,128)(2,1)S(1)}, u32[]{:S(2)}, u32[]{:S(2)}) %collective-permute-start.2) | collective-permute-done | bytes 65568 | tf_op jit(solution)/shard_map/ppermute | solution.py:229
  47.7 3.3 %collective-permute-done.1 = bf16[128,256]{1,0:T(8,128)(2,1)S(1)} collective-permute-done((bf16[128,256]{1,0:T(8,128)(2,1)S(1)}, bf16[128,256]{1,0:T(8,128)(2,1)S(1)}, u32[]{:S(2)}, u32[]{:S(2)}) %collective-permute-start.1) | collective-permute-done | bytes 65568 | tf_op jit(solution)/shard_map/ppermute | solution.py:229
  51.0 0.0 all-to-all-done.own_ref
  51.0 0.3 turn.1.own_ref
  51.3 1.9 %collective-permute-start.3 = (bf16[16,256,128]{2,1,0:T(8,128)(2,1)S(1)}, bf16[16,256,128]{2,1,0:T(8,128)(2,1)S(1)}, u32[]{:S(2)}, u32[]{:S(2)}) collective-permute-start(bf16[16,256,128]{2,1,0:T(8,128)(2,1)S(1)} %turn.1.own_ref), channel_id=1, source_target_pairs={{0,1},{1,0},{2,3},{3,2},{4,5},{5,4},{6,7},{7,6},{8,9},{9,8},{10,11... | collective-permute-start | bytes 3145736 | tf_op jit(solution)/shard_map/ppermute | solution.py:241
  53.2 3.5 %all-to-all-start.1 = ((bf16[8,128,256]{2,1,0:T(8,128)(2,1)}), bf16[8,128,256]{2,1,0:T(8,128)(2,1)S(1)}, u32[]{:S(2)}, u32[]{:S(2)}) async-start(bf16[8,128,256]{2,1,0:T(8,128)(2,1)} %broadcast_in_dim.36), calls=%async_computation.1 | async-start | bytes 1048576 | tf_op jit(solution)/shard_map/all_to_all | solution.py:46
  56.8 0.1 pad_add_fusion.place_ref
  56.9 2.1 %all-gather.1 = bf16[4,128,256]{2,1,0:T(8,128)(2,1)S(1)} all-gather(bf16[2,128,256]{2,1,0:T(8,128)(2,1)S(1)} %pad_maximum_fusion), channel_id=3, replica_groups={{0,1},{2,3},{4,5},{6,7},{8,9},{10,11},{12,13},{14,15},{16,17},{18,19},{..., dimensions={0}, use_global_device_ids=true | all-gather | bytes 393216 | tf_op jit(solution)/shard_map/all_gather | solution.py:242
  59.0 0.0 collective-permute-done.4.mate_ref
  59.0 0.0 collective-permute-done.3.other_ref
  59.0 5.5 %merge.1 = (bf16[16,256,512]{2,1,0:T(8,128)(2,1)}, bf16[4096,256]{1,0:T(8,128)(2,1)}) custom-call(s32[3]{0:T(128)S(1)} %pad_add_fusion.place_ref, bf16[16,256,128]{2,1,0:T(8,128)(2,1)S(1)} %turn.1.own_ref, bf16[16,256,128]{2,1,0:T(8,128)(2,1)S(1)} %collective-permute-done.3.other_ref, bf16[2,2,128,256]{3,2,1,0:T(8,128)(2,1)S(1)} %bitcast.19, ...), custom_call_target="tpu_custom_call" | custom-call | tf_op jit(solution)/shard_map/merge/pallas_call | solution.py:245
  64.6 3.9 %all-to-all-done.1.x_ref = bf16[8,128,256]{2,1,0:T(8,128)(2,1)S(1)} async-done(((bf16[8,128,256]{2,1,0:T(8,128)(2,1)}), bf16[8,128,256]{2,1,0:T(8,128)(2,1)S(1)}, u32[]{:S(2)}, u32[]{:S(2)}) %all-to-all-start.1) | async-done | bytes 524320 | tf_op jit(solution)/shard_map/all_to_all | solution.py:46
  68.5 2.4 %first.1 = (bf16[2,64,256]{2,1,0:T(8,128)(2,1)S(1)}, bf16[64,256]{1,0:T(8,128)(2,1)S(1)}, bf16[16,256,512]{2,1,0:T(8,128)(2,1)S(1)}) custom-call(bf16[8,128,256]{2,1,0:T(8,128)(2,1)S(1)} %all-to-all-done.1.x_ref, bf16[16,256,512]{2,1,0:T(8,128)(2,1)} %get-tuple-element.35.stored_ref, f32[16,1,256]{2,1,0:T(1,128)S(1)} %bitcast.24, ...), custom_call_target="tpu_custom_call" | custom-call | tf_op jit(solution)/shard_map/first/pallas_call | solution.py:271
  70.9 14.1 %all_to_all.25.x_ref = bf16[8,128,256]{2,1,0:T(8,128)(2,1)S(1)} all-to-all(bf16[8,128,256]{2,1,0:T(8,128)(2,1)S(1)} %broadcast_in_dim.38), channel_id=1, replica_groups={{0,2,4,6,8,10,12,14},{1,3,5,7,9,11,13,15},{16,18,20,22,24,26,28,30},{17..., dimensions={0} | all-to-all | bytes 1048576 | tf_op jit(solution)/shard_map/all_to_all | solution.py:46
  85.0 1.0 step.3
  86.1 12.7 %all_to_all.26.x_ref = bf16[8,128,256]{2,1,0:T(8,128)(2,1)S(1)} all-to-all(bf16[8,128,256]{2,1,0:T(8,128)(2,1)S(1)} %broadcast_in_dim.40), channel_id=1, replica_groups={{0,2,4,6,8,10,12,14},{1,3,5,7,9,11,13,15},{16,18,20,22,24,26,28,30},{17..., dimensions={0} | all-to-all | bytes 1048576 | tf_op jit(solution)/shard_map/all_to_all | solution.py:46
  98.7 1.0 step.4
  99.7 11.7 %all_to_all.27.x_ref = bf16[8,128,256]{2,1,0:T(8,128)(2,1)S(1)} all-to-all(bf16[8,128,256]{2,1,0:T(8,128)(2,1)S(1)} %broadcast_in_dim.42), channel_id=1, replica_groups={{0,2,4,6,8,10,12,14},{1,3,5,7,9,11,13,15},{16,18,20,22,24,26,28,30},{17..., dimensions={0} | all-to-all | bytes 1048576 | tf_op jit(solution)/shard_map/all_to_all | solution.py:46
  111.5 1.0 step.5
  112.5 5.2 %collective-permute-start.5 = (bf16[4,64,256]{2,1,0:T(8,128)(2,1)S(1)}, bf16[4,64,256]{2,1,0:T(8,128)(2,1)S(1)}, u32[]{:S(2)}, u32[]{:S(2)}) collective-permute-start(bf16[4,64,256]{2,1,0:T(8,128)(2,1)S(1)} %pad_maximum_fusion.1), channel_id=1, source_target_pairs={{0,1},{1,0},{2,3},{3,2},{4,5},{5,4},{6,7},{7,6},{8,9},{9,8},{10,11... | collective-permute-start | bytes 393224 | tf_op jit(solution)/shard_map/ppermute | solution.py:288
  117.7 1.0 collective-permute-done.5.swapped_ref
  118.7 0.7 finish.1
  (10 shorter events, 0.2 us)
Async XLA Ops:
  0.6 56.2 %copy-start = (f32[1,4096]{1,0:T(1,128)S(1)}, f32[1,4096]{1,0:T(1,128)}, u32[]{:S(2)}) copy-start(f32[1,4096]{1,0:T(1,128)} %param.13) | copy-start | bytes 49156
  2.2 21.3 %collective-permute-start = (bf16[256,256]{1,0:T(8,128)(2,1)}, bf16[256,256]{1,0:T(8,128)(2,1)S(1)}, u32[]{:S(2)}, u32[]{:S(2)}) collective-permute-start(bf16[256,256]{1,0:T(8,128)(2,1)} %block.1), channel_id=1, source_target_pairs={{0,0},{1,129},{2,18},{3,147},{4,36},{5,165},{6,54},{7,183},{8,72},... | collective-permute-start | bytes 393224 | tf_op jit(solution)/shard_map/ppermute | solution.py:207
  21.4 37.6 %collective-permute-start.4 = (bf16[4096,256]{1,0:T(8,128)(2,1)}, bf16[4096,256]{1,0:T(8,128)(2,1)}, u32[]{:S(2)}, u32[]{:S(2)}) collective-permute-start(bf16[4096,256]{1,0:T(8,128)(2,1)} %bitcast.32), channel_id=1, source_target_pairs={{0,1},{1,0},{2,3},{3,2},{4,5},{5,4},{6,7},{7,6},{8,9},{9,8},{10,11... | collective-permute-start | bytes 6291464 | tf_op jit(solution)/shard_map/ppermute | solution.py:214
  24.6 26.4 %all-to-all-start = ((bf16[16,128,256]{2,1,0:T(8,128)(2,1)}), bf16[16,128,256]{2,1,0:T(8,128)(2,1)S(1)}, u32[]{:S(2)}, u32[]{:S(2)}) async-start(bf16[16,128,256]{2,1,0:T(8,128)(2,1)} %get-tuple-element.26), calls=%async_computation | async-start | bytes 2097152 | tf_op jit(solution)/shard_map/all_to_all | solution.py:230
  33.3 14.4 %collective-permute-start.2 = (bf16[128,256]{1,0:T(8,128)(2,1)S(1)}, bf16[128,256]{1,0:T(8,128)(2,1)S(1)}, u32[]{:S(2)}, u32[]{:S(2)}) collective-permute-start(bf16[128,256]{1,0:T(8,128)(2,1)S(1)} %get-tuple-element.29), channel_id=1, source_target_pairs={{0,256},{15,257},{13,0},{11,1},{9,258},{7,259},{5,2},{3,3},{1,260}... | collective-permute-start | bytes 196616 | tf_op jit(solution)/shard_map/ppermute | solution.py:229
  36.2 14.8 %collective-permute-start.1 = (bf16[128,256]{1,0:T(8,128)(2,1)S(1)}, bf16[128,256]{1,0:T(8,128)(2,1)S(1)}, u32[]{:S(2)}, u32[]{:S(2)}) collective-permute-start(bf16[128,256]{1,0:T(8,128)(2,1)S(1)} %get-tuple-element.29), channel_id=1, source_target_pairs={{0,0},{15,1},{13,256},{11,257},{9,2},{7,3},{5,258},{3,259},{1,4},{... | collective-permute-start | bytes 196616 | tf_op jit(solution)/shard_map/ppermute | solution.py:229
  51.3 7.7 %collective-permute-start.3 = (bf16[16,256,128]{2,1,0:T(8,128)(2,1)S(1)}, bf16[16,256,128]{2,1,0:T(8,128)(2,1)S(1)}, u32[]{:S(2)}, u32[]{:S(2)}) collective-permute-start(bf16[16,256,128]{2,1,0:T(8,128)(2,1)S(1)} %turn.1.own_ref), channel_id=1, source_target_pairs={{0,1},{1,0},{2,3},{3,2},{4,5},{5,4},{6,7},{7,6},{8,9},{9,8},{10,11... | collective-permute-start | bytes 3145736 | tf_op jit(solution)/shard_map/ppermute | solution.py:241
  53.2 15.2 %all-to-all-start.1 = ((bf16[8,128,256]{2,1,0:T(8,128)(2,1)}), bf16[8,128,256]{2,1,0:T(8,128)(2,1)S(1)}, u32[]{:S(2)}, u32[]{:S(2)}) async-start(bf16[8,128,256]{2,1,0:T(8,128)(2,1)} %broadcast_in_dim.36), calls=%async_computation.1 | async-start | bytes 1048576 | tf_op jit(solution)/shard_map/all_to_all | solution.py:46
  112.5 6.2 %collective-permute-start.5 = (bf16[4,64,256]{2,1,0:T(8,128)(2,1)S(1)}, bf16[4,64,256]{2,1,0:T(8,128)(2,1)S(1)}, u32[]{:S(2)}, u32[]{:S(2)}) collective-permute-start(bf16[4,64,256]{2,1,0:T(8,128)(2,1)S(1)} %pad_maximum_fusion.1), channel_id=1, source_target_pairs={{0,1},{1,0},{2,3},{3,2},{4,5},{5,4},{6,7},{7,6},{8,9},{9,8},{10,11... | collective-permute-start | bytes 393224 | tf_op jit(solution)/shard_map/ppermute | solution.py:288

commit v12 on v10

--- a/solution.py
+++ b/solution.py
@@ -153,15 +153,15 @@
 
 def first_kernel(x_ref, stored_ref, gain_ref, mine_ref, out_ref, give_ref, weight_ref, sems):
     loads = [
-        pltpu.make_async_copy(stored_ref.at[2 * i : 2 * i + 2], weight_ref.at[2 * i : 2 * i + 2], sems.at[i])
-        for i in range(CHIPS)
+        pltpu.make_async_copy(stored_ref.at[4 * i : 4 * i + 4], weight_ref.at[4 * i : 4 * i + 4], sems.at[i])
+        for i in range(CHIPS // 2)
     ]
     for load in loads:
         load.start()
 
     def arrive(i):
-        if i % 2 == 0:
-            loads[i // 2].wait()
+        if i % 4 == 0:
+            loads[i // 4].wait()
 
     decode(x_ref, weight_ref, gain_ref, mine_ref, out_ref, give_ref, arrive)
 
@@ -266,7 +266,7 @@
             ),
             in_specs=[VMEM, VMEM if step else HBM, VMEM, VMEM],
             out_specs=(VMEM, VMEM, VMEM),
-            scratch_shapes=[] if step else [pltpu.SemaphoreType.DMA((CHIPS,))],
+            scratch_shapes=[] if step else [pltpu.SemaphoreType.DMA((CHIPS // 2,))],
             input_output_aliases={1: 2} if step else {},
             name="step" if step else "first",
             compiler_params=ROOM if step else pltpu.CompilerParams(vmem_limit_bytes=46 * 1024 * 1024),

time: 120 us -> 120 us (level)
  no operation moved by 1% of the time
where the time goes in v12:
time: 120 us; the launch traced here: 119 us
  blocking collectives  42.8 us (36%)
  starting transfers between devices  42.7 us (36%)
  waiting for transfers between devices  17.4 us (14%)
  Pallas kernels  14.3 us (12%)
    all_to_all x3, blocking collectives, spread(): return lax.all_to_all(blocks, 'tp', 0, 0, axis_index_groups=GROUPS)  38.5 us
    ppermute x1, starting transfers between devices, shards(): block = lax.ppermute(block, ('fsdp', 'tp'), SHIFTED)  16.3 us
    ppermute x2, waiting for transfers between devices, shards(): ups = [lax.ppermute(up, ('fsdp', 'tp'), relay(part)) for part in range(2)]  12.6 us
    all_to_all x1, starting transfers between devices, shards(): own = lax.all_to_all(down, ('fsdp', 'tp'), 0, 0, axis_index_groups=PLANES)  8.76 us
    pallas_call x1, Pallas kernels, shards(): pl.pallas_call(merge_kernel, out_shape=(jax.ShapeDtypeStruct((tp, cols, 2...  5.58 us
    pallas_call x4, Pallas kernels, shards(): pl.pallas_call(step_kernel if step else first_kernel, out_shape=(jax.Shap...  5.45 us
    ppermute x1, starting transfers between devices, shards(): swapped = lax.ppermute(jnp.stack(gives), 'tp', SWAP)  5.21 us
    ppermute x2, starting transfers between devices, shards(): ups = [lax.ppermute(up, ('fsdp', 'tp'), relay(part)) for part in range(2)]  5 us
  transfers between devices with their start and end apart: 8, of which 4 were waited for; matrix products, arithmetic and copies ran while one was open for 1% of the time, Pallas kernels for 6%

profile of v12, /device:TPU:1, one launch (start us, length us, event | category | flops | bytes accessed | tf_op | source)
XLA Modules:
  0.0 119.2 jit_solution(16280703395861182568)
XLA Ops:
  0.6 0.0 copy-start
  0.6 1.5 %block.1 = bf16[256,256]{1,0:T(8,128)(2,1)} custom-call(bf16[1,4,4096]{2,1,0:T(4,128)(2,1)} %a_new_ref.1, bf16[1,4,4096]{2,1,0:T(4,128)(2,1)} %a_old_ref.1, bf16[1,128,128]{2,1,0:T(8,128)(2,1)} %b_new_ref.1, bf16[1,128,128]{2,1,0:T(8,128)(2,1)} %b_old_ref.1), custom_call_target="tpu_custom_call" | custom-call | tf_op jit(solution)/shard_map/block/pallas_call | solution.py:191
  2.2 16.3 %collective-permute-start = (bf16[256,256]{1,0:T(8,128)(2,1)}, bf16[256,256]{1,0:T(8,128)(2,1)S(1)}, u32[]{:S(2)}, u32[]{:S(2)}) collective-permute-start(bf16[256,256]{1,0:T(8,128)(2,1)} %block.1), channel_id=1, source_target_pairs={{0,0},{1,129},{2,18},{3,147},{4,36},{5,165},{6,54},{7,183},{8,72},... | collective-permute-start | bytes 393224 | tf_op jit(solution)/shard_map/ppermute | solution.py:204
  18.5 2.1 %all-gather = bf16[256,256]{1,0:T(8,128)(2,1)S(1)} all-gather(bf16[128,256]{1,0:T(8,128)(2,1)} %param.7), channel_id=2, replica_groups={{0,1},{2,3},{4,5},{6,7},{8,9},{10,11},{12,13},{14,15},{16,17},{18,19},{..., dimensions={0}, use_global_device_ids=true | all-gather | bytes 196608 | tf_op jit(solution)/shard_map/all_gather | solution.py:206
  20.6 0.8 broadcast_in_dim.36
  21.4 2.1 %collective-permute-start.4 = (bf16[4096,256]{1,0:T(8,128)(2,1)}, bf16[4096,256]{1,0:T(8,128)(2,1)}, u32[]{:S(2)}, u32[]{:S(2)}) collective-permute-start(bf16[4096,256]{1,0:T(8,128)(2,1)} %bitcast.32), channel_id=1, source_target_pairs={{0,1},{1,0},{2,3},{3,2},{4,5},{5,4},{6,7},{7,6},{8,9},{9,8},{10,11... | collective-permute-start | bytes 6291464 | tf_op jit(solution)/shard_map/ppermute | solution.py:211
  23.5 0.0 collective-permute-done.block_ref
  23.5 1.0 split.1
  24.6 8.8 %all-to-all-start = ((bf16[16,128,256]{2,1,0:T(8,128)(2,1)}), bf16[16,128,256]{2,1,0:T(8,128)(2,1)S(1)}, u32[]{:S(2)}, u32[]{:S(2)}) async-start(bf16[16,128,256]{2,1,0:T(8,128)(2,1)} %get-tuple-element.26), calls=%async_computation | async-start | bytes 2097152 | tf_op jit(solution)/shard_map/all_to_all | solution.py:227
  33.3 2.8 %collective-permute-start.2 = (bf16[128,256]{1,0:T(8,128)(2,1)S(1)}, bf16[128,256]{1,0:T(8,128)(2,1)S(1)}, u32[]{:S(2)}, u32[]{:S(2)}) collective-permute-start(bf16[128,256]{1,0:T(8,128)(2,1)S(1)} %get-tuple-element.29), channel_id=1, source_target_pairs={{0,256},{15,257},{13,0},{11,1},{9,258},{7,259},{5,2},{3,3},{1,260}... | collective-permute-start | bytes 196616 | tf_op jit(solution)/shard_map/ppermute | solution.py:226
  36.2 2.2 %collective-permute-start.1 = (bf16[128,256]{1,0:T(8,128)(2,1)S(1)}, bf16[128,256]{1,0:T(8,128)(2,1)S(1)}, u32[]{:S(2)}, u32[]{:S(2)}) collective-permute-start(bf16[128,256]{1,0:T(8,128)(2,1)S(1)} %get-tuple-element.29), channel_id=1, source_target_pairs={{0,0},{15,1},{13,256},{11,257},{9,2},{7,3},{5,258},{3,259},{1,4},{... | collective-permute-start | bytes 196616 | tf_op jit(solution)/shard_map/ppermute | solution.py:226
  38.3 9.4 %collective-permute-done.2 = bf16[128,256]{1,0:T(8,128)(2,1)S(1)} collective-permute-done((bf16[128,256]{1,0:T(8,128)(2,1)S(1)}, bf16[128,256]{1,0:T(8,128)(2,1)S(1)}, u32[]{:S(2)}, u32[]{:S(2)}) %collective-permute-start.2) | collective-permute-done | bytes 65568 | tf_op jit(solution)/shard_map/ppermute | solution.py:226
  47.7 3.3 %collective-permute-done.1 = bf16[128,256]{1,0:T(8,128)(2,1)S(1)} collective-permute-done((bf16[128,256]{1,0:T(8,128)(2,1)S(1)}, bf16[128,256]{1,0:T(8,128)(2,1)S(1)}, u32[]{:S(2)}, u32[]{:S(2)}) %collective-permute-start.1) | collective-permute-done | bytes 65568 | tf_op jit(solution)/shard_map/ppermute | solution.py:226
  51.0 0.0 all-to-all-done.own_ref
  51.0 1.9 %collective-permute-start.3 = (bf16[16,128,256]{2,1,0:T(8,128)(2,1)S(1)}, bf16[16,128,256]{2,1,0:T(8,128)(2,1)S(1)}, u32[]{:S(2)}, u32[]{:S(2)}) collective-permute-start(bf16[16,128,256]{2,1,0:T(8,128)(2,1)S(1)} %all-to-all-done.own_ref), channel_id=1, source_target_pairs={{0,1},{1,0},{2,3},{3,2},{4,5},{5,4},{6,7},{7,6},{8,9},{9,8},{10,11... | collective-permute-start | bytes 3145736 | tf_op jit(solution)/shard_map/ppermute | solution.py:230
  52.9 3.5 %all-to-all-start.1 = ((bf16[8,128,256]{2,1,0:T(8,128)(2,1)}), bf16[8,128,256]{2,1,0:T(8,128)(2,1)S(1)}, u32[]{:S(2)}, u32[]{:S(2)}) async-start(bf16[8,128,256]{2,1,0:T(8,128)(2,1)} %broadcast_in_dim.36), calls=%async_computation.1 | async-start | bytes 1048576 | tf_op jit(solution)/shard_map/all_to_all | solution.py:46
  56.4 0.1 pad_add_fusion.place_ref
  56.5 2.1 %all-gather.1 = bf16[4,128,256]{2,1,0:T(8,128)(2,1)S(1)} all-gather(bf16[2,128,256]{2,1,0:T(8,128)(2,1)S(1)} %pad_maximum_fusion), channel_id=3, replica_groups={{0,1},{2,3},{4,5},{6,7},{8,9},{10,11},{12,13},{14,15},{16,17},{18,19},{..., dimensions={0}, use_global_device_ids=true | all-gather | bytes 393216 | tf_op jit(solution)/shard_map/all_gather | solution.py:231
  58.7 0.0 collective-permute-done.4.mate_ref
  58.7 0.0 collective-permute-done.3.other_ref
  58.7 5.6 %merge.1 = (bf16[16,256,512]{2,1,0:T(8,128)(2,1)}, bf16[4096,256]{1,0:T(8,128)(2,1)}) custom-call(s32[3]{0:T(128)S(1)} %pad_add_fusion.place_ref, bf16[16,128,256]{2,1,0:T(8,128)(2,1)S(1)} %all-to-all-done.own_ref, bf16[16,128,256]{2,1,0:T(8,128)(2,1)S(1)} %collective-permute-done.3.other_ref, bf16[2,2,128,256]{3,2,1,0:T(8,128)(2,1)S(1)} %bitcast.19, ...), custom_call_target="tpu_custom_call" | custom-call | tf_op jit(solution)/shard_map/merge/pallas_call | solution.py:234
  64.3 3.9 %all-to-all-done.1.x_ref = bf16[8,128,256]{2,1,0:T(8,128)(2,1)S(1)} async-done(((bf16[8,128,256]{2,1,0:T(8,128)(2,1)}), bf16[8,128,256]{2,1,0:T(8,128)(2,1)S(1)}, u32[]{:S(2)}, u32[]{:S(2)}) %all-to-all-start.1) | async-done | bytes 524320 | tf_op jit(solution)/shard_map/all_to_all | solution.py:46
  68.1 2.5 %first.1 = (bf16[2,64,256]{2,1,0:T(8,128)(2,1)S(1)}, bf16[64,256]{1,0:T(8,128)(2,1)S(1)}, bf16[16,256,512]{2,1,0:T(8,128)(2,1)S(1)}) custom-call(bf16[8,128,256]{2,1,0:T(8,128)(2,1)S(1)} %all-to-all-done.1.x_ref, bf16[16,256,512]{2,1,0:T(8,128)(2,1)} %get-tuple-element.35.stored_ref, f32[16,1,256]{2,1,0:T(1,128)S(1)} %bitcast.24, ...), custom_call_target="tpu_custom_call" | custom-call | tf_op jit(solution)/shard_map/first/pallas_call | solution.py:260
  70.7 14.1 %all_to_all.25.x_ref = bf16[8,128,256]{2,1,0:T(8,128)(2,1)S(1)} all-to-all(bf16[8,128,256]{2,1,0:T(8,128)(2,1)S(1)} %broadcast_in_dim.38), channel_id=1, replica_groups={{0,2,4,6,8,10,12,14},{1,3,5,7,9,11,13,15},{16,18,20,22,24,26,28,30},{17..., dimensions={0} | all-to-all | bytes 1048576 | tf_op jit(solution)/shard_map/all_to_all | solution.py:46
  84.8 1.0 step.3
  85.8 12.7 %all_to_all.26.x_ref = bf16[8,128,256]{2,1,0:T(8,128)(2,1)S(1)} all-to-all(bf16[8,128,256]{2,1,0:T(8,128)(2,1)S(1)} %broadcast_in_dim.40), channel_id=1, replica_groups={{0,2,4,6,8,10,12,14},{1,3,5,7,9,11,13,15},{16,18,20,22,24,26,28,30},{17..., dimensions={0} | all-to-all | bytes 1048576 | tf_op jit(solution)/shard_map/all_to_all | solution.py:46
  98.5 1.0 step.4
  99.5 11.7 %all_to_all.27.x_ref = bf16[8,128,256]{2,1,0:T(8,128)(2,1)S(1)} all-to-all(bf16[8,128,256]{2,1,0:T(8,128)(2,1)S(1)} %broadcast_in_dim.42), channel_id=1, replica_groups={{0,2,4,6,8,10,12,14},{1,3,5,7,9,11,13,15},{16,18,20,22,24,26,28,30},{17..., dimensions={0} | all-to-all | bytes 1048576 | tf_op jit(solution)/shard_map/all_to_all | solution.py:46
  111.2 1.0 step.5
  112.3 5.2 %collective-permute-start.5 = (bf16[4,64,256]{2,1,0:T(8,128)(2,1)S(1)}, bf16[4,64,256]{2,1,0:T(8,128)(2,1)S(1)}, u32[]{:S(2)}, u32[]{:S(2)}) collective-permute-start(bf16[4,64,256]{2,1,0:T(8,128)(2,1)S(1)} %pad_maximum_fusion.1), channel_id=1, source_target_pairs={{0,1},{1,0},{2,3},{3,2},{4,5},{5,4},{6,7},{7,6},{8,9},{9,8},{10,11... | collective-permute-start | bytes 393224 | tf_op jit(solution)/shard_map/ppermute | solution.py:277
  117.5 1.0 collective-permute-done.5.swapped_ref
  118.4 0.7 finish.1
  (9 shorter events, 0.2 us)
Async XLA Ops:
  0.6 55.9 %copy-start = (f32[1,4096]{1,0:T(1,128)S(1)}, f32[1,4096]{1,0:T(1,128)}, u32[]{:S(2)}) copy-start(f32[1,4096]{1,0:T(1,128)} %param.13) | copy-start | bytes 49156
  2.2 21.3 %collective-permute-start = (bf16[256,256]{1,0:T(8,128)(2,1)}, bf16[256,256]{1,0:T(8,128)(2,1)S(1)}, u32[]{:S(2)}, u32[]{:S(2)}) collective-permute-start(bf16[256,256]{1,0:T(8,128)(2,1)} %block.1), channel_id=1, source_target_pairs={{0,0},{1,129},{2,18},{3,147},{4,36},{5,165},{6,54},{7,183},{8,72},... | collective-permute-start | bytes 393224 | tf_op jit(solution)/shard_map/ppermute | solution.py:204
  21.4 37.2 %collective-permute-start.4 = (bf16[4096,256]{1,0:T(8,128)(2,1)}, bf16[4096,256]{1,0:T(8,128)(2,1)}, u32[]{:S(2)}, u32[]{:S(2)}) collective-permute-start(bf16[4096,256]{1,0:T(8,128)(2,1)} %bitcast.32), channel_id=1, source_target_pairs={{0,1},{1,0},{2,3},{3,2},{4,5},{5,4},{6,7},{7,6},{8,9},{9,8},{10,11... | collective-permute-start | bytes 6291464 | tf_op jit(solution)/shard_map/ppermute | solution.py:211
  24.6 26.4 %all-to-all-start = ((bf16[16,128,256]{2,1,0:T(8,128)(2,1)}), bf16[16,128,256]{2,1,0:T(8,128)(2,1)S(1)}, u32[]{:S(2)}, u32[]{:S(2)}) async-start(bf16[16,128,256]{2,1,0:T(8,128)(2,1)} %get-tuple-element.26), calls=%async_computation | async-start | bytes 2097152 | tf_op jit(solution)/shard_map/all_to_all | solution.py:227
  33.3 14.4 %collective-permute-start.2 = (bf16[128,256]{1,0:T(8,128)(2,1)S(1)}, bf16[128,256]{1,0:T(8,128)(2,1)S(1)}, u32[]{:S(2)}, u32[]{:S(2)}) collective-permute-start(bf16[128,256]{1,0:T(8,128)(2,1)S(1)} %get-tuple-element.29), channel_id=1, source_target_pairs={{0,256},{15,257},{13,0},{11,1},{9,258},{7,259},{5,2},{3,3},{1,260}... | collective-permute-start | bytes 196616 | tf_op jit(solution)/shard_map/ppermute | solution.py:226
  36.2 14.8 %collective-permute-start.1 = (bf16[128,256]{1,0:T(8,128)(2,1)S(1)}, bf16[128,256]{1,0:T(8,128)(2,1)S(1)}, u32[]{:S(2)}, u32[]{:S(2)}) collective-permute-start(bf16[128,256]{1,0:T(8,128)(2,1)S(1)} %get-tuple-element.29), channel_id=1, source_target_pairs={{0,0},{15,1},{13,256},{11,257},{9,2},{7,3},{5,258},{3,259},{1,4},{... | collective-permute-start | bytes 196616 | tf_op jit(solution)/shard_map/ppermute | solution.py:226
  51.0 7.7 %collective-permute-start.3 = (bf16[16,128,256]{2,1,0:T(8,128)(2,1)S(1)}, bf16[16,128,256]{2,1,0:T(8,128)(2,1)S(1)}, u32[]{:S(2)}, u32[]{:S(2)}) collective-permute-start(bf16[16,128,256]{2,1,0:T(8,128)(2,1)S(1)} %all-to-all-done.own_ref), channel_id=1, source_target_pairs={{0,1},{1,0},{2,3},{3,2},{4,5},{5,4},{6,7},{7,6},{8,9},{9,8},{10,11... | collective-permute-start | bytes 3145736 | tf_op jit(solution)/shard_map/ppermute | solution.py:230
  52.9 15.2 %all-to-all-start.1 = ((bf16[8,128,256]{2,1,0:T(8,128)(2,1)}), bf16[8,128,256]{2,1,0:T(8,128)(2,1)S(1)}, u32[]{:S(2)}, u32[]{:S(2)}) async-start(bf16[8,128,256]{2,1,0:T(8,128)(2,1)} %broadcast_in_dim.36), calls=%async_computation.1 | async-start | bytes 1048576 | tf_op jit(solution)/shard_map/all_to_all | solution.py:46
  112.3 6.2 %collective-permute-start.5 = (bf16[4,64,256]{2,1,0:T(8,128)(2,1)S(1)}, bf16[4,64,256]{2,1,0:T(8,128)(2,1)S(1)}, u32[]{:S(2)}, u32[]{:S(2)}) collective-permute-start(bf16[4,64,256]{2,1,0:T(8,128)(2,1)S(1)} %pad_maximum_fusion.1), channel_id=1, source_target_pairs={{0,1},{1,0},{2,3},{3,2},{4,5},{5,4},{6,7},{7,6},{8,9},{9,8},{10,11... | collective-permute-start | bytes 393224 | tf_op jit(solution)/shard_map/ppermute | solution.py:277
